TPU v7x, 32 devices: a whole 2x2x4 slice. The times are simulated.
32 devices in a mesh: case: 2 (over y), wall: 4 (over z), azim: 4 (over x, core).
Axes of the slice: x: 2, y: 2, z: 4, core: 2. Of those that a mesh axis runs over, the one named last changes fastest.
Arguments:
- state: float32 [12, 2, 32, 512], P(None, 'case', 'wall', 'azim'), parts along dimension 1, may hold values from 0.5 to 1.5
- courant: float32 [2, 32, 512], P('case', 'wall', 'azim'), parts along dimension 0, may hold values from -0.6 to 0.6
- cross_sections: float32 [64], replicated, may hold values from 0.02 to 0.6
- band_fractions: float32 [64], replicated, may hold values from 0.02 to 0.2
- absorb_index: int32 [11, 16], replicated, may hold values from 0 to 63
- band_index: int32 [16], replicated, may hold values from 0 to 63
Outputs:
- new_state: float32 [12, 2, 32, 512], P(None, 'case', 'wall', 'azim'), parts along dimension 1
- wall_flux: float32 [2, 512], P('case', 'azim'), parts along dimension 0
There are 2 independent parts, one for each index of `case`. A program takes and returns all parts, laid end to end along the dimension named above; an argument that names none is the same for every part. Nothing has to cross between parts.
All inputs are finite; a program needn't handle non-finite values.
Results may differ from a plain program's by a relative error of at most 0.0003.
Values sent between devices are 32-bit elements; how exact they have to be, the bound alone decides.
No kernel may reach another device: no remote copies, remote signals or barrier semaphores. Data moves between devices by JAX's collectives and lax.ppermute only.
A program may use at most 64 MiB of HBM per device.

v0:
```python
import jax
import jax.numpy as jnp
from jax import lax
from jax.sharding import PartitionSpec as P

KERNEL_WEIGHTS = (0.55, 0.45)
KERNEL_RATES = (1.15, 3.4)
FILTER_STRENGTH = 0.02
COUPLING = 0.1


def with_halo(block, sides, width):
    for axis, dim in sides:
        count = lax.axis_size(axis)
        forward = [(i, i + 1) for i in range(count - 1)]
        forward.append((count - 1, 0))
        backward = [(target, source) for source, target in forward]
        low = lax.ppermute(
            lax.slice_in_dim(block, block.shape[dim] - width, None, axis=dim), axis, forward
        )
        high = lax.ppermute(lax.slice_in_dim(block, 0, width, axis=dim), axis, backward)
        block = jnp.concatenate([low, block, high], axis=dim)
    return block


def band_tables(absorb_index, band_index, cross_sections, band_fractions):
    entries = cross_sections.shape[0]
    table_slots = lax.broadcasted_iota(jnp.int32, (1, 1, entries), 2)
    spectral_absorber_area = jnp.sum(
        jnp.where(absorb_index[:, :, None] == table_slots, cross_sections[None, None, :], 0.0),
        axis=2,
    )
    chosen_values = jnp.where(band_index[:, None] == table_slots[0], band_fractions[None, :], 0.0)
    return (spectral_absorber_area, jnp.sum(chosen_values, axis=1))


def viewing_line_irradiance(
    kinetic_heat_level,
    species_concentrations,
    spectral_absorber_area,
    spectral_fraction_weight,
    mesh_cell_width,
    viewing_line_dimension,
):
    absorption = jnp.einsum(
        "kb,kij->bij",
        spectral_absorber_area,
        species_concentrations,
        precision=lax.Precision.HIGHEST,
    )
    optical_thickness_step = absorption * mesh_cell_width
    optical_depth = (
        lax.cumsum(optical_thickness_step, viewing_line_dimension) - 0.5 * optical_thickness_step
    )
    radiated_energy_rate = (
        spectral_fraction_weight[:, None, None]
        * kinetic_heat_level[None] ** 4
        * optical_thickness_step
    )
    net_flux = 0.0
    wall_flux = 0.0
    for weight, decay_rate in zip(KERNEL_WEIGHTS, KERNEL_RATES):
        growth = jnp.exp(decay_rate * optical_depth)
        falloff = jnp.exp(-decay_rate * optical_depth)
        upward = falloff * lax.cumsum(radiated_energy_rate * growth, viewing_line_dimension)
        tail_sum = lax.cumsum(radiated_energy_rate * falloff, viewing_line_dimension, reverse=True)
        net_flux = net_flux + weight * jnp.sum(upward - growth * tail_sum, axis=0)
        wall_flux = wall_flux + weight * jnp.sum(
            lax.index_in_dim(tail_sum, 0, viewing_line_dimension, keepdims=False), axis=0
        )
    return (net_flux, wall_flux)


def edge_pad(net_flux, viewing_line_dimension):
    count = net_flux.shape[viewing_line_dimension]
    first_row = lax.slice_in_dim(net_flux, 0, 1, axis=viewing_line_dimension)
    last_row = lax.slice_in_dim(net_flux, count - 1, count, axis=viewing_line_dimension)
    return jnp.concatenate([first_row, net_flux, last_row], viewing_line_dimension)


def divergence(padded, viewing_line_dimension, mesh_cell_width):
    count = padded.shape[viewing_line_dimension] - 2
    before = lax.slice_in_dim(padded, 0, count, axis=viewing_line_dimension)
    after = lax.slice_in_dim(padded, 2, count + 2, axis=viewing_line_dimension)
    return (before - after) / (2.0 * mesh_cell_width)


def tendency(shifted, courant, heating):
    gradient = (
        45.0 * (shifted(1) - shifted(-1))
        - 9.0 * (shifted(2) - shifted(-2))
        + (shifted(3) - shifted(-3))
    ) / 60.0
    smoothing = (
        shifted(-3)
        + shifted(3)
        - 6.0 * (shifted(-2) + shifted(2))
        + 15.0 * (shifted(-1) + shifted(1))
        - 20.0 * shifted(0)
    )
    change_sum = FILTER_STRENGTH * smoothing - courant[None] * gradient
    return change_sum.at[0].add(COUPLING * heating)


def radiate(current, spectral_absorber_area, spectral_fraction_weight, mesh_cell_width):
    components, stations, row_count, col_count = current.shape
    line_data = jnp.transpose(current, (0, 2, 1, 3)).reshape(
        components, row_count, stations * col_count
    )
    gathered = lax.all_gather(line_data, "wall", axis=1, tiled=True)
    net_flux, wall_flux = viewing_line_irradiance(
        gathered[0],
        gathered[1:],
        spectral_absorber_area,
        spectral_fraction_weight,
        mesh_cell_width,
        1,
    )
    padded = edge_pad(net_flux, 0)
    row_start = lax.axis_index("wall") * row_count
    heating = divergence(
        lax.dynamic_slice_in_dim(padded, row_start, row_count + 2, 0), 0, mesh_cell_width
    )
    heating = jnp.transpose(heating.reshape(row_count, stations, col_count), (1, 0, 2))
    return (heating, wall_flux.reshape(stations, col_count))


def local(state, courant, cross_sections, band_fractions, absorb_index, band_index):
    spectral_absorber_area, spectral_fraction_weight = band_tables(
        absorb_index, band_index, cross_sections, band_fractions
    )
    mesh_cell_width = 1.0 / (state.shape[2] * lax.axis_size("wall"))
    col_count = state.shape[3]

    def segment_change(current):
        heating, wall_flux = radiate(
            current, spectral_absorber_area, spectral_fraction_weight, mesh_cell_width
        )
        padded = with_halo(current, (("azim", 3),), 3)

        def shifted(offset):
            return lax.slice_in_dim(padded, 3 + offset, 3 + offset + col_count, axis=3)

        return (tendency(shifted, courant, heating), wall_flux)

    first_change, first_flux = segment_change(state)
    middle = state + first_change
    second_change, second_flux = segment_change(middle)
    new_state = 0.5 * (state + middle + second_change)
    return (new_state, 0.5 * (first_flux + second_flux))


def solution(mesh):
    return jax.shard_map(
        local,
        mesh=mesh,
        in_specs=(P(None, "case", "wall", "azim"), P("case", "wall", "azim"), P(), P(), P(), P()),
        out_specs=(P(None, "case", "wall", "azim"), P("case", "azim")),
        check_vma=False,
    )
```

profile of v0, /device:TPU:0, one launch (start us, length us, event | category | flops | bytes accessed | tf_op | source)
XLA Modules:
  0.0 42.3 jit_solution(989441874617617582)
XLA Ops:
  0.6 0.0 copy-start
  0.6 1.0 %fusion.71 = (f32[12,1,8,3]{3,2,1,0:T(8,128)S(1)}, f32[12,1,8,3]{3,2,1,0:T(8,128)S(1)}) fusion(f32[12,1,8,128]{3,2,1,0:T(8,128)} %param.10), kind=kLoop, calls=%fused_computation.127 | loop fusion | bytes 4608 | tf_op jit(solution)/shard_map/slice | solution.py:21
  1.6 2.4 %collective-permute-start.1 = (f32[12,1,8,3]{3,2,1,0:T(8,128)S(1)}, f32[12,1,8,3]{3,2,1,0:T(8,128)S(1)}, u32[]{:S(2)}, u32[]{:S(2)}) collective-permute-start(f32[12,1,8,3]{3,2,1,0:T(8,128)S(1)} %get-tuple-element.34), channel_id=1, source_target_pairs={{1,0},{2,1},{3,2},{0,3},{5,4},{6,5},{7,6},{4,7},{9,8},{10,9},{11,1... | collective-permute-start | bytes 3464 | tf_op jit(solution)/shard_map/ppermute | solution.py:21
  4.0 0.0 collective-permute-start
  4.0 0.0 copy-done
  4.0 0.1 copy.53
  4.1 14.1 %all-gather = f32[12,1,32,128]{3,1,0,2:T(1,128)S(1)} all-gather(f32[12,1,8,128]{3,1,0,2:T(1,128)S(1)} %copy.53), channel_id=2, replica_groups=mesh['case'=2,'wall'=4,'azim'=4] {'wall'}, dimensions={2}, use_global_device_ids=true | all-gather | bytes 245760 | tf_op jit(solution)/shard_map/all_gather | solution.py:110
  18.2 0.0 copy-start.1
  18.2 0.0 copy-start.3
  18.3 0.6 %copy-done.1 = s32[11,16]{1,0:T(8,128)S(1)} copy-done((s32[11,16]{1,0:T(8,128)S(1)}, s32[11,16]{1,0:T(8,128)}, u32[]{:S(2)}) %copy-start.1) | copy-done | bytes 728
  18.9 0.0 copy-done.3
  18.9 0.2 select_reduce_fusion
  19.1 0.4 fusion.5
  19.5 0.0 copy-start.4
  19.6 0.0 copy-start.5
  19.6 0.6 %copy-done.4 = f32[64]{0:T(128)S(1)} copy-done((f32[64]{0:T(128)S(1)}, f32[64]{0:T(128)}, u32[]{:S(2)}) %copy-start.4) | copy-done | bytes 280
  20.2 0.0 copy-done.5
  20.2 0.2 select_reduce_fusion.1
  20.4 0.2 fusion.16
  20.7 0.2 fusion.21
  20.9 0.2 fusion.74
  21.1 0.2 fusion.75
  21.4 0.0 copy-start.2
  21.4 0.7 %copy-done.2 = f32[1,8,128]{2,1,0:T(8,128)S(1)} copy-done((f32[1,8,128]{2,1,0:T(8,128)S(1)}, f32[1,8,128]{2,1,0:T(8,128)}, u32[]{:S(2)}) %copy-start.2) | copy-done | bytes 4120
  22.1 0.0 collective-permute-done.1
  22.2 0.0 collective-permute-done
  22.2 0.2 multiply_subtract_fusion.1
  22.4 0.1 copy.56
  22.5 0.1 fusion.70
  22.5 13.8 %all-gather.1 = f32[12,1,32,128]{3,1,0,2:T(1,128)S(1)} all-gather(f32[12,1,8,128]{3,1,0,2:T(1,128)S(1)} %copy.56), channel_id=3, replica_groups=mesh['case'=2,'wall'=4,'azim'=4] {'wall'}, dimensions={2}, use_global_device_ids=true | all-gather | bytes 245760 | tf_op jit(solution)/shard_map/all_gather | solution.py:110
  36.4 0.4 fusion.4
  36.8 0.2 fusion.6
  37.1 0.2 fusion.11
  37.3 0.2 fusion.76
  37.6 0.2 fusion.77
  37.8 0.1 collective-permute-start.3
  37.9 0.5 %collective-permute-start.2 = (f32[12,1,8,3]{3,2,1,0:T(8,128)S(1)}, f32[12,1,8,3]{3,2,1,0:T(8,128)S(1)}, u32[]{:S(2)}, u32[]{:S(2)}) collective-permute-start(f32[12,1,8,3]{3,2,1,0:T(8,128)S(1)} %get-tuple-element.33), channel_id=1, source_target_pairs={{0,1},{1,2},{2,3},{3,0},{4,5},{5,6},{6,7},{7,4},{8,9},{9,10},{10,1... | collective-permute-start | bytes 3464 | tf_op jit(solution)/shard_map/ppermute | solution.py:18
  38.4 0.5 %multiply_bitcast_fusion.1 = f32[1,128]{1,0:T(1,128)} fusion(f32[128]{0:T(128)S(1)} %get-tuple-element.40, f32[128]{0:T(128)S(1)} %get-tuple-element.41, f32[128]{0:T(128)S(1)} %get-tuple-element.42, f32[128]{0:T(128)S(1)} %get-tuple-element.43), kind=kLoop, calls=%fused_computation.115 | loop fusion | flops 1024 | bytes 2560 | tf_op jit(solution)/shard_map/mul | solution.py:150
  38.9 0.7 %collective-permute-done.3 = f32[12,1,8,3]{3,2,1,0:T(8,128)S(1)} collective-permute-done((f32[12,1,8,3]{3,2,1,0:T(8,128)S(1)}, f32[12,1,8,3]{3,2,1,0:T(8,128)S(1)}, u32[]{:S(2)}, u32[]{:S(2)}) %collective-permute-start.3) | collective-permute-done | bytes 1184 | tf_op jit(solution)/shard_map/ppermute | solution.py:21
  39.7 1.8 %collective-permute-done.2 = f32[12,1,8,3]{3,2,1,0:T(8,128)S(1)} collective-permute-done((f32[12,1,8,3]{3,2,1,0:T(8,128)S(1)}, f32[12,1,8,3]{3,2,1,0:T(8,128)S(1)}, u32[]{:S(2)}, u32[]{:S(2)}) %collective-permute-start.2) | collective-permute-done | bytes 1184 | tf_op jit(solution)/shard_map/ppermute | solution.py:18
  41.5 0.2 multiply_subtract_fusion
  41.7 0.6 %add_multiply_fusion = f32[12,1,8,128]{3,2,1,0:T(8,128)} fusion(f32[12,1,8,128]{3,2,1,0:T(8,128)S(1)} %fusion.55, f32[12,1,8,128]{3,2,1,0:T(8,128)S(1)} %copy-done, f32[12,1,8,128]{3,2,1,0:T(8,128)S(1)} %add.105), kind=kLoop, calls=%fused_computation.75 | loop fusion | flops 36864 | bytes 196608 | tf_op jit(solution)/shard_map/mul | solution.py:149
  (20 shorter events, 0.3 us)
Async XLA Ops:
  0.6 3.4 %copy-start = (f32[12,1,8,128]{3,2,1,0:T(8,128)S(1)}, f32[12,1,8,128]{3,2,1,0:T(8,128)}, u32[]{:S(2)}) copy-start(f32[12,1,8,128]{3,2,1,0:T(8,128)} %param.10) | copy-start | bytes 147460
  1.6 20.5 %collective-permute-start.1 = (f32[12,1,8,3]{3,2,1,0:T(8,128)S(1)}, f32[12,1,8,3]{3,2,1,0:T(8,128)S(1)}, u32[]{:S(2)}, u32[]{:S(2)}) collective-permute-start(f32[12,1,8,3]{3,2,1,0:T(8,128)S(1)} %get-tuple-element.34), channel_id=1, source_target_pairs={{1,0},{2,1},{3,2},{0,3},{5,4},{6,5},{7,6},{4,7},{9,8},{10,9},{11,1... | collective-permute-start | bytes 3464 | tf_op jit(solution)/shard_map/ppermute | solution.py:21
  4.0 18.2 %collective-permute-start = (f32[12,1,8,3]{3,2,1,0:T(8,128)S(1)}, f32[12,1,8,3]{3,2,1,0:T(8,128)S(1)}, u32[]{:S(2)}, u32[]{:S(2)}) collective-permute-start(f32[12,1,8,3]{3,2,1,0:T(8,128)S(1)} %get-tuple-element.35), channel_id=1, source_target_pairs={{0,1},{1,2},{2,3},{3,0},{4,5},{5,6},{6,7},{7,4},{8,9},{9,10},{10,1... | collective-permute-start | bytes 3464 | tf_op jit(solution)/shard_map/ppermute | solution.py:18
  18.2 0.7 %copy-start.1 = (s32[11,16]{1,0:T(8,128)S(1)}, s32[11,16]{1,0:T(8,128)}, u32[]{:S(2)}) copy-start(s32[11,16]{1,0:T(8,128)} %param.14) | copy-start | bytes 2116
  18.2 0.7 %copy-start.3 = (f32[64]{0:T(128)S(1)}, f32[64]{0:T(128)}, u32[]{:S(2)}) copy-start(f32[64]{0:T(128)} %param.12) | copy-start | bytes 772
  19.5 0.7 %copy-start.4 = (f32[64]{0:T(128)S(1)}, f32[64]{0:T(128)}, u32[]{:S(2)}) copy-start(f32[64]{0:T(128)} %param.13) | copy-start | bytes 772
  19.6 0.7 %copy-start.5 = (s32[16]{0:T(128)S(1)}, s32[16]{0:T(128)}, u32[]{:S(2)}) copy-start(s32[16]{0:T(128)} %param.15) | copy-start | bytes 196
  21.4 0.7 %copy-start.2 = (f32[1,8,128]{2,1,0:T(8,128)S(1)}, f32[1,8,128]{2,1,0:T(8,128)}, u32[]{:S(2)}) copy-start(f32[1,8,128]{2,1,0:T(8,128)} %param.11) | copy-start | bytes 12292
  37.8 1.8 %collective-permute-start.3 = (f32[12,1,8,3]{3,2,1,0:T(8,128)S(1)}, f32[12,1,8,3]{3,2,1,0:T(8,128)S(1)}, u32[]{:S(2)}, u32[]{:S(2)}) collective-permute-start(f32[12,1,8,3]{3,2,1,0:T(8,128)S(1)} %get-tuple-element.32), channel_id=1, source_target_pairs={{1,0},{2,1},{3,2},{0,3},{5,4},{6,5},{7,6},{4,7},{9,8},{10,9},{11,1... | collective-permute-start | bytes 3464 | tf_op jit(solution)/shard_map/ppermute | solution.py:21
  37.9 3.6 %collective-permute-start.2 = (f32[12,1,8,3]{3,2,1,0:T(8,128)S(1)}, f32[12,1,8,3]{3,2,1,0:T(8,128)S(1)}, u32[]{:S(2)}, u32[]{:S(2)}) collective-permute-start(f32[12,1,8,3]{3,2,1,0:T(8,128)S(1)} %get-tuple-element.33), channel_id=1, source_target_pairs={{0,1},{1,2},{2,3},{3,0},{4,5},{5,6},{6,7},{7,4},{8,9},{9,10},{10,1... | collective-permute-start | bytes 3464 | tf_op jit(solution)/shard_map/ppermute | solution.py:18
where the time goes:
time: 42.6 us; the launch traced here: 42.3 us
  blocking collectives  27.9 us (65%)
  other arithmetic  4.04 us (9%)
  local copies, waits for them, and re-layouts  3.18 us (7%)
  starting transfers between devices  2.94 us (7%)
  waiting for transfers between devices  2.52 us (6%)
  between operations  0.89 us (2%)
  matrix products  0.84 us (2%)
    all_gather x2, blocking collectives, radiate(): gathered = lax.all_gather(line_data, 'wall', axis=1, tiled=True)  27.9 us
    ppermute x2, starting transfers between devices, with_halo(): lax.ppermute(lax.slice_in_dim(block, 0, width, axis=dim), axis, backward)  2.44 us
    unnamed x14, local copies, waits for them, and re-layouts  2 us
    ppermute x2, waiting for transfers between devices, with_halo(): lax.ppermute(lax.slice_in_dim(block, block.shape[dim] - width, None, axis...  1.79 us
    slice x2, local copies, waits for them, and re-layouts, with_halo(): lax.slice_in_dim(block, 0, width, axis=dim)  1.05 us
    another operation x6, other arithmetic, viewing_line_irradiance(): lax.cumsum(optical_thickness_step, viewing_line_dimension)  1.01 us
    another operation x4, other arithmetic, viewing_line_irradiance(): lax.cumsum(radiated_energy_rate * falloff, viewing_line_dimension, revers...  0.98 us
  transfers between devices with their start and end apart: 4, of which 2 were waited for; matrix products, arithmetic and copies ran while one was open for 6% of the time, Pallas kernels for 0%

commit v1 on v0

v1 whole, which is shorter than its diff:
```python
import functools

import jax
import jax.numpy as jnp
from jax import lax
from jax.experimental import pallas as pl
from jax.experimental.pallas import tpu as pltpu
from jax.sharding import PartitionSpec as P

KERNEL_WEIGHTS = (0.55, 0.45)
KERNEL_RATES = (1.15, 3.4)
COUPLING = 0.1
LOG2E = 1.4426950408889634
COMPS = 12
SPECIES = 11
BANDS = 16
EDGE = 6
COURANT = 12
TO_RIGHT = 13
TO_LEFT = 14
TILES = 15
HEAT_SLOT = 13
OFFSETS = (1, -1, 2, -2, 3, -3)


def lanes(shape):
    return lax.broadcasted_iota(jnp.int32, shape, len(shape) - 1)


def roll(x, shift):
    return pltpu.roll(x, shift % x.shape[-1], x.ndim - 1)


def pack_kernel(state_ref, courant_ref, block_ref):
    tile = courant_ref.shape
    cols = tile[-1]
    lane = lanes(tile)
    to_right = jnp.zeros(tile, jnp.float32)
    to_left = jnp.zeros(tile, jnp.float32)
    for k in range(COMPS + 1):
        value = state_ref[k] if k < COMPS else courant_ref[...]
        block_ref[k] = value
        here = (lane >= EDGE * k) & (lane < EDGE * (k + 1))
        to_right = jnp.where(here, roll(value, EDGE * k - (cols - EDGE)), to_right)
        to_left = jnp.where(here, roll(value, EDGE * k), to_left)
    block_ref[TO_RIGHT] = to_right
    block_ref[TO_LEFT] = to_left


def loop(count, body, carry):
    if count <= 4:
        for i in range(count):
            carry = body(i, carry)
        return carry
    return lax.fori_loop(0, count, body, carry)


def radiate(blocks, me, rows, cross_ref, share_ref, step_ref, emit_ref, decay_ref, up_ref, down_ref, net_ref, heat_ref):
    count = step_ref.shape[0]
    parts = count // rows
    cols = step_ref.shape[-1]

    def absorb(slot, carry):
        block = blocks(slot)
        base = (me ^ slot) * rows
        hot = block[0]
        hot = hot * hot
        hot = hot * hot
        for r in range(rows):
            step = None
            for k in range(SPECIES):
                term = cross_ref[k] * block[1 + k, pl.ds(r, 1), :]
                step = term if step is None else step + term
            step_ref[base + r] = step
            emit_ref[base + r] = share_ref[...] * step * hot[r : r + 1]
        return carry

    loop(parts, absorb, 0)

    def attenuate(part, before):
        for r in range(rows):
            at = part * rows + r
            step = step_ref[at]
            gap = before + step
            for i, rate in enumerate(KERNEL_RATES):
                decay_ref[i, at] = jnp.exp2(gap * (-0.5 * LOG2E * rate))
            before = step
        return before

    zero = jnp.zeros((BANDS, cols), jnp.float32)
    loop(parts, attenuate, zero)

    ratio = KERNEL_WEIGHTS[1] / KERNEL_WEIGHTS[0]

    def halve(x):
        return x[: BANDS // 2] + x[BANDS // 2 :]

    def sweep(part, carry):
        up0, up1, down0, down1 = carry
        for r in range(rows):
            at = part * rows + r
            emitted = emit_ref[at]
            up0 = up0 * decay_ref[0, at] + emitted
            up1 = up1 * decay_ref[1, at] + emitted
            up_ref[at] = halve(up0 + ratio * up1)
            back = count - 1 - at
            emitted = emit_ref[back]
            down0 = down0 + emitted
            down1 = down1 + emitted
            down_ref[back] = halve(down0 + ratio * down1)
            down0 = down0 * decay_ref[0, back]
            down1 = down1 * decay_ref[1, back]
        return up0, up1, down0, down1

    _, _, down0, down1 = loop(parts, sweep, (zero, zero, zero, zero))
    wall = KERNEL_WEIGHTS[0] * jnp.sum(down0 + ratio * down1, axis=0, keepdims=True)

    def combine(part, carry):
        rows_here = pl.ds(part * rows, rows)
        net = jnp.sum(up_ref[rows_here] - down_ref[rows_here], axis=1)
        net_ref[pl.ds(pl.multiple_of(part * rows + rows, rows), rows), :] = net
        return carry

    loop(parts, combine, 0)
    net_ref[rows - 1 : rows, :] = net_ref[rows : rows + 1, :]
    net_ref[rows + count : rows + count + 1, :] = net_ref[rows + count - 1 : rows + count, :]
    scale = KERNEL_WEIGHTS[0] * count / 2.0
    for part in range(parts):
        first = part * rows + rows
        heat_ref[part] = (net_ref[first - 1 : first - 1 + rows, :] - net_ref[first + 1 : first + 1 + rows, :]) * scale
    return wall


def slot_of(slots, s):
    return slots[0].at[s] if len(slots) == 1 else slots[s]


def first_kernel(given, parts, *refs):
    slots = refs[:given]
    cross_ref, share_ref, heating_ref, wall_ref, right_ref, left_ref = refs[given : given + 6]
    scratch = refs[given + 6 :]
    heat_ref = scratch[-1]
    tile = heating_ref.shape[1:]
    rows, cols = tile
    me = lax.axis_index("wall")
    wall_ref[...] = radiate(lambda s: slot_of(slots, s), me, rows, cross_ref, share_ref, *scratch)
    for s in range(parts):
        heating = heat_ref[me ^ s]
        heating_ref[s] = heating
        block = slot_of(slots, s)
        to_right = block[TO_RIGHT]
        to_left = block[TO_LEFT]
        if s == 0:
            lane = lanes(tile)
            here = (lane >= EDGE * HEAT_SLOT) & (lane < EDGE * (HEAT_SLOT + 1))
            to_right = jnp.where(here, roll(heating, EDGE * HEAT_SLOT - (cols - EDGE)), to_right)
            to_left = jnp.where(here, roll(heating, EDGE * HEAT_SLOT), to_left)
        right_ref[s] = to_right
        left_ref[s] = to_left


def coefficients(courant):
    return (0.3 - 0.75 * courant, 0.3 + 0.75 * courant, 0.15 * courant - 0.12, -0.12 - 0.15 * courant, 0.02 - courant / 60.0, 0.02 + courant / 60.0)


def stencil(value, halo, factors, lane, cols):
    total = 0.6 * value
    for offset, factor in zip(OFFSETS, factors):
        if halo is None:
            source = value
        elif offset > 0:
            source = jnp.where(lane < offset, halo, value)
        else:
            source = jnp.where(lane >= cols + offset, halo, value)
        total = total + factor * roll(source, -offset)
    return total


def second_kernel(given, parts, *refs):
    slots = refs[:given]
    (heating_ref, wall_in_ref, from_left_ref, from_right_ref, cross_ref, share_ref, out_ref, wall_ref, middle_ref, edge_ref) = refs[given : given + 10]
    scratch = refs[given + 10 :]
    own = slot_of(slots, 0)
    heat_ref = scratch[-1]
    tile = heating_ref.shape[1:]
    rows, cols = tile
    half = cols // 2
    lane = lanes(tile)
    me = lax.axis_index("wall")

    def advance(s, carry):
        left, right = from_left_ref[s], from_right_ref[s]
        three = EDGE // 2
        both = jnp.where(lane % EDGE < three, roll(left, -three), roll(right, three))
        block = slot_of(slots, s)
        factors = coefficients(block[COURANT])
        for k in range(COMPS):
            halo = roll(both, -(EDGE * k + three))
            moved = stencil(block[k], halo, factors, lane, cols)
            if k == 0:
                moved = moved + COUPLING * heating_ref[s]
            middle_ref[s, k] = moved
        return carry

    loop(parts, advance, 0)

    left, right = from_left_ref[0], from_right_ref[0]

    def placed(k, value):
        from_left = roll(left, half - EDGE - EDGE * k)
        from_right = roll(right, -EDGE * k)
        inner = from_left
        if value is not None:
            inner = jnp.where(lane < half, from_left, jnp.where(lane < half + half // 2, roll(value, half), value))
        return jnp.where(lane < EDGE, from_right, inner)

    factors = coefficients(placed(COURANT, None))
    for k in range(COMPS):
        moved = stencil(placed(k, own[k]), None, factors, lane, cols)
        if k == 0:
            moved = moved + COUPLING * placed(HEAT_SLOT, None)
        edge_ref[k] = jnp.where(lane < half // 2, moved, roll(moved, half))

    wall = radiate(lambda s: middle_ref.at[s], me, rows, cross_ref, share_ref, *scratch)
    wall_ref[...] = 0.5 * (wall_in_ref[...] + wall)
    heating = heat_ref[me]
    factors = coefficients(own[COURANT])
    for k in range(COMPS):
        moved = stencil(middle_ref[0, k], edge_ref[k], factors, lane, cols)
        if k == 0:
            moved = moved + COUPLING * heating
        out_ref[k] = 0.5 * (own[k] + moved)


def band_tables(absorb_index, band_index, cross_sections, band_fractions, height, cols):
    entries = cross_sections.shape[0]
    table_slots = lax.broadcasted_iota(jnp.int32, (1, 1, entries), 2)
    area = jnp.sum(jnp.where(absorb_index[:, :, None] == table_slots, cross_sections[None, None, :], 0.0), axis=2)
    share = jnp.sum(jnp.where(band_index[:, None] == table_slots[0], band_fractions[None, :], 0.0), axis=1)
    area = jnp.broadcast_to((area * height)[:, :, None], area.shape + (cols,))
    return area, jnp.broadcast_to(share[:, None], share.shape + (cols,))


def exchange(x, axis, distance):
    return lax.ppermute(x, axis, [(i, i ^ distance) for i in range(lax.axis_size(axis))])


def gather_lines(block, axis):
    count = lax.axis_size(axis)
    distance = count // 2
    if count > 4:
        stack = block[None]
        for step in range(count.bit_length() - 1):
            stack = jnp.concatenate([stack, exchange(stack, axis, 1 << step)])
        return [stack]
    held = {0: block}
    while distance:
        for slot in list(held):
            held[slot ^ distance] = exchange(held[slot], axis, distance)
        distance //= 2
    return [held[s] for s in range(count)]


def call(kernel, outs, scratch, *args):
    vmem = pl.BlockSpec(memory_space=pltpu.VMEM)
    return pl.pallas_call(
        kernel,
        out_shape=[jax.ShapeDtypeStruct(shape, jnp.float32) for shape in outs],
        in_specs=[vmem] * len(args),
        out_specs=[vmem] * len(outs),
        scratch_shapes=[pltpu.VMEM(shape, jnp.float32) for shape in scratch],
        compiler_params=pltpu.CompilerParams(vmem_limit_bytes=32 * 1024 * 1024),
    )(*args)


def local(state, courant, cross_sections, band_fractions, absorb_index, band_index):
    comps, stations, rows, cols = state.shape
    parts = lax.axis_size("wall")
    count = parts * rows
    ring = lax.axis_size("azim")
    tile = (rows, cols)
    (block,) = call(pack_kernel, [(TILES,) + tile], [], state.reshape(comps, rows, cols), courant.reshape(tile))
    slots = gather_lines(block, "wall")
    cross, share = band_tables(absorb_index, band_index, cross_sections, band_fractions, 1.0 / count, cols)
    deep = (count, BANDS, cols)
    flat = (count, BANDS // 2, cols)
    scratch = [deep, deep, (2,) + deep, flat, flat, (count + 2 * rows, cols), (parts,) + tile]
    whole = (parts,) + tile
    heating, wall, right, left = call(
        functools.partial(first_kernel, len(slots), parts), [whole, (1, cols), whole, whole], scratch, *slots, cross, share
    )
    from_left = lax.ppermute(right, "azim", [(i, (i + 1) % ring) for i in range(ring)])
    from_right = lax.ppermute(left, "azim", [(i, (i - 1) % ring) for i in range(ring)])
    middle = (parts, comps) + tile
    new_state, wall = call(
        functools.partial(second_kernel, len(slots), parts),
        [(comps,) + tile, (1, cols)],
        [middle, (comps,) + tile] + scratch,
        *slots, heating, wall, from_left, from_right, cross, share,
    )
    return new_state.reshape(state.shape), wall


def solution(mesh):
    return jax.shard_map(
        local,
        mesh=mesh,
        in_specs=(P(None, "case", "wall", "azim"), P("case", "wall", "azim"), P(), P(), P(), P()),
        out_specs=(P(None, "case", "wall", "azim"), P("case", "azim")),
        check_vma=False,
    )
```

time: 42.6 us -> 23.3 us (0.55)
  the two profiles are of different devices: /device:TPU:0 before, /device:TPU:1 now
where the time goes in v1:
time: 23.3 us; the launch traced here: 23.1 us
  starting transfers between devices  10.2 us (44%)
  waiting for transfers between devices  5.25 us (23%)
  Pallas kernels  4.9 us (21%)
  local copies, waits for them, and re-layouts  1.65 us (7%)
  between operations  0.7 us (3%)
  other arithmetic  0.36 us (2%)
    ppermute x3, starting transfers between devices, exchange(): lax.ppermute(x, axis, [(i, i ^ distance) for i in range(lax.axis_size(axi...  5.95 us
    pallas_call x3, Pallas kernels, call(): pl.pallas_call(kernel, out_shape=[jax.ShapeDtypeStruct(shape, jnp.float32...  4.9 us
    ppermute x1, starting transfers between devices, local(): lax.ppermute(right, 'azim', [(i, (i + 1) % ring) for i in range(ring)])  4.29 us
    ppermute x1, waiting for transfers between devices, local(): lax.ppermute(left, 'azim', [(i, (i - 1) % ring) for i in range(ring)])  2.29 us
    ppermute x3, waiting for transfers between devices, exchange(): lax.ppermute(x, axis, [(i, i ^ distance) for i in range(lax.axis_size(axi...  2.09 us
    unnamed x12, local copies, waits for them, and re-layouts  1.5 us
    ppermute x1, waiting for transfers between devices, local(): lax.ppermute(right, 'azim', [(i, (i + 1) % ring) for i in range(ring)])  0.87 us
  transfers between devices with their start and end apart: 5, of which 5 were waited for; matrix products, arithmetic and copies ran while one was open for 2% of the time, Pallas kernels for 0%

profile of v1, /device:TPU:1, one launch (start us, length us, event | category | flops | bytes accessed | tf_op | source)
XLA Modules:
  0.0 23.1 jit_solution(13686803962704056373)
XLA Ops:
  0.6 0.0 copy-start
  0.6 0.8 %copy-done = f32[12,1,8,128]{3,2,1,0:T(8,128)S(1)} copy-done((f32[12,1,8,128]{3,2,1,0:T(8,128)S(1)}, f32[12,1,8,128]{3,2,1,0:T(8,128)}, u32[]{:S(2)}) %copy-start) | copy-done | bytes 49176
  1.4 0.0 copy-start.1
  1.4 0.7 %copy-done.1 = f32[1,8,128]{2,1,0:T(8,128)S(1)} copy-done((f32[1,8,128]{2,1,0:T(8,128)S(1)}, f32[1,8,128]{2,1,0:T(8,128)}, u32[]{:S(2)}) %copy-start.1) | copy-done | bytes 4120
  2.1 0.0 copy-start.2
  2.1 0.0 copy-start.3
  2.1 0.1 shard_map.77.refs_0_
  2.2 3.2 %collective-permute-start.1 = (f32[15,8,128]{2,1,0:T(8,128)S(1)}, f32[15,8,128]{2,1,0:T(8,128)S(1)}, u32[]{:S(2)}, u32[]{:S(2)}) collective-permute-start(f32[15,8,128]{2,1,0:T(8,128)S(1)} %shard_map.77.refs_0_), channel_id=1, source_target_pairs={{0,8},{4,12},{8,0},{12,4},{1,9},{5,13},{9,1},{13,5},{2,10},{6,14},... | collective-permute-start | bytes 184328 | tf_op jit(solution)/shard_map/ppermute | solution.py:245
  5.4 1.3 %collective-permute-start = (f32[15,8,128]{2,1,0:T(8,128)S(1)}, f32[15,8,128]{2,1,0:T(8,128)S(1)}, u32[]{:S(2)}, u32[]{:S(2)}) collective-permute-start(f32[15,8,128]{2,1,0:T(8,128)S(1)} %shard_map.77.refs_0_), channel_id=1, source_target_pairs={{0,4},{4,0},{8,12},{12,8},{1,5},{5,1},{9,13},{13,9},{2,6},{6,2},{1... | collective-permute-start | bytes 184328 | tf_op jit(solution)/shard_map/ppermute | solution.py:245
  6.7 0.0 copy-done.2
  6.7 0.0 copy-done.3
  6.7 0.2 select_reduce_fusion
  6.9 0.0 copy-start.4
  6.9 0.0 copy-start.5
  6.9 0.1 collective-permute-done.1.refs_2_
  7.0 1.4 %collective-permute-start.2 = (f32[15,8,128]{2,1,0:T(8,128)S(1)}, f32[15,8,128]{2,1,0:T(8,128)S(1)}, u32[]{:S(2)}, u32[]{:S(2)}) collective-permute-start(f32[15,8,128]{2,1,0:T(8,128)S(1)} %collective-permute-done.1.refs_2_), channel_id=1, source_target_pairs={{0,4},{4,0},{8,12},{12,8},{1,5},{5,1},{9,13},{13,9},{2,6},{6,2},{1... | collective-permute-start | bytes 184328 | tf_op jit(solution)/shard_map/ppermute | solution.py:245
  8.5 0.0 copy-done.4
  8.5 0.0 copy-done.5
  8.5 0.2 select_reduce_fusion.1
  8.7 0.2 collective-permute-done.refs_1_
  8.8 1.8 %collective-permute-done.2.refs_3_ = f32[15,8,128]{2,1,0:T(8,128)S(1)} collective-permute-done((f32[15,8,128]{2,1,0:T(8,128)S(1)}, f32[15,8,128]{2,1,0:T(8,128)S(1)}, u32[]{:S(2)}, u32[]{:S(2)}) %collective-permute-start.2) | collective-permute-done | bytes 61472 | tf_op jit(solution)/shard_map/ppermute | solution.py:245
  10.7 0.1 broadcast_in_dim.45.refs_5_.refs_9_
  10.7 0.1 broadcast_in_dim.42.refs_4_.refs_8_
  10.8 0.5 %shard_map.78 = (f32[4,8,128]{2,1,0:T(8,128)S(1)}, f32[1,128]{1,0:T(1,128)S(1)}, f32[4,8,128]{2,1,0:T(8,128)S(1)}, f32[4,8,128]{2,1,0:T(8,128)S(1)}) custom-call(f32[15,8,128]{2,1,0:T(8,128)S(1)} %shard_map.77.refs_0_, f32[15,8,128]{2,1,0:T(8,128)S(1)} %collective-permute-done.refs_1_, f32[15,8,128]{2,1,0:T(8,128)S(1)} %collective-permute-done.1.refs_2_, ...), custom_call_target="tpu_custom_call" | custom-call | tf_op jit(solution)/shard_map/pallas_call | solution.py:266
  11.3 4.3 %collective-permute-start.3 = (f32[4,8,128]{2,1,0:T(8,128)S(1)}, f32[4,8,128]{2,1,0:T(8,128)S(1)}, u32[]{:S(2)}, u32[]{:S(2)}) collective-permute-start(f32[4,8,128]{2,1,0:T(8,128)S(1)} %get-tuple-element.10), channel_id=1, source_target_pairs={{0,1},{1,2},{2,3},{3,0},{4,5},{5,6},{6,7},{7,4},{8,9},{9,10},{10,1... | collective-permute-start | bytes 49160 | tf_op jit(solution)/shard_map/ppermute | solution.py:292
  15.6 0.0 collective-permute-start.4
  15.6 0.9 %collective-permute-done.3.refs_6_ = f32[4,8,128]{2,1,0:T(8,128)S(1)} collective-permute-done((f32[4,8,128]{2,1,0:T(8,128)S(1)}, f32[4,8,128]{2,1,0:T(8,128)S(1)}, u32[]{:S(2)}, u32[]{:S(2)}) %collective-permute-start.3) | collective-permute-done | bytes 16416 | tf_op jit(solution)/shard_map/ppermute | solution.py:292
  16.5 2.3 %collective-permute-done.4.refs_7_ = f32[4,8,128]{2,1,0:T(8,128)S(1)} collective-permute-done((f32[4,8,128]{2,1,0:T(8,128)S(1)}, f32[4,8,128]{2,1,0:T(8,128)S(1)}, u32[]{:S(2)}, u32[]{:S(2)}) %collective-permute-start.4) | collective-permute-done | bytes 16416 | tf_op jit(solution)/shard_map/ppermute | solution.py:293
  18.8 4.3 %shard_map.79 = (f32[12,8,128]{2,1,0:T(8,128)}, f32[1,128]{1,0:T(1,128)}) custom-call(f32[15,8,128]{2,1,0:T(8,128)S(1)} %shard_map.77.refs_0_, f32[15,8,128]{2,1,0:T(8,128)S(1)} %collective-permute-done.refs_1_, f32[15,8,128]{2,1,0:T(8,128)S(1)} %collective-permute-done.1.refs_2_, f32[15,8,128]{2,1,0:T(8,128)S(1)} %collective-permute-done.2.refs_3_, ...), custom_call_target="tpu_custom_call" | custom-call | tf_op jit(solution)/shard_map/pallas_call | solution.py:266
  (1 shorter events, 0.0 us)
Async XLA Ops:
  0.6 0.8 %copy-start = (f32[12,1,8,128]{3,2,1,0:T(8,128)S(1)}, f32[12,1,8,128]{3,2,1,0:T(8,128)}, u32[]{:S(2)}) copy-start(f32[12,1,8,128]{3,2,1,0:T(8,128)} %param.6) | copy-start | bytes 147460
  1.4 0.7 %copy-start.1 = (f32[1,8,128]{2,1,0:T(8,128)S(1)}, f32[1,8,128]{2,1,0:T(8,128)}, u32[]{:S(2)}) copy-start(f32[1,8,128]{2,1,0:T(8,128)} %param.7) | copy-start | bytes 12292
  2.1 4.6 %copy-start.2 = (s32[11,16]{1,0:T(8,128)S(1)}, s32[11,16]{1,0:T(8,128)}, u32[]{:S(2)}) copy-start(s32[11,16]{1,0:T(8,128)} %param.10) | copy-start | bytes 2116
  2.1 4.6 %copy-start.3 = (f32[64]{0:T(128)S(1)}, f32[64]{0:T(128)}, u32[]{:S(2)}) copy-start(f32[64]{0:T(128)} %param.8) | copy-start | bytes 772
  2.2 4.8 %collective-permute-start.1 = (f32[15,8,128]{2,1,0:T(8,128)S(1)}, f32[15,8,128]{2,1,0:T(8,128)S(1)}, u32[]{:S(2)}, u32[]{:S(2)}) collective-permute-start(f32[15,8,128]{2,1,0:T(8,128)S(1)} %shard_map.77.refs_0_), channel_id=1, source_target_pairs={{0,8},{4,12},{8,0},{12,4},{1,9},{5,13},{9,1},{13,5},{2,10},{6,14},... | collective-permute-start | bytes 184328 | tf_op jit(solution)/shard_map/ppermute | solution.py:245
  5.4 3.4 %collective-permute-start = (f32[15,8,128]{2,1,0:T(8,128)S(1)}, f32[15,8,128]{2,1,0:T(8,128)S(1)}, u32[]{:S(2)}, u32[]{:S(2)}) collective-permute-start(f32[15,8,128]{2,1,0:T(8,128)S(1)} %shard_map.77.refs_0_), channel_id=1, source_target_pairs={{0,4},{4,0},{8,12},{12,8},{1,5},{5,1},{9,13},{13,9},{2,6},{6,2},{1... | collective-permute-start | bytes 184328 | tf_op jit(solution)/shard_map/ppermute | solution.py:245
  6.9 1.6 %copy-start.4 = (f32[64]{0:T(128)S(1)}, f32[64]{0:T(128)}, u32[]{:S(2)}) copy-start(f32[64]{0:T(128)} %param.9) | copy-start | bytes 772
  6.9 1.6 %copy-start.5 = (s32[16]{0:T(128)S(1)}, s32[16]{0:T(128)}, u32[]{:S(2)}) copy-start(s32[16]{0:T(128)} %param.11) | copy-start | bytes 196
  7.0 3.6 %collective-permute-start.2 = (f32[15,8,128]{2,1,0:T(8,128)S(1)}, f32[15,8,128]{2,1,0:T(8,128)S(1)}, u32[]{:S(2)}, u32[]{:S(2)}) collective-permute-start(f32[15,8,128]{2,1,0:T(8,128)S(1)} %collective-permute-done.1.refs_2_), channel_id=1, source_target_pairs={{0,4},{4,0},{8,12},{12,8},{1,5},{5,1},{9,13},{13,9},{2,6},{6,2},{1... | collective-permute-start | bytes 184328 | tf_op jit(solution)/shard_map/ppermute | solution.py:245
  11.3 5.2 %collective-permute-start.3 = (f32[4,8,128]{2,1,0:T(8,128)S(1)}, f32[4,8,128]{2,1,0:T(8,128)S(1)}, u32[]{:S(2)}, u32[]{:S(2)}) collective-permute-start(f32[4,8,128]{2,1,0:T(8,128)S(1)} %get-tuple-element.10), channel_id=1, source_target_pairs={{0,1},{1,2},{2,3},{3,0},{4,5},{5,6},{6,7},{7,4},{8,9},{9,10},{10,1... | collective-permute-start | bytes 49160 | tf_op jit(solution)/shard_map/ppermute | solution.py:292
  15.6 3.2 %collective-permute-start.4 = (f32[4,8,128]{2,1,0:T(8,128)S(1)}, f32[4,8,128]{2,1,0:T(8,128)S(1)}, u32[]{:S(2)}, u32[]{:S(2)}) collective-permute-start(f32[4,8,128]{2,1,0:T(8,128)S(1)} %get-tuple-element.11), channel_id=1, source_target_pairs={{0,3},{1,0},{2,1},{3,2},{4,7},{5,4},{6,5},{7,6},{8,11},{9,8},{10,9... | collective-permute-start | bytes 49160 | tf_op jit(solution)/shard_map/ppermute | solution.py:293

commit v2 on v1

--- a/solution.py
+++ b/solution.py
@@ -176,27 +176,40 @@
     return total
 
 
-def second_kernel(given, parts, *refs):
+def advance_kernel(given, parts, *refs):
     slots = refs[:given]
-    (heating_ref, wall_in_ref, from_left_ref, from_right_ref, cross_ref, share_ref, out_ref, wall_ref, middle_ref, edge_ref) = refs[given : given + 10]
-    scratch = refs[given + 10 :]
+    heating_ref, from_left_ref, from_right_ref, middle_ref, edge_ref, halo_ref, near_ref = refs[given:]
     own = slot_of(slots, 0)
-    heat_ref = scratch[-1]
     tile = heating_ref.shape[1:]
     rows, cols = tile
     half = cols // 2
     lane = lanes(tile)
-    me = lax.axis_index("wall")
+    three = EDGE // 2
+    first_half = lax.rem(lane, EDGE) < three
+
+    def place(s, carry):
+        both = jnp.where(first_half, roll(from_left_ref[s], -three), roll(from_right_ref[s], three))
+        for k in range(COMPS):
+            halo_ref[s, k] = roll(both, -(EDGE * k + three))
+        return carry
+
+    loop(parts, place, 0)
+
+    left, right = from_left_ref[0], from_right_ref[0]
+    for k in range(HEAT_SLOT + 1):
+        from_left = roll(left, half - EDGE - EDGE * k)
+        from_right = roll(right, -EDGE * k)
+        inner = from_left
+        if k < COMPS:
+            value = own[k]
+            inner = jnp.where(lane < half, from_left, jnp.where(lane < half + half // 2, roll(value, half), value))
+        near_ref[k] = jnp.where(lane < EDGE, from_right, inner)
 
     def advance(s, carry):
-        left, right = from_left_ref[s], from_right_ref[s]
-        three = EDGE // 2
-        both = jnp.where(lane % EDGE < three, roll(left, -three), roll(right, three))
         block = slot_of(slots, s)
         factors = coefficients(block[COURANT])
         for k in range(COMPS):
-            halo = roll(both, -(EDGE * k + three))
-            moved = stencil(block[k], halo, factors, lane, cols)
+            moved = stencil(block[k], halo_ref[s, k], factors, lane, cols)
             if k == 0:
                 moved = moved + COUPLING * heating_ref[s]
             middle_ref[s, k] = moved
@@ -204,31 +217,30 @@
 
     loop(parts, advance, 0)
 
-    left, right = from_left_ref[0], from_right_ref[0]
-
-    def placed(k, value):
-        from_left = roll(left, half - EDGE - EDGE * k)
-        from_right = roll(right, -EDGE * k)
-        inner = from_left
-        if value is not None:
-            inner = jnp.where(lane < half, from_left, jnp.where(lane < half + half // 2, roll(value, half), value))
-        return jnp.where(lane < EDGE, from_right, inner)
-
-    factors = coefficients(placed(COURANT, None))
+    factors = coefficients(near_ref[COURANT])
     for k in range(COMPS):
-        moved = stencil(placed(k, own[k]), None, factors, lane, cols)
+        moved = stencil(near_ref[k], None, factors, lane, cols)
         if k == 0:
-            moved = moved + COUPLING * placed(HEAT_SLOT, None)
+            moved = moved + COUPLING * near_ref[HEAT_SLOT]
+        halo_ref[0, k] = moved
+    for k in range(COMPS):
+        moved = halo_ref[0, k]
         edge_ref[k] = jnp.where(lane < half // 2, moved, roll(moved, half))
 
+
+def last_kernel(given, block_ref, middle_ref, edge_ref, wall_in_ref, cross_ref, share_ref, out_ref, wall_ref, *scratch):
+    heat_ref = scratch[-1]
+    own = block_ref if given > 1 else block_ref.at[0]
+    rows, cols = out_ref.shape[1:]
+    lane = lanes((rows, cols))
+    me = lax.axis_index("wall")
     wall = radiate(lambda s: middle_ref.at[s], me, rows, cross_ref, share_ref, *scratch)
     wall_ref[...] = 0.5 * (wall_in_ref[...] + wall)
-    heating = heat_ref[me]
     factors = coefficients(own[COURANT])
     for k in range(COMPS):
         moved = stencil(middle_ref[0, k], edge_ref[k], factors, lane, cols)
         if k == 0:
-            moved = moved + COUPLING * heating
+            moved = moved + COUPLING * heat_ref[me]
         out_ref[k] = 0.5 * (own[k] + moved)
 
 
@@ -291,12 +303,15 @@
     )
     from_left = lax.ppermute(right, "azim", [(i, (i + 1) % ring) for i in range(ring)])
     from_right = lax.ppermute(left, "azim", [(i, (i - 1) % ring) for i in range(ring)])
-    middle = (parts, comps) + tile
+    middle, edge = call(
+        functools.partial(advance_kernel, len(slots), parts),
+        [(parts, comps) + tile, (comps,) + tile],
+        [(parts, comps) + tile, (HEAT_SLOT + 1,) + tile],
+        *slots, heating, from_left, from_right,
+    )
     new_state, wall = call(
-        functools.partial(second_kernel, len(slots), parts),
-        [(comps,) + tile, (1, cols)],
-        [middle, (comps,) + tile] + scratch,
-        *slots, heating, wall, from_left, from_right, cross, share,
+        functools.partial(last_kernel, len(slots)), [(comps,) + tile, (1, cols)], scratch,
+        slots[0], middle, edge, wall, cross, share,
     )
     return new_state.reshape(state.shape), wall
 

time: 23.3 us -> 20.8 us (0.89)
  Pallas kernels: 4.9 us -> 2.42 us
    pallas_call x3 -> x4, Pallas kernels: 4.9 us -> 2.42 us  [call(): pl.pallas_call(kernel, out_shape=[jax.ShapeDtypeStruct(shape, jnp.float32...]
where the time goes in v2:
time: 20.8 us; the launch traced here: 20.6 us
  starting transfers between devices  10.2 us (49%)
  waiting for transfers between devices  5.25 us (25%)
  Pallas kernels  2.42 us (12%)
  local copies, waits for them, and re-layouts  1.65 us (8%)
  between operations  0.7 us (3%)
  other arithmetic  0.36 us (2%)
    ppermute x3, starting transfers between devices, exchange(): lax.ppermute(x, axis, [(i, i ^ distance) for i in range(lax.axis_size(axi...  5.95 us
    ppermute x1, starting transfers between devices, local(): lax.ppermute(right, 'azim', [(i, (i + 1) % ring) for i in range(ring)])  4.29 us
    pallas_call x4, Pallas kernels, call(): pl.pallas_call(kernel, out_shape=[jax.ShapeDtypeStruct(shape, jnp.float32...  2.42 us
    ppermute x1, waiting for transfers between devices, local(): lax.ppermute(left, 'azim', [(i, (i - 1) % ring) for i in range(ring)])  2.29 us
    ppermute x3, waiting for transfers between devices, exchange(): lax.ppermute(x, axis, [(i, i ^ distance) for i in range(lax.axis_size(axi...  2.09 us
    unnamed x12, local copies, waits for them, and re-layouts  1.5 us
    ppermute x1, waiting for transfers between devices, local(): lax.ppermute(right, 'azim', [(i, (i + 1) % ring) for i in range(ring)])  0.87 us
  transfers between devices with their start and end apart: 5, of which 5 were waited for; matrix products, arithmetic and copies ran while one was open for 2% of the time, Pallas kernels for 0%

profile of v2, /device:TPU:1, one launch (start us, length us, event | category | flops | bytes accessed | tf_op | source)
XLA Modules:
  0.0 20.6 jit_solution(8094626130522773469)
XLA Ops:
  0.6 0.0 copy-start
  0.6 0.8 %copy-done = f32[12,1,8,128]{3,2,1,0:T(8,128)S(1)} copy-done((f32[12,1,8,128]{3,2,1,0:T(8,128)S(1)}, f32[12,1,8,128]{3,2,1,0:T(8,128)}, u32[]{:S(2)}) %copy-start) | copy-done | bytes 49176
  1.4 0.0 copy-start.1
  1.4 0.7 %copy-done.1 = f32[1,8,128]{2,1,0:T(8,128)S(1)} copy-done((f32[1,8,128]{2,1,0:T(8,128)S(1)}, f32[1,8,128]{2,1,0:T(8,128)}, u32[]{:S(2)}) %copy-start.1) | copy-done | bytes 4120
  2.1 0.0 copy-start.2
  2.1 0.0 copy-start.3
  2.1 0.1 shard_map.77.refs_0_.block_ref
  2.2 3.2 %collective-permute-start.1 = (f32[15,8,128]{2,1,0:T(8,128)S(1)}, f32[15,8,128]{2,1,0:T(8,128)S(1)}, u32[]{:S(2)}, u32[]{:S(2)}) collective-permute-start(f32[15,8,128]{2,1,0:T(8,128)S(1)} %shard_map.77.refs_0_.block_ref), channel_id=1, source_target_pairs={{0,8},{4,12},{8,0},{12,4},{1,9},{5,13},{9,1},{13,5},{2,10},{6,14},... | collective-permute-start | bytes 184328 | tf_op jit(solution)/shard_map/ppermute | solution.py:257
  5.4 1.3 %collective-permute-start = (f32[15,8,128]{2,1,0:T(8,128)S(1)}, f32[15,8,128]{2,1,0:T(8,128)S(1)}, u32[]{:S(2)}, u32[]{:S(2)}) collective-permute-start(f32[15,8,128]{2,1,0:T(8,128)S(1)} %shard_map.77.refs_0_.block_ref), channel_id=1, source_target_pairs={{0,4},{4,0},{8,12},{12,8},{1,5},{5,1},{9,13},{13,9},{2,6},{6,2},{1... | collective-permute-start | bytes 184328 | tf_op jit(solution)/shard_map/ppermute | solution.py:257
  6.7 0.0 copy-done.2
  6.7 0.0 copy-done.3
  6.7 0.2 select_reduce_fusion
  6.9 0.0 copy-start.4
  6.9 0.0 copy-start.5
  6.9 0.1 collective-permute-done.1.refs_2_
  7.0 1.4 %collective-permute-start.2 = (f32[15,8,128]{2,1,0:T(8,128)S(1)}, f32[15,8,128]{2,1,0:T(8,128)S(1)}, u32[]{:S(2)}, u32[]{:S(2)}) collective-permute-start(f32[15,8,128]{2,1,0:T(8,128)S(1)} %collective-permute-done.1.refs_2_), channel_id=1, source_target_pairs={{0,4},{4,0},{8,12},{12,8},{1,5},{5,1},{9,13},{13,9},{2,6},{6,2},{1... | collective-permute-start | bytes 184328 | tf_op jit(solution)/shard_map/ppermute | solution.py:257
  8.5 0.0 copy-done.4
  8.5 0.0 copy-done.5
  8.5 0.2 select_reduce_fusion.1
  8.7 0.2 collective-permute-done.refs_1_
  8.8 1.8 %collective-permute-done.2.refs_3_ = f32[15,8,128]{2,1,0:T(8,128)S(1)} collective-permute-done((f32[15,8,128]{2,1,0:T(8,128)S(1)}, f32[15,8,128]{2,1,0:T(8,128)S(1)}, u32[]{:S(2)}, u32[]{:S(2)}) %collective-permute-start.2) | collective-permute-done | bytes 61472 | tf_op jit(solution)/shard_map/ppermute | solution.py:257
  10.7 0.1 broadcast_in_dim.45.refs_5_.share_ref
  10.7 0.1 broadcast_in_dim.42.refs_4_.cross_ref
  10.8 0.5 %shard_map.78 = (f32[4,8,128]{2,1,0:T(8,128)S(1)}, f32[1,128]{1,0:T(1,128)S(1)}, f32[4,8,128]{2,1,0:T(8,128)S(1)}, f32[4,8,128]{2,1,0:T(8,128)S(1)}) custom-call(f32[15,8,128]{2,1,0:T(8,128)S(1)} %shard_map.77.refs_0_.block_ref, f32[15,8,128]{2,1,0:T(8,128)S(1)} %collective-permute-done.refs_1_, f32[15,8,128]{2,1,0:T(8,128)S(1)} %collective-permute-done.1.refs_2_, ...), custom_call_target="tpu_custom_call" | custom-call | tf_op jit(solution)/shard_map/pallas_call | solution.py:278
  11.3 4.3 %collective-permute-start.3 = (f32[4,8,128]{2,1,0:T(8,128)S(1)}, f32[4,8,128]{2,1,0:T(8,128)S(1)}, u32[]{:S(2)}, u32[]{:S(2)}) collective-permute-start(f32[4,8,128]{2,1,0:T(8,128)S(1)} %get-tuple-element.11), channel_id=1, source_target_pairs={{0,1},{1,2},{2,3},{3,0},{4,5},{5,6},{6,7},{7,4},{8,9},{9,10},{10,1... | collective-permute-start | bytes 49160 | tf_op jit(solution)/shard_map/ppermute | solution.py:304
  15.6 0.0 collective-permute-start.4
  15.6 0.9 %collective-permute-done.3.refs_5_ = f32[4,8,128]{2,1,0:T(8,128)S(1)} collective-permute-done((f32[4,8,128]{2,1,0:T(8,128)S(1)}, f32[4,8,128]{2,1,0:T(8,128)S(1)}, u32[]{:S(2)}, u32[]{:S(2)}) %collective-permute-start.3) | collective-permute-done | bytes 16416 | tf_op jit(solution)/shard_map/ppermute | solution.py:304
  16.5 2.3 %collective-permute-done.4.refs_6_ = f32[4,8,128]{2,1,0:T(8,128)S(1)} collective-permute-done((f32[4,8,128]{2,1,0:T(8,128)S(1)}, f32[4,8,128]{2,1,0:T(8,128)S(1)}, u32[]{:S(2)}, u32[]{:S(2)}) %collective-permute-start.4) | collective-permute-done | bytes 16416 | tf_op jit(solution)/shard_map/ppermute | solution.py:305
  18.8 0.7 %shard_map.79 = (f32[4,12,8,128]{3,2,1,0:T(8,128)S(1)}, f32[12,8,128]{2,1,0:T(8,128)S(1)}) custom-call(f32[15,8,128]{2,1,0:T(8,128)S(1)} %shard_map.77.refs_0_.block_ref, f32[15,8,128]{2,1,0:T(8,128)S(1)} %collective-permute-done.refs_1_, f32[15,8,128]{2,1,0:T(8,128)S(1)} %collective-permute-done.1.refs_2_, ...), custom_call_target="tpu_custom_call" | custom-call | tf_op jit(solution)/shard_map/pallas_call | solution.py:278
  19.5 1.1 %shard_map.80 = (f32[12,8,128]{2,1,0:T(8,128)}, f32[1,128]{1,0:T(1,128)}) custom-call(f32[15,8,128]{2,1,0:T(8,128)S(1)} %shard_map.77.refs_0_.block_ref, f32[4,12,8,128]{3,2,1,0:T(8,128)S(1)} %get-tuple-element.13.middle_ref, f32[12,8,128]{2,1,0:T(8,128)S(1)} %get-tuple-element.14.edge_ref, f32[1,128]{1,0:T(1,128)S(1)} %get-tuple-element.15.wall_in_ref, ...), custom_call_target="tpu_custom_call" | custom-call | tf_op jit(solution)/shard_map/pallas_call | solution.py:278
  (1 shorter events, 0.0 us)
Async XLA Ops:
  0.6 0.8 %copy-start = (f32[12,1,8,128]{3,2,1,0:T(8,128)S(1)}, f32[12,1,8,128]{3,2,1,0:T(8,128)}, u32[]{:S(2)}) copy-start(f32[12,1,8,128]{3,2,1,0:T(8,128)} %param.6) | copy-start | bytes 147460
  1.4 0.7 %copy-start.1 = (f32[1,8,128]{2,1,0:T(8,128)S(1)}, f32[1,8,128]{2,1,0:T(8,128)}, u32[]{:S(2)}) copy-start(f32[1,8,128]{2,1,0:T(8,128)} %param.7) | copy-start | bytes 12292
  2.1 4.6 %copy-start.2 = (s32[11,16]{1,0:T(8,128)S(1)}, s32[11,16]{1,0:T(8,128)}, u32[]{:S(2)}) copy-start(s32[11,16]{1,0:T(8,128)} %param.10) | copy-start | bytes 2116
  2.1 4.6 %copy-start.3 = (f32[64]{0:T(128)S(1)}, f32[64]{0:T(128)}, u32[]{:S(2)}) copy-start(f32[64]{0:T(128)} %param.8) | copy-start | bytes 772
  2.2 4.8 %collective-permute-start.1 = (f32[15,8,128]{2,1,0:T(8,128)S(1)}, f32[15,8,128]{2,1,0:T(8,128)S(1)}, u32[]{:S(2)}, u32[]{:S(2)}) collective-permute-start(f32[15,8,128]{2,1,0:T(8,128)S(1)} %shard_map.77.refs_0_.block_ref), channel_id=1, source_target_pairs={{0,8},{4,12},{8,0},{12,4},{1,9},{5,13},{9,1},{13,5},{2,10},{6,14},... | collective-permute-start | bytes 184328 | tf_op jit(solution)/shard_map/ppermute | solution.py:257
  5.4 3.4 %collective-permute-start = (f32[15,8,128]{2,1,0:T(8,128)S(1)}, f32[15,8,128]{2,1,0:T(8,128)S(1)}, u32[]{:S(2)}, u32[]{:S(2)}) collective-permute-start(f32[15,8,128]{2,1,0:T(8,128)S(1)} %shard_map.77.refs_0_.block_ref), channel_id=1, source_target_pairs={{0,4},{4,0},{8,12},{12,8},{1,5},{5,1},{9,13},{13,9},{2,6},{6,2},{1... | collective-permute-start | bytes 184328 | tf_op jit(solution)/shard_map/ppermute | solution.py:257
  6.9 1.6 %copy-start.4 = (f32[64]{0:T(128)S(1)}, f32[64]{0:T(128)}, u32[]{:S(2)}) copy-start(f32[64]{0:T(128)} %param.9) | copy-start | bytes 772
  6.9 1.6 %copy-start.5 = (s32[16]{0:T(128)S(1)}, s32[16]{0:T(128)}, u32[]{:S(2)}) copy-start(s32[16]{0:T(128)} %param.11) | copy-start | bytes 196
  7.0 3.6 %collective-permute-start.2 = (f32[15,8,128]{2,1,0:T(8,128)S(1)}, f32[15,8,128]{2,1,0:T(8,128)S(1)}, u32[]{:S(2)}, u32[]{:S(2)}) collective-permute-start(f32[15,8,128]{2,1,0:T(8,128)S(1)} %collective-permute-done.1.refs_2_), channel_id=1, source_target_pairs={{0,4},{4,0},{8,12},{12,8},{1,5},{5,1},{9,13},{13,9},{2,6},{6,2},{1... | collective-permute-start | bytes 184328 | tf_op jit(solution)/shard_map/ppermute | solution.py:257
  11.3 5.2 %collective-permute-start.3 = (f32[4,8,128]{2,1,0:T(8,128)S(1)}, f32[4,8,128]{2,1,0:T(8,128)S(1)}, u32[]{:S(2)}, u32[]{:S(2)}) collective-permute-start(f32[4,8,128]{2,1,0:T(8,128)S(1)} %get-tuple-element.11), channel_id=1, source_target_pairs={{0,1},{1,2},{2,3},{3,0},{4,5},{5,6},{6,7},{7,4},{8,9},{9,10},{10,1... | collective-permute-start | bytes 49160 | tf_op jit(solution)/shard_map/ppermute | solution.py:304
  15.6 3.2 %collective-permute-start.4 = (f32[4,8,128]{2,1,0:T(8,128)S(1)}, f32[4,8,128]{2,1,0:T(8,128)S(1)}, u32[]{:S(2)}, u32[]{:S(2)}) collective-permute-start(f32[4,8,128]{2,1,0:T(8,128)S(1)} %get-tuple-element.12), channel_id=1, source_target_pairs={{0,3},{1,0},{2,1},{3,2},{4,7},{5,4},{6,5},{7,6},{8,11},{9,8},{10,9... | collective-permute-start | bytes 49160 | tf_op jit(solution)/shard_map/ppermute | solution.py:305

commit v3 on v2

--- a/solution.py
+++ b/solution.py
@@ -16,9 +16,7 @@
 BANDS = 16
 EDGE = 6
 COURANT = 12
-TO_RIGHT = 13
-TO_LEFT = 14
-TILES = 15
+TILES = 13
 HEAT_SLOT = 13
 OFFSETS = (1, -1, 2, -2, 3, -3)
 
@@ -31,20 +29,32 @@
     return pltpu.roll(x, shift % x.shape[-1], x.ndim - 1)
 
 
-def pack_kernel(state_ref, courant_ref, block_ref):
-    tile = courant_ref.shape
-    cols = tile[-1]
-    lane = lanes(tile)
-    to_right = jnp.zeros(tile, jnp.float32)
-    to_left = jnp.zeros(tile, jnp.float32)
-    for k in range(COMPS + 1):
-        value = state_ref[k] if k < COMPS else courant_ref[...]
-        block_ref[k] = value
+def pack_kernel(state_ref, courant_ref, block_ref, sems):
+    copies = [
+        pltpu.make_async_copy(state_ref, block_ref.at[pl.ds(0, COMPS)], sems.at[0]),
+        pltpu.make_async_copy(courant_ref, block_ref.at[COURANT], sems.at[1]),
+    ]
+    for copy in copies:
+        copy.start()
+    for copy in copies:
+        copy.wait()
+
+
+def edge_tiles(block, lane, extra):
+    cols = lane.shape[-1]
+    last = jnp.zeros(lane.shape, jnp.float32)
+    first = jnp.zeros(lane.shape, jnp.float32)
+    for k in range(COMPS + 2):
+        if k <= COMPS:
+            value = block[k]
+        elif extra is not None:
+            value = extra
+        else:
+            continue
         here = (lane >= EDGE * k) & (lane < EDGE * (k + 1))
-        to_right = jnp.where(here, roll(value, EDGE * k - (cols - EDGE)), to_right)
-        to_left = jnp.where(here, roll(value, EDGE * k), to_left)
-    block_ref[TO_RIGHT] = to_right
-    block_ref[TO_LEFT] = to_left
+        last = jnp.where(here, roll(value, EDGE * k - (cols - EDGE)), last)
+        first = jnp.where(here, roll(value, EDGE * k), first)
+    return last, first
 
 
 def loop(count, body, carry):
@@ -137,26 +147,21 @@
 
 def first_kernel(given, parts, *refs):
     slots = refs[:given]
-    cross_ref, share_ref, heating_ref, wall_ref, right_ref, left_ref = refs[given : given + 6]
+    cross_ref, share_ref, heating_ref, wall_ref, outer_ref, inner_ref = refs[given : given + 6]
     scratch = refs[given + 6 :]
     heat_ref = scratch[-1]
     tile = heating_ref.shape[1:]
     rows, cols = tile
     me = lax.axis_index("wall")
     wall_ref[...] = radiate(lambda s: slot_of(slots, s), me, rows, cross_ref, share_ref, *scratch)
+    lane = lanes(tile)
+    odd = lax.rem(lax.axis_index("azim"), 2) == 1
     for s in range(parts):
         heating = heat_ref[me ^ s]
         heating_ref[s] = heating
-        block = slot_of(slots, s)
-        to_right = block[TO_RIGHT]
-        to_left = block[TO_LEFT]
-        if s == 0:
-            lane = lanes(tile)
-            here = (lane >= EDGE * HEAT_SLOT) & (lane < EDGE * (HEAT_SLOT + 1))
-            to_right = jnp.where(here, roll(heating, EDGE * HEAT_SLOT - (cols - EDGE)), to_right)
-            to_left = jnp.where(here, roll(heating, EDGE * HEAT_SLOT), to_left)
-        right_ref[s] = to_right
-        left_ref[s] = to_left
+        last, first = edge_tiles(slot_of(slots, s), lane, heating if s == 0 else None)
+        outer_ref[s] = jnp.where(odd, last, first)
+        inner_ref[s] = jnp.where(odd, first, last)
 
 
 def coefficients(courant):
@@ -178,7 +183,7 @@
 
 def advance_kernel(given, parts, *refs):
     slots = refs[:given]
-    heating_ref, from_left_ref, from_right_ref, middle_ref, edge_ref, halo_ref, near_ref = refs[given:]
+    heating_ref, outer_ref, inner_ref, middle_ref, edge_ref, halo_ref, near_ref = refs[given:]
     own = slot_of(slots, 0)
     tile = heating_ref.shape[1:]
     rows, cols = tile
@@ -186,16 +191,22 @@
     lane = lanes(tile)
     three = EDGE // 2
     first_half = lax.rem(lane, EDGE) < three
+    odd = lax.rem(lax.axis_index("azim"), 2) == 1
+
+    def received(s):
+        outer, inner = outer_ref[s], inner_ref[s]
+        return jnp.where(odd, inner, outer), jnp.where(odd, outer, inner)
 
     def place(s, carry):
-        both = jnp.where(first_half, roll(from_left_ref[s], -three), roll(from_right_ref[s], three))
+        left, right = received(s)
+        both = jnp.where(first_half, roll(left, -three), roll(right, three))
         for k in range(COMPS):
             halo_ref[s, k] = roll(both, -(EDGE * k + three))
         return carry
 
     loop(parts, place, 0)
 
-    left, right = from_left_ref[0], from_right_ref[0]
+    left, right = received(0)
     for k in range(HEAT_SLOT + 1):
         from_left = roll(left, half - EDGE - EDGE * k)
         from_right = roll(right, -EDGE * k)
@@ -257,31 +268,30 @@
     return lax.ppermute(x, axis, [(i, i ^ distance) for i in range(lax.axis_size(axis))])
 
 
-def gather_lines(block, axis):
+def gather_lines(block, axis, tables):
     count = lax.axis_size(axis)
     distance = count // 2
     if count > 4:
         stack = block[None]
         for step in range(count.bit_length() - 1):
             stack = jnp.concatenate([stack, exchange(stack, axis, 1 << step)])
-        return [stack]
+        return [stack], tables
     held = {0: block}
-    while distance:
-        for slot in list(held):
-            held[slot ^ distance] = exchange(held[slot], axis, distance)
-        distance //= 2
-    return [held[s] for s in range(count)]
-
-
-def call(kernel, outs, scratch, *args):
-    vmem = pl.BlockSpec(memory_space=pltpu.VMEM)
+    for d in (3,2,1): held[d]=exchange(block,axis,d)
+    return [held[s] for s in range(count)], tables
+
+
+VMEM = pl.BlockSpec(memory_space=pltpu.VMEM)
+
+
+def call(kernel, outs, scratch, *args, in_specs=None, limit=32 * 1024 * 1024):
     return pl.pallas_call(
         kernel,
         out_shape=[jax.ShapeDtypeStruct(shape, jnp.float32) for shape in outs],
-        in_specs=[vmem] * len(args),
-        out_specs=[vmem] * len(outs),
-        scratch_shapes=[pltpu.VMEM(shape, jnp.float32) for shape in scratch],
-        compiler_params=pltpu.CompilerParams(vmem_limit_bytes=32 * 1024 * 1024),
+        in_specs=in_specs or [VMEM] * len(args),
+        out_specs=[VMEM] * len(outs),
+        scratch_shapes=[pltpu.VMEM(shape, jnp.float32) if isinstance(shape, tuple) else shape for shape in scratch],
+        compiler_params=pltpu.CompilerParams(vmem_limit_bytes=limit),
     )(*args)
 
 
@@ -291,23 +301,23 @@
     count = parts * rows
     ring = lax.axis_size("azim")
     tile = (rows, cols)
-    (block,) = call(pack_kernel, [(TILES,) + tile], [], state.reshape(comps, rows, cols), courant.reshape(tile))
-    slots = gather_lines(block, "wall")
-    cross, share = band_tables(absorb_index, band_index, cross_sections, band_fractions, 1.0 / count, cols)
+    block = jnp.concatenate([state.reshape(comps, rows, cols), courant.reshape((1,) + tile)])
+    tables = band_tables(absorb_index, band_index, cross_sections, band_fractions, 1.0 / count, cols)
+    slots, (cross, share) = gather_lines(block, "wall", tables)
     deep = (count, BANDS, cols)
     flat = (count, BANDS // 2, cols)
     scratch = [deep, deep, (2,) + deep, flat, flat, (count + 2 * rows, cols), (parts,) + tile]
     whole = (parts,) + tile
-    heating, wall, right, left = call(
+    heating, wall, outer, inner = call(
         functools.partial(first_kernel, len(slots), parts), [whole, (1, cols), whole, whole], scratch, *slots, cross, share
     )
-    from_left = lax.ppermute(right, "azim", [(i, (i + 1) % ring) for i in range(ring)])
-    from_right = lax.ppermute(left, "azim", [(i, (i - 1) % ring) for i in range(ring)])
+    inner = lax.ppermute(inner, "azim", [(i, i ^ 1) for i in range(ring)])
+    outer = lax.ppermute(outer, "azim", [(i, (i + 1) % ring if i % 2 else (i - 1) % ring) for i in range(ring)])
     middle, edge = call(
         functools.partial(advance_kernel, len(slots), parts),
         [(parts, comps) + tile, (comps,) + tile],
         [(parts, comps) + tile, (HEAT_SLOT + 1,) + tile],
-        *slots, heating, from_left, from_right,
+        *slots, heating, outer, inner,
     )
     new_state, wall = call(
         functools.partial(last_kernel, len(slots)), [(comps,) + tile, (1, cols)], scratch,

time: 20.8 us -> 17.6 us (0.85)
  the two profiles are of different devices: /device:TPU:1 before, /device:TPU:0 now
where the time goes in v3:
time: 17.6 us; the launch traced here: 17.4 us
  starting transfers between devices  7.25 us (41%)
  waiting for transfers between devices  5.09 us (29%)
  Pallas kernels  2.36 us (13%)
  other arithmetic  1.19 us (7%)
  local copies, waits for them, and re-layouts  0.8 us (5%)
  between operations  0.7 us (4%)
    ppermute x3, starting transfers between devices, exchange(): lax.ppermute(x, axis, [(i, i ^ distance) for i in range(lax.axis_size(axi...  5.64 us
    ppermute x3, waiting for transfers between devices, exchange(): lax.ppermute(x, axis, [(i, i ^ distance) for i in range(lax.axis_size(axi...  3.4 us
    pallas_call x3, Pallas kernels, call(): pl.pallas_call(kernel, out_shape=[jax.ShapeDtypeStruct(shape, jnp.float32...  2.36 us
    ppermute x1, waiting for transfers between devices, local(): lax.ppermute(outer, 'azim', [(i, (i + 1) % ring if i % 2 else (i - 1) % r...  1.69 us
    ppermute x1, starting transfers between devices, local(): inner = lax.ppermute(inner, 'azim', [(i, i ^ 1) for i in range(ring)])  1.52 us
    concatenate x1, other arithmetic, local(): jnp.concatenate([state.reshape(comps, rows, cols), courant.reshape((1,) +...  0.83 us
    unnamed x8, local copies, waits for them, and re-layouts  0.66 us
  transfers between devices with their start and end apart: 5, of which 3 were waited for; matrix products, arithmetic and copies ran while one was open for 2% of the time, Pallas kernels for 0%

profile of v3, /device:TPU:0, one launch (start us, length us, event | category | flops | bytes accessed | tf_op | source)
XLA Modules:
  0.0 17.4 jit_solution(16330459720353830515)
XLA Ops:
  0.6 0.0 copy-start
  0.6 0.0 copy-start.1
  0.7 0.8 %pad_maximum_fusion.refs_0_.block_ref = f32[13,8,128]{2,1,0:T(8,128)S(1)} fusion(f32[1,8,128]{2,1,0:T(8,128)} %param.7, f32[12,8,128]{2,1,0:T(8,128)} %bitcast.4), kind=kLoop, calls=%fused_computation.2 | loop fusion | flops 13312 | bytes 106496 | tf_op jit(solution)/shard_map/concatenate | solution.py:304
  1.5 5.0 %collective-permute-start.2 = (f32[13,8,128]{2,1,0:T(8,128)S(1)}, f32[13,8,128]{2,1,0:T(8,128)S(1)}, u32[]{:S(2)}, u32[]{:S(2)}) collective-permute-start(f32[13,8,128]{2,1,0:T(8,128)S(1)} %pad_maximum_fusion.refs_0_.block_ref), channel_id=1, source_target_pairs={{0,12},{4,8},{8,4},{12,0},{1,13},{5,9},{9,5},{13,1},{2,14},{6,10},... | collective-permute-start | bytes 159752 | tf_op jit(solution)/shard_map/ppermute | solution.py:268
  6.5 0.0 collective-permute-start.1
  6.5 0.6 %collective-permute-start = (f32[13,8,128]{2,1,0:T(8,128)S(1)}, f32[13,8,128]{2,1,0:T(8,128)S(1)}, u32[]{:S(2)}, u32[]{:S(2)}) collective-permute-start(f32[13,8,128]{2,1,0:T(8,128)S(1)} %pad_maximum_fusion.refs_0_.block_ref), channel_id=1, source_target_pairs={{0,4},{4,0},{8,12},{12,8},{1,5},{5,1},{9,13},{13,9},{2,6},{6,2},{1... | collective-permute-start | bytes 159752 | tf_op jit(solution)/shard_map/ppermute | solution.py:268
  7.1 0.0 copy-done
  7.1 0.0 copy-done.1
  7.1 0.2 select_reduce_fusion
  7.3 0.0 copy-start.2
  7.3 0.0 copy-start.3
  7.3 0.6 %copy-done.2 = f32[64]{0:T(128)S(1)} copy-done((f32[64]{0:T(128)S(1)}, f32[64]{0:T(128)}, u32[]{:S(2)}) %copy-start.2) | copy-done | bytes 280
  8.0 0.0 copy-done.3
  8.0 0.2 %select_reduce_fusion.1 = f32[16]{0:T(128)S(1)} fusion(f32[64]{0:T(128)S(1)} %copy-done.2, s32[16]{0:T(128)S(1)} %copy-done.3), kind=kLoop, calls=%fused_computation.3 | loop fusion | flops 3056 | bytes 384 | tf_op jit(solution)/shard_map/reduce_sum | solution.py:262
  8.2 0.7 %collective-permute-done.2.refs_3_ = f32[13,8,128]{2,1,0:T(8,128)S(1)} collective-permute-done((f32[13,8,128]{2,1,0:T(8,128)S(1)}, f32[13,8,128]{2,1,0:T(8,128)S(1)}, u32[]{:S(2)}, u32[]{:S(2)}) %collective-permute-start.2) | collective-permute-done | bytes 53280 | tf_op jit(solution)/shard_map/ppermute | solution.py:268
  8.8 2.7 %collective-permute-done.1.refs_2_ = f32[13,8,128]{2,1,0:T(8,128)S(1)} collective-permute-done((f32[13,8,128]{2,1,0:T(8,128)S(1)}, f32[13,8,128]{2,1,0:T(8,128)S(1)}, u32[]{:S(2)}, u32[]{:S(2)}) %collective-permute-start.1) | collective-permute-done | bytes 53280 | tf_op jit(solution)/shard_map/ppermute | solution.py:268
  11.6 0.0 collective-permute-done.refs_1_
  11.6 0.1 broadcast_in_dim.45.refs_5_.share_ref
  11.6 0.1 broadcast_in_dim.42.refs_4_.cross_ref
  11.7 0.5 %shard_map.77 = (f32[4,8,128]{2,1,0:T(8,128)S(1)}, f32[1,128]{1,0:T(1,128)S(1)}, f32[4,8,128]{2,1,0:T(8,128)S(1)}, f32[4,8,128]{2,1,0:T(8,128)S(1)}) custom-call(f32[13,8,128]{2,1,0:T(8,128)S(1)} %pad_maximum_fusion.refs_0_.block_ref, f32[13,8,128]{2,1,0:T(8,128)S(1)} %collective-permute-done.refs_1_, f32[13,8,128]{2,1,0:T(8,128)S(1)} %collective-permute-done.1.refs_2_, ...), custom_call_target="tpu_custom_call" | custom-call | tf_op jit(solution)/shard_map/pallas_call | solution.py:288
  12.3 0.1 collective-permute-start.3
  12.4 1.5 %collective-permute-start.4 = (f32[4,8,128]{2,1,0:T(8,128)S(1)}, f32[4,8,128]{2,1,0:T(8,128)S(1)}, u32[]{:S(2)}, u32[]{:S(2)}) collective-permute-start(f32[4,8,128]{2,1,0:T(8,128)S(1)} %get-tuple-element.12), channel_id=1, source_target_pairs={{0,1},{1,0},{2,3},{3,2},{4,5},{5,4},{6,7},{7,6},{8,9},{9,8},{10,11... | collective-permute-start | bytes 49160 | tf_op jit(solution)/shard_map/ppermute | solution.py:314
  13.9 1.7 %collective-permute-done.3.refs_5_ = f32[4,8,128]{2,1,0:T(8,128)S(1)} collective-permute-done((f32[4,8,128]{2,1,0:T(8,128)S(1)}, f32[4,8,128]{2,1,0:T(8,128)S(1)}, u32[]{:S(2)}, u32[]{:S(2)}) %collective-permute-start.3) | collective-permute-done | bytes 16416 | tf_op jit(solution)/shard_map/ppermute | solution.py:315
  15.6 0.0 collective-permute-done.4.refs_6_
  15.6 0.7 %shard_map.78 = (f32[4,12,8,128]{3,2,1,0:T(8,128)S(1)}, f32[12,8,128]{2,1,0:T(8,128)S(1)}) custom-call(f32[13,8,128]{2,1,0:T(8,128)S(1)} %pad_maximum_fusion.refs_0_.block_ref, f32[13,8,128]{2,1,0:T(8,128)S(1)} %collective-permute-done.refs_1_, f32[13,8,128]{2,1,0:T(8,128)S(1)} %collective-permute-done.1.refs_2_, ...), custom_call_target="tpu_custom_call" | custom-call | tf_op jit(solution)/shard_map/pallas_call | solution.py:288
  16.2 1.2 %shard_map.79 = (f32[12,8,128]{2,1,0:T(8,128)}, f32[1,128]{1,0:T(1,128)}) custom-call(f32[13,8,128]{2,1,0:T(8,128)S(1)} %pad_maximum_fusion.refs_0_.block_ref, f32[4,12,8,128]{3,2,1,0:T(8,128)S(1)} %get-tuple-element.13.middle_ref, f32[12,8,128]{2,1,0:T(8,128)S(1)} %get-tuple-element.14.edge_ref, f32[1,128]{1,0:T(1,128)S(1)} %get-tuple-element.15.wall_in_ref, ...), custom_call_target="tpu_custom_call" | custom-call | tf_op jit(solution)/shard_map/pallas_call | solution.py:288
  (1 shorter events, 0.0 us)
Async XLA Ops:
  0.6 6.5 %copy-start = (s32[11,16]{1,0:T(8,128)S(1)}, s32[11,16]{1,0:T(8,128)}, u32[]{:S(2)}) copy-start(s32[11,16]{1,0:T(8,128)} %param.10) | copy-start | bytes 2116
  0.6 6.5 %copy-start.1 = (f32[64]{0:T(128)S(1)}, f32[64]{0:T(128)}, u32[]{:S(2)}) copy-start(f32[64]{0:T(128)} %param.8) | copy-start | bytes 772
  1.5 7.4 %collective-permute-start.2 = (f32[13,8,128]{2,1,0:T(8,128)S(1)}, f32[13,8,128]{2,1,0:T(8,128)S(1)}, u32[]{:S(2)}, u32[]{:S(2)}) collective-permute-start(f32[13,8,128]{2,1,0:T(8,128)S(1)} %pad_maximum_fusion.refs_0_.block_ref), channel_id=1, source_target_pairs={{0,12},{4,8},{8,4},{12,0},{1,13},{5,9},{9,5},{13,1},{2,14},{6,10},... | collective-permute-start | bytes 159752 | tf_op jit(solution)/shard_map/ppermute | solution.py:268
  6.5 5.0 %collective-permute-start.1 = (f32[13,8,128]{2,1,0:T(8,128)S(1)}, f32[13,8,128]{2,1,0:T(8,128)S(1)}, u32[]{:S(2)}, u32[]{:S(2)}) collective-permute-start(f32[13,8,128]{2,1,0:T(8,128)S(1)} %pad_maximum_fusion.refs_0_.block_ref), channel_id=1, source_target_pairs={{0,8},{4,12},{8,0},{12,4},{1,9},{5,13},{9,1},{13,5},{2,10},{6,14},... | collective-permute-start | bytes 159752 | tf_op jit(solution)/shard_map/ppermute | solution.py:268
  6.5 5.0 %collective-permute-start = (f32[13,8,128]{2,1,0:T(8,128)S(1)}, f32[13,8,128]{2,1,0:T(8,128)S(1)}, u32[]{:S(2)}, u32[]{:S(2)}) collective-permute-start(f32[13,8,128]{2,1,0:T(8,128)S(1)} %pad_maximum_fusion.refs_0_.block_ref), channel_id=1, source_target_pairs={{0,4},{4,0},{8,12},{12,8},{1,5},{5,1},{9,13},{13,9},{2,6},{6,2},{1... | collective-permute-start | bytes 159752 | tf_op jit(solution)/shard_map/ppermute | solution.py:268
  7.3 0.7 %copy-start.2 = (f32[64]{0:T(128)S(1)}, f32[64]{0:T(128)}, u32[]{:S(2)}) copy-start(f32[64]{0:T(128)} %param.9) | copy-start | bytes 772
  7.3 0.7 %copy-start.3 = (s32[16]{0:T(128)S(1)}, s32[16]{0:T(128)}, u32[]{:S(2)}) copy-start(s32[16]{0:T(128)} %param.11) | copy-start | bytes 196
  12.3 3.3 %collective-permute-start.3 = (f32[4,8,128]{2,1,0:T(8,128)S(1)}, f32[4,8,128]{2,1,0:T(8,128)S(1)}, u32[]{:S(2)}, u32[]{:S(2)}) collective-permute-start(f32[4,8,128]{2,1,0:T(8,128)S(1)} %get-tuple-element.11), channel_id=1, source_target_pairs={{0,3},{1,2},{2,1},{3,0},{4,7},{5,6},{6,5},{7,4},{8,11},{9,10},{10,... | collective-permute-start | bytes 49160 | tf_op jit(solution)/shard_map/ppermute | solution.py:315
  12.4 3.2 %collective-permute-start.4 = (f32[4,8,128]{2,1,0:T(8,128)S(1)}, f32[4,8,128]{2,1,0:T(8,128)S(1)}, u32[]{:S(2)}, u32[]{:S(2)}) collective-permute-start(f32[4,8,128]{2,1,0:T(8,128)S(1)} %get-tuple-element.12), channel_id=1, source_target_pairs={{0,1},{1,0},{2,3},{3,2},{4,5},{5,4},{6,7},{7,6},{8,9},{9,8},{10,11... | collective-permute-start | bytes 49160 | tf_op jit(solution)/shard_map/ppermute | solution.py:314

commit v4 on v3

--- a/solution.py
+++ b/solution.py
@@ -65,27 +65,23 @@
     return lax.fori_loop(0, count, body, carry)
 
 
-def radiate(blocks, me, rows, cross_ref, share_ref, step_ref, emit_ref, decay_ref, up_ref, down_ref, net_ref, heat_ref):
+def absorb(block, base, rows, cross_ref, share_ref, step_ref, emit_ref):
+    hot = block[0]
+    hot = hot * hot
+    hot = hot * hot
+    for r in range(rows):
+        step = None
+        for k in range(SPECIES):
+            term = cross_ref[k] * block[1 + k, pl.ds(r, 1), :]
+            step = term if step is None else step + term
+        step_ref[base + r] = step
+        emit_ref[base + r] = share_ref[...] * step * hot[r : r + 1]
+
+
+def radiate(rows, step_ref, emit_ref, decay_ref, up_ref, down_ref, net_ref, heat_ref):
     count = step_ref.shape[0]
     parts = count // rows
     cols = step_ref.shape[-1]
-
-    def absorb(slot, carry):
-        block = blocks(slot)
-        base = (me ^ slot) * rows
-        hot = block[0]
-        hot = hot * hot
-        hot = hot * hot
-        for r in range(rows):
-            step = None
-            for k in range(SPECIES):
-                term = cross_ref[k] * block[1 + k, pl.ds(r, 1), :]
-                step = term if step is None else step + term
-            step_ref[base + r] = step
-            emit_ref[base + r] = share_ref[...] * step * hot[r : r + 1]
-        return carry
-
-    loop(parts, absorb, 0)
 
     def attenuate(part, before):
         for r in range(rows):
@@ -141,27 +137,47 @@
     return wall
 
 
-def slot_of(slots, s):
-    return slots[0].at[s] if len(slots) == 1 else slots[s]
-
-
-def first_kernel(given, parts, *refs):
-    slots = refs[:given]
-    cross_ref, share_ref, heating_ref, wall_ref, outer_ref, inner_ref = refs[given : given + 6]
-    scratch = refs[given + 6 :]
+def arrive_kernel(slot, block_ref, cross_ref, share_ref, *refs):
+    step_ref, emit_ref, outer_ref, inner_ref = refs[-4:]
+    rows, cols = block_ref.shape[-2:]
+    lane = lanes((rows, cols))
+    me = lax.axis_index("wall")
+    odd = lax.rem(lax.axis_index("azim"), 2) == 1
+
+    def take(block, slot):
+        absorb(block, (me ^ slot) * rows, rows, cross_ref, share_ref, step_ref, emit_ref)
+        last, first = edge_tiles(block, lane, None)
+        outer_ref[slot] = jnp.where(odd, last, first)
+        inner_ref[slot] = jnp.where(odd, first, last)
+
+    if len(block_ref.shape) == 3:
+        take(block_ref, slot)
+    else:
+
+        def body(i, carry):
+            take(block_ref.at[i], i)
+            return carry
+
+        loop(block_ref.shape[0], body, 0)
+
+
+def first_kernel(step_ref, emit_ref, outer_in_ref, inner_in_ref, heating_ref, wall_ref, outer_ref, inner_ref, *scratch):
     heat_ref = scratch[-1]
-    tile = heating_ref.shape[1:]
-    rows, cols = tile
+    parts, rows, cols = heating_ref.shape
     me = lax.axis_index("wall")
-    wall_ref[...] = radiate(lambda s: slot_of(slots, s), me, rows, cross_ref, share_ref, *scratch)
-    lane = lanes(tile)
+    wall_ref[...] = radiate(rows, step_ref, emit_ref, *scratch)
+    lane = lanes((rows, cols))
     odd = lax.rem(lax.axis_index("azim"), 2) == 1
     for s in range(parts):
-        heating = heat_ref[me ^ s]
-        heating_ref[s] = heating
-        last, first = edge_tiles(slot_of(slots, s), lane, heating if s == 0 else None)
-        outer_ref[s] = jnp.where(odd, last, first)
-        inner_ref[s] = jnp.where(odd, first, last)
+        heating_ref[s] = heat_ref[me ^ s]
+        outer_ref[s] = outer_in_ref[s]
+        inner_ref[s] = inner_in_ref[s]
+    here = (lane >= EDGE * HEAT_SLOT) & (lane < EDGE * (HEAT_SLOT + 1))
+    own = heat_ref[me]
+    last = roll(own, EDGE * HEAT_SLOT - (cols - EDGE))
+    first = roll(own, EDGE * HEAT_SLOT)
+    outer_ref[0] = jnp.where(here, jnp.where(odd, last, first), outer_ref[0])
+    inner_ref[0] = jnp.where(here, jnp.where(odd, first, last), inner_ref[0])
 
 
 def coefficients(courant):
@@ -181,10 +197,11 @@
     return total
 
 
-def advance_kernel(given, parts, *refs):
-    slots = refs[:given]
-    heating_ref, outer_ref, inner_ref, middle_ref, edge_ref, halo_ref, near_ref = refs[given:]
-    own = slot_of(slots, 0)
+def advance_kernel(ids, *refs):
+    slots = refs[: len(ids)]
+    heating_ref, outer_ref, inner_ref, middle_ref, edge_ref, halo_ref, near_ref = refs[len(ids) :]
+    parts = heating_ref.shape[0]
+    own = slots[0] if len(ids) > 1 else slots[0].at[0]
     tile = heating_ref.shape[1:]
     rows, cols = tile
     half = cols // 2
@@ -216,17 +233,24 @@
             inner = jnp.where(lane < half, from_left, jnp.where(lane < half + half // 2, roll(value, half), value))
         near_ref[k] = jnp.where(lane < EDGE, from_right, inner)
 
-    def advance(s, carry):
-        block = slot_of(slots, s)
+    def advance(block, s):
         factors = coefficients(block[COURANT])
         for k in range(COMPS):
             moved = stencil(block[k], halo_ref[s, k], factors, lane, cols)
             if k == 0:
                 moved = moved + COUPLING * heating_ref[s]
             middle_ref[s, k] = moved
-        return carry
-
-    loop(parts, advance, 0)
+
+    if len(ids) > 1:
+        for block, slot in zip(slots, ids):
+            advance(block, slot)
+    else:
+
+        def body(s, carry):
+            advance(slots[0].at[s], s)
+            return carry
+
+        loop(parts, body, 0)
 
     factors = coefficients(near_ref[COURANT])
     for k in range(COMPS):
@@ -239,13 +263,20 @@
         edge_ref[k] = jnp.where(lane < half // 2, moved, roll(moved, half))
 
 
-def last_kernel(given, block_ref, middle_ref, edge_ref, wall_in_ref, cross_ref, share_ref, out_ref, wall_ref, *scratch):
+def last_kernel(block_ref, middle_ref, edge_ref, wall_in_ref, cross_ref, share_ref, out_ref, wall_ref, *scratch):
     heat_ref = scratch[-1]
-    own = block_ref if given > 1 else block_ref.at[0]
+    own = block_ref if len(block_ref.shape) == 3 else block_ref.at[0]
     rows, cols = out_ref.shape[1:]
     lane = lanes((rows, cols))
     me = lax.axis_index("wall")
-    wall = radiate(lambda s: middle_ref.at[s], me, rows, cross_ref, share_ref, *scratch)
+    step_ref, emit_ref = scratch[:2]
+
+    def take(slot, carry):
+        absorb(middle_ref.at[slot], (me ^ slot) * rows, rows, cross_ref, share_ref, step_ref, emit_ref)
+        return carry
+
+    loop(middle_ref.shape[0], take, 0)
+    wall = radiate(rows, *scratch)
     wall_ref[...] = 0.5 * (wall_in_ref[...] + wall)
     factors = coefficients(own[COURANT])
     for k in range(COMPS):
@@ -268,29 +299,30 @@
     return lax.ppermute(x, axis, [(i, i ^ distance) for i in range(lax.axis_size(axis))])
 
 
-def gather_lines(block, axis, tables):
-    count = lax.axis_size(axis)
-    distance = count // 2
-    if count > 4:
-        stack = block[None]
-        for step in range(count.bit_length() - 1):
-            stack = jnp.concatenate([stack, exchange(stack, axis, 1 << step)])
-        return [stack], tables
-    held = {0: block}
-    for d in (3,2,1): held[d]=exchange(block,axis,d)
-    return [held[s] for s in range(count)], tables
+EXCHANGES = (1, 2, 3)
+
+
+def gather_lines(block):
+    count = lax.axis_size("wall")
+    if count == 4:
+        return [block] + [exchange(block, "wall", s) for s in EXCHANGES], (0,) + EXCHANGES
+    stack = block[None]
+    for step in range(count.bit_length() - 1):
+        stack = jnp.concatenate([stack, exchange(stack, "wall", 1 << step)])
+    return [stack], (0,)
 
 
 VMEM = pl.BlockSpec(memory_space=pltpu.VMEM)
 
 
-def call(kernel, outs, scratch, *args, in_specs=None, limit=32 * 1024 * 1024):
+def call(kernel, outs, scratch, *args, aliases=None, limit=32 * 1024 * 1024):
     return pl.pallas_call(
         kernel,
         out_shape=[jax.ShapeDtypeStruct(shape, jnp.float32) for shape in outs],
-        in_specs=in_specs or [VMEM] * len(args),
+        in_specs=[VMEM] * len(args),
         out_specs=[VMEM] * len(outs),
-        scratch_shapes=[pltpu.VMEM(shape, jnp.float32) if isinstance(shape, tuple) else shape for shape in scratch],
+        scratch_shapes=[pltpu.VMEM(shape, jnp.float32) for shape in scratch],
+        input_output_aliases=aliases or {},
         compiler_params=pltpu.CompilerParams(vmem_limit_bytes=limit),
     )(*args)
 
@@ -302,26 +334,31 @@
     ring = lax.axis_size("azim")
     tile = (rows, cols)
     block = jnp.concatenate([state.reshape(comps, rows, cols), courant.reshape((1,) + tile)])
-    tables = band_tables(absorb_index, band_index, cross_sections, band_fractions, 1.0 / count, cols)
-    slots, (cross, share) = gather_lines(block, "wall", tables)
+    cross, share = band_tables(absorb_index, band_index, cross_sections, band_fractions, 1.0 / count, cols)
+    blocks, ids = gather_lines(block)
     deep = (count, BANDS, cols)
     flat = (count, BANDS // 2, cols)
-    scratch = [deep, deep, (2,) + deep, flat, flat, (count + 2 * rows, cols), (parts,) + tile]
     whole = (parts,) + tile
-    heating, wall, outer, inner = call(
-        functools.partial(first_kernel, len(slots), parts), [whole, (1, cols), whole, whole], scratch, *slots, cross, share
-    )
+    state_of = [deep, deep, whole, whole]
+    held = []
+    for received, slot in zip(blocks, ids):
+        held = call(
+            functools.partial(arrive_kernel, slot), state_of, [], received, cross, share, *held,
+            aliases={3 + j: j for j in range(len(held))},
+        )
+    scratch = [(2,) + deep, flat, flat, (count + 2 * rows, cols), whole]
+    heating, wall, outer, inner = call(first_kernel, [whole, (1, cols), whole, whole], scratch, *held)
     inner = lax.ppermute(inner, "azim", [(i, i ^ 1) for i in range(ring)])
     outer = lax.ppermute(outer, "azim", [(i, (i + 1) % ring if i % 2 else (i - 1) % ring) for i in range(ring)])
     middle, edge = call(
-        functools.partial(advance_kernel, len(slots), parts),
+        functools.partial(advance_kernel, ids),
         [(parts, comps) + tile, (comps,) + tile],
         [(parts, comps) + tile, (HEAT_SLOT + 1,) + tile],
-        *slots, heating, outer, inner,
+        *blocks, heating, outer, inner,
     )
     new_state, wall = call(
-        functools.partial(last_kernel, len(slots)), [(comps,) + tile, (1, cols)], scratch,
-        slots[0], middle, edge, wall, cross, share,
+        last_kernel, [(comps,) + tile, (1, cols)], [deep, deep] + scratch,
+        blocks[0], middle, edge, wall, cross, share,
     )
     return new_state.reshape(state.shape), wall
 

time: 17.6 us -> 17.4 us (0.989)
  waiting for transfers between devices: 5.09 us -> 4.72 us
    ppermute x3, waiting for transfers between devices: 3.4 us -> 3.03 us  [exchange(): lax.ppermute(x, axis, [(i, i ^ distance) for i in range(lax.axis_size(axi...]
    pallas_call x3 -> x7, Pallas kernels: 2.36 us -> 2.51 us  [call(): pl.pallas_call(kernel, out_shape=[jax.ShapeDtypeStruct(shape, jnp.float32...]
  transfers between devices with their start and end apart: 5 -> 5, of which waited for: 3 -> 3; matrix products, arithmetic and copies ran while one was open for 2% -> 3% of each run, Pallas kernels for 0% -> 2%
where the time goes in v4:
time: 17.4 us; the launch traced here: 17.2 us
  starting transfers between devices  7.26 us (42%)
  waiting for transfers between devices  4.72 us (27%)
  Pallas kernels  2.51 us (14%)
  other arithmetic  1.19 us (7%)
  local copies, waits for them, and re-layouts  0.81 us (5%)
  between operations  0.7 us (4%)
    ppermute x3, starting transfers between devices, exchange(): lax.ppermute(x, axis, [(i, i ^ distance) for i in range(lax.axis_size(axi...  5.64 us
    ppermute x3, waiting for transfers between devices, exchange(): lax.ppermute(x, axis, [(i, i ^ distance) for i in range(lax.axis_size(axi...  3.03 us
    pallas_call x7, Pallas kernels, call(): pl.pallas_call(kernel, out_shape=[jax.ShapeDtypeStruct(shape, jnp.float32...  2.51 us
    ppermute x1, waiting for transfers between devices, local(): lax.ppermute(outer, 'azim', [(i, (i + 1) % ring if i % 2 else (i - 1) % r...  1.68 us
    ppermute x1, starting transfers between devices, local(): inner = lax.ppermute(inner, 'azim', [(i, i ^ 1) for i in range(ring)])  1.52 us
    concatenate x1, other arithmetic, local(): jnp.concatenate([state.reshape(comps, rows, cols), courant.reshape((1,) +...  0.83 us
    unnamed x8, local copies, waits for them, and re-layouts  0.66 us
  transfers between devices with their start and end apart: 5, of which 3 were waited for; matrix products, arithmetic and copies ran while one was open for 3% of the time, Pallas kernels for 2%

profile of v4, /device:TPU:0, one launch (start us, length us, event | category | flops | bytes accessed | tf_op | source)
XLA Modules:
  0.0 17.2 jit_solution(8207222230982944513)
XLA Ops:
  0.6 0.0 copy-start
  0.6 0.0 copy-start.1
  0.7 0.8 %pad_maximum_fusion.block_ref.refs_0_ = f32[13,8,128]{2,1,0:T(8,128)S(1)} fusion(f32[1,8,128]{2,1,0:T(8,128)} %param.7, f32[12,8,128]{2,1,0:T(8,128)} %bitcast.4), kind=kLoop, calls=%fused_computation.2 | loop fusion | flops 13312 | bytes 106496 | tf_op jit(solution)/shard_map/concatenate | solution.py:336
  1.5 5.0 %collective-permute-start.2 = (f32[13,8,128]{2,1,0:T(8,128)S(1)}, f32[13,8,128]{2,1,0:T(8,128)S(1)}, u32[]{:S(2)}, u32[]{:S(2)}) collective-permute-start(f32[13,8,128]{2,1,0:T(8,128)S(1)} %pad_maximum_fusion.block_ref.refs_0_), channel_id=1, source_target_pairs={{0,12},{4,8},{8,4},{12,0},{1,13},{5,9},{9,5},{13,1},{2,14},{6,10},... | collective-permute-start | bytes 159752 | tf_op jit(solution)/shard_map/ppermute | solution.py:299
  6.5 0.0 collective-permute-start.1
  6.5 0.6 %collective-permute-start = (f32[13,8,128]{2,1,0:T(8,128)S(1)}, f32[13,8,128]{2,1,0:T(8,128)S(1)}, u32[]{:S(2)}, u32[]{:S(2)}) collective-permute-start(f32[13,8,128]{2,1,0:T(8,128)S(1)} %pad_maximum_fusion.block_ref.refs_0_), channel_id=1, source_target_pairs={{0,4},{4,0},{8,12},{12,8},{1,5},{5,1},{9,13},{13,9},{2,6},{6,2},{1... | collective-permute-start | bytes 159752 | tf_op jit(solution)/shard_map/ppermute | solution.py:299
  7.1 0.0 copy-done
  7.1 0.0 copy-done.1
  7.1 0.2 %select_reduce_fusion = f32[11,16]{1,0:T(8,128)S(1)} fusion(f32[64]{0:T(128)S(1)} %copy-done.1, s32[11,16]{1,0:T(8,128)S(1)} %copy-done), kind=kLoop, calls=%fused_computation | loop fusion | flops 33616 | bytes 1664 | tf_op jit(solution)/shard_map/reduce_sum | solution.py:292
  7.3 0.0 copy-start.2
  7.3 0.0 copy-start.3
  7.3 0.6 %copy-done.2 = f32[64]{0:T(128)S(1)} copy-done((f32[64]{0:T(128)S(1)}, f32[64]{0:T(128)}, u32[]{:S(2)}) %copy-start.2) | copy-done | bytes 280
  8.0 0.0 copy-done.3
  8.0 0.2 %select_reduce_fusion.1 = f32[16]{0:T(128)S(1)} fusion(f32[64]{0:T(128)S(1)} %copy-done.2, s32[16]{0:T(128)S(1)} %copy-done.3), kind=kLoop, calls=%fused_computation.3 | loop fusion | flops 3056 | bytes 384 | tf_op jit(solution)/shard_map/reduce_sum | solution.py:293
  8.2 0.1 broadcast_in_dim.45.share_ref
  8.2 0.1 broadcast_in_dim.42.cross_ref
  8.3 0.1 shard_map.77
  8.4 2.2 %collective-permute-done.block_ref.refs_1_ = f32[13,8,128]{2,1,0:T(8,128)S(1)} collective-permute-done((f32[13,8,128]{2,1,0:T(8,128)S(1)}, f32[13,8,128]{2,1,0:T(8,128)S(1)}, u32[]{:S(2)}, u32[]{:S(2)}) %collective-permute-start) | collective-permute-done | bytes 53280 | tf_op jit(solution)/shard_map/ppermute | solution.py:299
  10.7 0.1 shard_map.78
  10.8 0.8 %collective-permute-done.1.block_ref.refs_2_ = f32[13,8,128]{2,1,0:T(8,128)S(1)} collective-permute-done((f32[13,8,128]{2,1,0:T(8,128)S(1)}, f32[13,8,128]{2,1,0:T(8,128)S(1)}, u32[]{:S(2)}, u32[]{:S(2)}) %collective-permute-start.1) | collective-permute-done | bytes 53280 | tf_op jit(solution)/shard_map/ppermute | solution.py:299
  11.6 0.1 shard_map.79
  11.7 0.0 collective-permute-done.2.block_ref.refs_3_
  11.7 0.1 shard_map.80
  11.8 0.3 %shard_map.81 = (f32[4,8,128]{2,1,0:T(8,128)S(1)}, f32[1,128]{1,0:T(1,128)S(1)}, f32[4,8,128]{2,1,0:T(8,128)S(1)}, f32[4,8,128]{2,1,0:T(8,128)S(1)}) custom-call(f32[32,16,128]{2,1,0:T(8,128)S(1)} %get-tuple-element.38.step_ref, f32[32,16,128]{2,1,0:T(8,128)S(1)} %get-tuple-element.39.emit_ref, f32[4,8,128]{2,1,0:T(8,128)S(1)} %get-tuple-element.40.outer_in_ref, ...), custom_call_target="tpu_custom_call" | custom-call | tf_op jit(solution)/shard_map/pallas_call | solution.py:319
  12.1 0.1 collective-permute-start.3
  12.2 1.5 %collective-permute-start.4 = (f32[4,8,128]{2,1,0:T(8,128)S(1)}, f32[4,8,128]{2,1,0:T(8,128)S(1)}, u32[]{:S(2)}, u32[]{:S(2)}) collective-permute-start(f32[4,8,128]{2,1,0:T(8,128)S(1)} %get-tuple-element.44), channel_id=1, source_target_pairs={{0,1},{1,0},{2,3},{3,2},{4,5},{5,4},{6,7},{7,6},{8,9},{9,8},{10,11... | collective-permute-start | bytes 49160 | tf_op jit(solution)/shard_map/ppermute | solution.py:351
  13.7 1.7 %collective-permute-done.3.refs_5_ = f32[4,8,128]{2,1,0:T(8,128)S(1)} collective-permute-done((f32[4,8,128]{2,1,0:T(8,128)S(1)}, f32[4,8,128]{2,1,0:T(8,128)S(1)}, u32[]{:S(2)}, u32[]{:S(2)}) %collective-permute-start.3) | collective-permute-done | bytes 16416 | tf_op jit(solution)/shard_map/ppermute | solution.py:352
  15.4 0.0 collective-permute-done.4.refs_6_
  15.4 0.7 %shard_map.82 = (f32[4,12,8,128]{3,2,1,0:T(8,128)S(1)}, f32[12,8,128]{2,1,0:T(8,128)S(1)}) custom-call(f32[13,8,128]{2,1,0:T(8,128)S(1)} %pad_maximum_fusion.block_ref.refs_0_, f32[13,8,128]{2,1,0:T(8,128)S(1)} %collective-permute-done.block_ref.refs_1_, f32[13,8,128]{2,1,0:T(8,128)S(1)} %collective-permute-done.1.block_ref.refs_2_, ...), custom_call_target="tpu_custom_call" | custom-call | tf_op jit(solution)/shard_map/pallas_call | solution.py:319
  16.0 1.2 %shard_map.83 = (f32[12,8,128]{2,1,0:T(8,128)}, f32[1,128]{1,0:T(1,128)}) custom-call(f32[13,8,128]{2,1,0:T(8,128)S(1)} %pad_maximum_fusion.block_ref.refs_0_, f32[4,12,8,128]{3,2,1,0:T(8,128)S(1)} %get-tuple-element.45.middle_ref, f32[12,8,128]{2,1,0:T(8,128)S(1)} %get-tuple-element.46.edge_ref, f32[1,128]{1,0:T(1,128)S(1)} %get-tuple-element.47.wall_in_ref, ...), custom_call_target="tpu_custom_call" | custom-call | tf_op jit(solution)/shard_map/pallas_call | solution.py:319
  (1 shorter events, 0.0 us)
Async XLA Ops:
  0.6 6.5 %copy-start = (s32[11,16]{1,0:T(8,128)S(1)}, s32[11,16]{1,0:T(8,128)}, u32[]{:S(2)}) copy-start(s32[11,16]{1,0:T(8,128)} %param.10) | copy-start | bytes 2116
  0.6 6.5 %copy-start.1 = (f32[64]{0:T(128)S(1)}, f32[64]{0:T(128)}, u32[]{:S(2)}) copy-start(f32[64]{0:T(128)} %param.8) | copy-start | bytes 772
  1.5 10.2 %collective-permute-start.2 = (f32[13,8,128]{2,1,0:T(8,128)S(1)}, f32[13,8,128]{2,1,0:T(8,128)S(1)}, u32[]{:S(2)}, u32[]{:S(2)}) collective-permute-start(f32[13,8,128]{2,1,0:T(8,128)S(1)} %pad_maximum_fusion.block_ref.refs_0_), channel_id=1, source_target_pairs={{0,12},{4,8},{8,4},{12,0},{1,13},{5,9},{9,5},{13,1},{2,14},{6,10},... | collective-permute-start | bytes 159752 | tf_op jit(solution)/shard_map/ppermute | solution.py:299
  6.5 5.0 %collective-permute-start.1 = (f32[13,8,128]{2,1,0:T(8,128)S(1)}, f32[13,8,128]{2,1,0:T(8,128)S(1)}, u32[]{:S(2)}, u32[]{:S(2)}) collective-permute-start(f32[13,8,128]{2,1,0:T(8,128)S(1)} %pad_maximum_fusion.block_ref.refs_0_), channel_id=1, source_target_pairs={{0,8},{4,12},{8,0},{12,4},{1,9},{5,13},{9,1},{13,5},{2,10},{6,14},... | collective-permute-start | bytes 159752 | tf_op jit(solution)/shard_map/ppermute | solution.py:299
  6.5 4.1 %collective-permute-start = (f32[13,8,128]{2,1,0:T(8,128)S(1)}, f32[13,8,128]{2,1,0:T(8,128)S(1)}, u32[]{:S(2)}, u32[]{:S(2)}) collective-permute-start(f32[13,8,128]{2,1,0:T(8,128)S(1)} %pad_maximum_fusion.block_ref.refs_0_), channel_id=1, source_target_pairs={{0,4},{4,0},{8,12},{12,8},{1,5},{5,1},{9,13},{13,9},{2,6},{6,2},{1... | collective-permute-start | bytes 159752 | tf_op jit(solution)/shard_map/ppermute | solution.py:299
  7.3 0.7 %copy-start.2 = (f32[64]{0:T(128)S(1)}, f32[64]{0:T(128)}, u32[]{:S(2)}) copy-start(f32[64]{0:T(128)} %param.9) | copy-start | bytes 772
  7.3 0.7 %copy-start.3 = (s32[16]{0:T(128)S(1)}, s32[16]{0:T(128)}, u32[]{:S(2)}) copy-start(s32[16]{0:T(128)} %param.11) | copy-start | bytes 196
  12.1 3.3 %collective-permute-start.3 = (f32[4,8,128]{2,1,0:T(8,128)S(1)}, f32[4,8,128]{2,1,0:T(8,128)S(1)}, u32[]{:S(2)}, u32[]{:S(2)}) collective-permute-start(f32[4,8,128]{2,1,0:T(8,128)S(1)} %get-tuple-element.43), channel_id=1, source_target_pairs={{0,3},{1,2},{2,1},{3,0},{4,7},{5,6},{6,5},{7,4},{8,11},{9,10},{10,... | collective-permute-start | bytes 49160 | tf_op jit(solution)/shard_map/ppermute | solution.py:352
  12.2 3.2 %collective-permute-start.4 = (f32[4,8,128]{2,1,0:T(8,128)S(1)}, f32[4,8,128]{2,1,0:T(8,128)S(1)}, u32[]{:S(2)}, u32[]{:S(2)}) collective-permute-start(f32[4,8,128]{2,1,0:T(8,128)S(1)} %get-tuple-element.44), channel_id=1, source_target_pairs={{0,1},{1,0},{2,3},{3,2},{4,5},{5,4},{6,7},{7,6},{8,9},{9,8},{10,11... | collective-permute-start | bytes 49160 | tf_op jit(solution)/shard_map/ppermute | solution.py:351

commit v5 on v4

--- a/solution.py
+++ b/solution.py
@@ -17,7 +17,8 @@
 EDGE = 6
 COURANT = 12
 TILES = 13
-HEAT_SLOT = 13
+PACKED = EDGE * COMPS
+HEAT_AT = 96
 OFFSETS = (1, -1, 2, -2, 3, -3)
 
 
@@ -40,21 +41,22 @@
         copy.wait()
 
 
-def edge_tiles(block, lane, extra):
+def edge_tiles(block, lane):
     cols = lane.shape[-1]
     last = jnp.zeros(lane.shape, jnp.float32)
     first = jnp.zeros(lane.shape, jnp.float32)
-    for k in range(COMPS + 2):
-        if k <= COMPS:
-            value = block[k]
-        elif extra is not None:
-            value = extra
-        else:
-            continue
+    for k in range(COMPS):
         here = (lane >= EDGE * k) & (lane < EDGE * (k + 1))
-        last = jnp.where(here, roll(value, EDGE * k - (cols - EDGE)), last)
-        first = jnp.where(here, roll(value, EDGE * k), first)
+        last = jnp.where(here, roll(block[k], EDGE * k - (cols - EDGE)), last)
+        first = jnp.where(here, roll(block[k], EDGE * k), first)
     return last, first
+
+
+def spread(value, lane):
+    group = jnp.where(lane < EDGE, roll(value, EDGE // 2), 0.0)
+    for width in (1, 2, 4, 8):
+        group = group + roll(group, EDGE * width)
+    return group
 
 
 def loop(count, body, carry):
@@ -137,7 +139,7 @@
     return wall
 
 
-def arrive_kernel(slot, block_ref, cross_ref, share_ref, *refs):
+def arrive_kernel(slots, block_ref, cross_ref, share_ref, *refs):
     step_ref, emit_ref, outer_ref, inner_ref = refs[-4:]
     rows, cols = block_ref.shape[-2:]
     lane = lanes((rows, cols))
@@ -146,12 +148,12 @@
 
     def take(block, slot):
         absorb(block, (me ^ slot) * rows, rows, cross_ref, share_ref, step_ref, emit_ref)
-        last, first = edge_tiles(block, lane, None)
+        last, first = edge_tiles(block, lane)
         outer_ref[slot] = jnp.where(odd, last, first)
         inner_ref[slot] = jnp.where(odd, first, last)
 
     if len(block_ref.shape) == 3:
-        take(block_ref, slot)
+        take(block_ref, slot_here(slots))
     else:
 
         def body(i, carry):
@@ -159,6 +161,11 @@
             return carry
 
         loop(block_ref.shape[0], body, 0)
+    if slots[0] == 0:
+        own = block_ref if len(block_ref.shape) == 3 else block_ref.at[0]
+        edges = spread(own[COURANT], lane)
+        outer_ref[outer_ref.shape[0] - 1] = edges
+        inner_ref[outer_ref.shape[0] - 1] = edges
 
 
 def first_kernel(step_ref, emit_ref, outer_in_ref, inner_in_ref, heating_ref, wall_ref, outer_ref, inner_ref, *scratch):
@@ -167,17 +174,14 @@
     me = lax.axis_index("wall")
     wall_ref[...] = radiate(rows, step_ref, emit_ref, *scratch)
     lane = lanes((rows, cols))
-    odd = lax.rem(lax.axis_index("azim"), 2) == 1
     for s in range(parts):
         heating_ref[s] = heat_ref[me ^ s]
         outer_ref[s] = outer_in_ref[s]
         inner_ref[s] = inner_in_ref[s]
-    here = (lane >= EDGE * HEAT_SLOT) & (lane < EDGE * (HEAT_SLOT + 1))
-    own = heat_ref[me]
-    last = roll(own, EDGE * HEAT_SLOT - (cols - EDGE))
-    first = roll(own, EDGE * HEAT_SLOT)
-    outer_ref[0] = jnp.where(here, jnp.where(odd, last, first), outer_ref[0])
-    inner_ref[0] = jnp.where(here, jnp.where(odd, first, last), inner_ref[0])
+    here = (lane >= HEAT_AT) & (lane < HEAT_AT + EDGE)
+    edges = jnp.where(here, roll(heat_ref[me], EDGE // 2 + HEAT_AT), outer_in_ref[parts])
+    outer_ref[parts] = edges
+    inner_ref[parts] = edges
 
 
 def coefficients(courant):
@@ -197,70 +201,86 @@
     return total
 
 
-def advance_kernel(ids, *refs):
-    slots = refs[: len(ids)]
-    heating_ref, outer_ref, inner_ref, middle_ref, edge_ref, halo_ref, near_ref = refs[len(ids) :]
-    parts = heating_ref.shape[0]
-    own = slots[0] if len(ids) > 1 else slots[0].at[0]
-    tile = heating_ref.shape[1:]
-    rows, cols = tile
-    half = cols // 2
-    lane = lanes(tile)
-    three = EDGE // 2
-    first_half = lax.rem(lane, EDGE) < three
-    odd = lax.rem(lax.axis_index("azim"), 2) == 1
-
-    def received(s):
-        outer, inner = outer_ref[s], inner_ref[s]
-        return jnp.where(odd, inner, outer), jnp.where(odd, outer, inner)
-
-    def place(s, carry):
-        left, right = received(s)
-        both = jnp.where(first_half, roll(left, -three), roll(right, three))
-        for k in range(COMPS):
-            halo_ref[s, k] = roll(both, -(EDGE * k + three))
-        return carry
-
-    loop(parts, place, 0)
-
-    left, right = received(0)
-    for k in range(HEAT_SLOT + 1):
-        from_left = roll(left, half - EDGE - EDGE * k)
-        from_right = roll(right, -EDGE * k)
-        inner = from_left
-        if k < COMPS:
-            value = own[k]
-            inner = jnp.where(lane < half, from_left, jnp.where(lane < half + half // 2, roll(value, half), value))
-        near_ref[k] = jnp.where(lane < EDGE, from_right, inner)
+def center_kernel(ids, *refs):
+    blocks = refs[: len(ids)]
+    heating_ref, middle_ref, packed_ref = refs[len(ids) :]
+    rows, cols = heating_ref.shape[1:]
+    lane = lanes((rows, cols))
 
     def advance(block, s):
         factors = coefficients(block[COURANT])
+        packed_ref[s] = spread(block[COURANT], lane)
         for k in range(COMPS):
-            moved = stencil(block[k], halo_ref[s, k], factors, lane, cols)
+            moved = stencil(block[k], None, factors, lane, cols)
             if k == 0:
                 moved = moved + COUPLING * heating_ref[s]
             middle_ref[s, k] = moved
 
     if len(ids) > 1:
-        for block, slot in zip(slots, ids):
-            advance(block, slot)
+        for block, slot in zip(blocks, ids):
+            advance(block, slot_here(slot))
     else:
 
         def body(s, carry):
-            advance(slots[0].at[s], s)
+            advance(blocks[0].at[s], s)
             return carry
 
-        loop(parts, body, 0)
-
-    factors = coefficients(near_ref[COURANT])
+        loop(heating_ref.shape[0], body, 0)
+
+
+def border_kernel(middle_in_ref, packed_ref, my_outer_ref, my_inner_ref, outer_ref, inner_ref, middle_ref, edge_ref, change_ref):
+    parts, comps, rows, cols = middle_ref.shape
+    lane = lanes((rows, cols))
+    at = lax.rem(lane, EDGE)
+    three = EDGE // 2
+    odd = lax.rem(lax.axis_index("azim"), 2) == 1
+
+    def sides(s):
+        outer, inner = outer_ref[s], inner_ref[s]
+        my_outer, my_inner = my_outer_ref[s], my_inner_ref[s]
+        return (
+            jnp.where(odd, inner, outer), jnp.where(odd, outer, inner),
+            jnp.where(odd, my_outer, my_inner), jnp.where(odd, my_inner, my_outer),
+        )
+
+    def differ(s, carry):
+        left, right, last, first = sides(s)
+        left, right = left - last, right - first
+        factors = coefficients(packed_ref[s])
+        change = jnp.zeros((rows, cols), jnp.float32)
+        for reach in range(1, three + 1):
+            ahead = factors[2 * reach - 2] * roll(right, three - reach)
+            behind = factors[2 * reach - 1] * roll(left, reach - three)
+            ahead = jnp.where((at >= three - reach) & (at < three), ahead, 0.0)
+            change = change + jnp.where((at >= three) & (at < three + reach), behind, ahead)
+        change_ref[s] = change
+        return carry
+
+    loop(parts, differ, 0)
+
+    left, right, last, first = sides(0)
+    outside = jnp.where(at < three, jnp.where(odd, inner_ref[parts], outer_ref[parts]), jnp.where(odd, outer_ref[parts], inner_ref[parts]))
+    factors = dict(zip(OFFSETS, coefficients(outside)))
+    factors[0] = 0.6
+    edge = jnp.where(lane < EDGE, COUPLING * roll(outside, -HEAT_AT), 0.0)
+    for offset in range(-three, three + 1):
+        behind = roll(jnp.where(at <= EDGE - 1 + offset, left, last), -(three + offset))
+        ahead = roll(jnp.where(at < offset, first, right), three - offset)
+        edge = edge + factors[offset] * jnp.where(at <= three - 1 - offset, behind, ahead)
+    change_ref[parts] = edge
+
+    border = (lane < three) | (lane >= cols - three)
+
+    def mend(s, carry):
+        change = change_ref[s]
+        for k in range(COMPS):
+            middle_ref[s, k] = middle_in_ref[s, k] + jnp.where(border, roll(change, -(EDGE * k + three)), 0.0)
+        return carry
+
+    loop(parts, mend, 0)
+    edge = change_ref[parts]
     for k in range(COMPS):
-        moved = stencil(near_ref[k], None, factors, lane, cols)
-        if k == 0:
-            moved = moved + COUPLING * near_ref[HEAT_SLOT]
-        halo_ref[0, k] = moved
-    for k in range(COMPS):
-        moved = halo_ref[0, k]
-        edge_ref[k] = jnp.where(lane < half // 2, moved, roll(moved, half))
+        edge_ref[k] = roll(edge, -(EDGE * k + three))
 
 
 def last_kernel(block_ref, middle_ref, edge_ref, wall_in_ref, cross_ref, share_ref, out_ref, wall_ref, *scratch):
@@ -299,17 +319,28 @@
     return lax.ppermute(x, axis, [(i, i ^ distance) for i in range(lax.axis_size(axis))])
 
 
-EXCHANGES = (1, 2, 3)
+EXCHANGES = ((1, 0, 3, 2), (3, 2, 0, 1), (2, 3, 1, 0))
 
 
 def gather_lines(block):
     count = lax.axis_size("wall")
     if count == 4:
-        return [block] + [exchange(block, "wall", s) for s in EXCHANGES], (0,) + EXCHANGES
+        blocks, slots = [block], [(0,) * count]
+        for targets in EXCHANGES:
+            blocks.append(lax.ppermute(block, "wall", list(enumerate(targets))))
+            slots.append(tuple(w ^ targets.index(w) for w in range(count)))
+        return blocks, tuple(slots)
     stack = block[None]
     for step in range(count.bit_length() - 1):
         stack = jnp.concatenate([stack, exchange(stack, "wall", 1 << step)])
-    return [stack], (0,)
+    return [stack], ((0,) * count,)
+
+
+def slot_here(slots):
+    me = lax.axis_index("wall")
+    if len(set(slots)) == 1:
+        return slots[0]
+    return sum(jnp.where(me == w, slot, 0) for w, slot in enumerate(slots))
 
 
 VMEM = pl.BlockSpec(memory_space=pltpu.VMEM)
@@ -339,7 +370,8 @@
     deep = (count, BANDS, cols)
     flat = (count, BANDS // 2, cols)
     whole = (parts,) + tile
-    state_of = [deep, deep, whole, whole]
+    message = (parts + 1,) + tile
+    state_of = [deep, deep, message, message]
     held = []
     for received, slot in zip(blocks, ids):
         held = call(
@@ -347,14 +379,15 @@
             aliases={3 + j: j for j in range(len(held))},
         )
     scratch = [(2,) + deep, flat, flat, (count + 2 * rows, cols), whole]
-    heating, wall, outer, inner = call(first_kernel, [whole, (1, cols), whole, whole], scratch, *held)
-    inner = lax.ppermute(inner, "azim", [(i, i ^ 1) for i in range(ring)])
-    outer = lax.ppermute(outer, "azim", [(i, (i + 1) % ring if i % 2 else (i - 1) % ring) for i in range(ring)])
+    heating, wall, my_outer, my_inner = call(first_kernel, [whole, (1, cols), message, message], scratch, *held)
+    inner = lax.ppermute(my_inner, "azim", [(i, i ^ 1) for i in range(ring)])
+    outer = lax.ppermute(my_outer, "azim", [(i, (i + 1) % ring if i % 2 else (i - 1) % ring) for i in range(ring)])
+    middle, packed = call(
+        functools.partial(center_kernel, ids), [(parts, comps) + tile, whole], [], *blocks, heating,
+    )
     middle, edge = call(
-        functools.partial(advance_kernel, ids),
-        [(parts, comps) + tile, (comps,) + tile],
-        [(parts, comps) + tile, (HEAT_SLOT + 1,) + tile],
-        *blocks, heating, outer, inner,
+        border_kernel, [(parts, comps) + tile, (comps,) + tile], [message],
+        middle, packed, my_outer, my_inner, outer, inner, aliases={0: 0},
     )
     new_state, wall = call(
         last_kernel, [(comps,) + tile, (1, cols)], [deep, deep] + scratch,

time: 17.4 us -> 16.8 us (0.966)
  waiting for transfers between devices: 4.72 us -> 3.59 us
  Pallas kernels: 2.51 us -> 3 us
    ppermute x5, waiting for transfers between devices: 4.72 us -> 3.59 us  [the longest x3 2.6 us: gather_lines(): blocks.append(lax.ppermute(block, 'wall', list(enumerate(targets))))]
    pallas_call x7 -> x8, Pallas kernels: 2.51 us -> 3 us  [call(): pl.pallas_call(kernel, out_shape=[jax.ShapeDtypeStruct(shape, jnp.float32...]
  transfers between devices with their start and end apart: 5 -> 5, of which waited for: 3 -> 2; matrix products, arithmetic and copies ran while one was open for 3% -> 3% of each run, Pallas kernels for 2% -> 7%
where the time goes in v5:
time: 16.8 us; the launch traced here: 16.6 us
  starting transfers between devices  7.27 us (43%)
  waiting for transfers between devices  3.59 us (21%)
  Pallas kernels  3 us (18%)
  other arithmetic  1.19 us (7%)
  local copies, waits for them, and re-layouts  0.81 us (5%)
  between operations  0.72 us (4%)
    ppermute x3, starting transfers between devices, gather_lines(): blocks.append(lax.ppermute(block, 'wall', list(enumerate(targets))))  5.62 us
    pallas_call x8, Pallas kernels, call(): pl.pallas_call(kernel, out_shape=[jax.ShapeDtypeStruct(shape, jnp.float32...  3 us
    ppermute x3, waiting for transfers between devices, gather_lines(): blocks.append(lax.ppermute(block, 'wall', list(enumerate(targets))))  2.6 us
    ppermute x1, starting transfers between devices, local(): inner = lax.ppermute(my_inner, 'azim', [(i, i ^ 1) for i in range(ring)])  1.61 us
    ppermute x1, waiting for transfers between devices, local(): lax.ppermute(my_outer, 'azim', [(i, (i + 1) % ring if i % 2 else (i - 1)...  0.99 us
    concatenate x1, other arithmetic, local(): jnp.concatenate([state.reshape(comps, rows, cols), courant.reshape((1,) +...  0.83 us
    unnamed x8, local copies, waits for them, and re-layouts  0.66 us
  transfers between devices with their start and end apart: 5, of which 2 were waited for; matrix products, arithmetic and copies ran while one was open for 3% of the time, Pallas kernels for 7%

profile of v5, /device:TPU:0, one launch (start us, length us, event | category | flops | bytes accessed | tf_op | source)
XLA Modules:
  0.0 16.6 jit_solution(11248518824071729396)
XLA Ops:
  0.6 0.0 copy-start
  0.6 0.0 copy-start.1
  0.7 0.8 %pad_maximum_fusion.block_ref.refs_0_ = f32[13,8,128]{2,1,0:T(8,128)S(1)} fusion(f32[1,8,128]{2,1,0:T(8,128)} %param.7, f32[12,8,128]{2,1,0:T(8,128)} %bitcast.4), kind=kLoop, calls=%fused_computation.2 | loop fusion | flops 13312 | bytes 106496 | tf_op jit(solution)/shard_map/concatenate | solution.py:367
  1.5 4.0 %collective-permute-start.2 = (f32[13,8,128]{2,1,0:T(8,128)S(1)}, f32[13,8,128]{2,1,0:T(8,128)S(1)}, u32[]{:S(2)}, u32[]{:S(2)}) collective-permute-start(f32[13,8,128]{2,1,0:T(8,128)S(1)} %pad_maximum_fusion.block_ref.refs_0_), channel_id=1, source_target_pairs={{0,8},{4,12},{8,4},{12,0},{1,9},{5,13},{9,5},{13,1},{2,10},{6,14},... | collective-permute-start | bytes 159752 | tf_op jit(solution)/shard_map/ppermute | solution.py:330
  5.5 1.0 %collective-permute-start.1 = (f32[13,8,128]{2,1,0:T(8,128)S(1)}, f32[13,8,128]{2,1,0:T(8,128)S(1)}, u32[]{:S(2)}, u32[]{:S(2)}) collective-permute-start(f32[13,8,128]{2,1,0:T(8,128)S(1)} %pad_maximum_fusion.block_ref.refs_0_), channel_id=1, source_target_pairs={{0,12},{4,8},{8,0},{12,4},{1,13},{5,9},{9,1},{13,5},{2,14},{6,10},... | collective-permute-start | bytes 159752 | tf_op jit(solution)/shard_map/ppermute | solution.py:330
  6.5 0.5 %collective-permute-start = (f32[13,8,128]{2,1,0:T(8,128)S(1)}, f32[13,8,128]{2,1,0:T(8,128)S(1)}, u32[]{:S(2)}, u32[]{:S(2)}) collective-permute-start(f32[13,8,128]{2,1,0:T(8,128)S(1)} %pad_maximum_fusion.block_ref.refs_0_), channel_id=1, source_target_pairs={{0,4},{4,0},{8,12},{12,8},{1,5},{5,1},{9,13},{13,9},{2,6},{6,2},{1... | collective-permute-start | bytes 159752 | tf_op jit(solution)/shard_map/ppermute | solution.py:330
  7.1 0.0 copy-done
  7.1 0.0 copy-done.1
  7.1 0.2 %select_reduce_fusion = f32[11,16]{1,0:T(8,128)S(1)} fusion(f32[64]{0:T(128)S(1)} %copy-done.1, s32[11,16]{1,0:T(8,128)S(1)} %copy-done), kind=kLoop, calls=%fused_computation | loop fusion | flops 33616 | bytes 1664 | tf_op jit(solution)/shard_map/reduce_sum | solution.py:312
  7.3 0.0 copy-start.2
  7.3 0.0 copy-start.3
  7.3 0.6 %copy-done.2 = f32[64]{0:T(128)S(1)} copy-done((f32[64]{0:T(128)S(1)}, f32[64]{0:T(128)}, u32[]{:S(2)}) %copy-start.2) | copy-done | bytes 280
  7.9 0.0 copy-done.3
  8.0 0.2 %select_reduce_fusion.1 = f32[16]{0:T(128)S(1)} fusion(f32[64]{0:T(128)S(1)} %copy-done.2, s32[16]{0:T(128)S(1)} %copy-done.3), kind=kLoop, calls=%fused_computation.3 | loop fusion | flops 3056 | bytes 384 | tf_op jit(solution)/shard_map/reduce_sum | solution.py:313
  8.1 0.1 broadcast_in_dim.45.share_ref
  8.2 0.1 broadcast_in_dim.42.cross_ref
  8.3 0.3 %shard_map.77 = (f32[32,16,128]{2,1,0:T(8,128)S(1)}, f32[32,16,128]{2,1,0:T(8,128)S(1)}, f32[5,8,128]{2,1,0:T(8,128)S(1)}, f32[5,8,128]{2,1,0:T(8,128)S(1)}) custom-call(f32[13,8,128]{2,1,0:T(8,128)S(1)} %pad_maximum_fusion.block_ref.refs_0_, f32[11,16,128]{2,1,0:T(8,128)S(1)} %broadcast_in_dim.42.cross_ref, f32[16,128]{1,0:T(8,128)S(1)} %broadcast_in_dim.45.share_ref), custom_call_target="tpu_custom_call" | custom-call | tf_op jit(solution)/shard_map/pallas_call | solution.py:350
  8.6 2.6 %collective-permute-done.block_ref.refs_1_ = f32[13,8,128]{2,1,0:T(8,128)S(1)} collective-permute-done((f32[13,8,128]{2,1,0:T(8,128)S(1)}, f32[13,8,128]{2,1,0:T(8,128)S(1)}, u32[]{:S(2)}, u32[]{:S(2)}) %collective-permute-start) | collective-permute-done | bytes 53280 | tf_op jit(solution)/shard_map/ppermute | solution.py:330
  11.2 0.1 shard_map.78
  11.3 0.0 collective-permute-done.1.block_ref.refs_2_
  11.3 0.1 shard_map.79
  11.4 0.0 collective-permute-done.2.block_ref.refs_3_
  11.5 0.1 shard_map.80
  11.6 0.3 %shard_map.81 = (f32[4,8,128]{2,1,0:T(8,128)S(1)}, f32[1,128]{1,0:T(1,128)S(1)}, f32[5,8,128]{2,1,0:T(8,128)S(1)}, f32[5,8,128]{2,1,0:T(8,128)S(1)}) custom-call(f32[32,16,128]{2,1,0:T(8,128)S(1)} %get-tuple-element.40.step_ref, f32[32,16,128]{2,1,0:T(8,128)S(1)} %get-tuple-element.41.emit_ref, f32[5,8,128]{2,1,0:T(8,128)S(1)} %get-tuple-element.42.outer_in_ref, ...), custom_call_target="tpu_custom_call" | custom-call | tf_op jit(solution)/shard_map/pallas_call | solution.py:350
  11.9 0.0 collective-permute-start.3
  11.9 1.6 %collective-permute-start.4 = (f32[5,8,128]{2,1,0:T(8,128)S(1)}, f32[5,8,128]{2,1,0:T(8,128)S(1)}, u32[]{:S(2)}, u32[]{:S(2)}) collective-permute-start(f32[5,8,128]{2,1,0:T(8,128)S(1)} %get-tuple-element.48.my_inner_ref), channel_id=1, source_target_pairs={{0,1},{1,0},{2,3},{3,2},{4,5},{5,4},{6,7},{7,6},{8,9},{9,8},{10,11... | collective-permute-start | bytes 61448 | tf_op jit(solution)/shard_map/ppermute | solution.py:383
  13.5 0.7 %shard_map.82 = (f32[4,12,8,128]{3,2,1,0:T(8,128)S(1)}, f32[4,8,128]{2,1,0:T(8,128)S(1)}) custom-call(f32[13,8,128]{2,1,0:T(8,128)S(1)} %pad_maximum_fusion.block_ref.refs_0_, f32[13,8,128]{2,1,0:T(8,128)S(1)} %collective-permute-done.block_ref.refs_1_, f32[13,8,128]{2,1,0:T(8,128)S(1)} %collective-permute-done.1.block_ref.refs_2_, ...), custom_call_target="tpu_custom_call" | custom-call | tf_op jit(solution)/shard_map/pallas_call | solution.py:350
  14.2 1.0 %collective-permute-done.3.outer_ref = f32[5,8,128]{2,1,0:T(8,128)S(1)} collective-permute-done((f32[5,8,128]{2,1,0:T(8,128)S(1)}, f32[5,8,128]{2,1,0:T(8,128)S(1)}, u32[]{:S(2)}, u32[]{:S(2)}) %collective-permute-start.3) | collective-permute-done | bytes 20512 | tf_op jit(solution)/shard_map/ppermute | solution.py:384
  15.2 0.0 collective-permute-done.4.inner_ref
  15.2 0.2 %shard_map.83 = (f32[4,12,8,128]{3,2,1,0:T(8,128)S(1)}, f32[12,8,128]{2,1,0:T(8,128)S(1)}) custom-call(f32[4,12,8,128]{3,2,1,0:T(8,128)S(1)} %get-tuple-element.45.middle_in_ref, f32[4,8,128]{2,1,0:T(8,128)S(1)} %get-tuple-element.46.packed_ref, f32[5,8,128]{2,1,0:T(8,128)S(1)} %get-tuple-element.47.my_outer_ref, ...), custom_call_target="tpu_custom_call", output_to_operand_aliasing={{0}: (0, {})} | custom-call | tf_op jit(solution)/shard_map/pallas_call | solution.py:350
  15.4 1.1 %shard_map.84 = (f32[12,8,128]{2,1,0:T(8,128)}, f32[1,128]{1,0:T(1,128)}) custom-call(f32[13,8,128]{2,1,0:T(8,128)S(1)} %pad_maximum_fusion.block_ref.refs_0_, f32[4,12,8,128]{3,2,1,0:T(8,128)S(1)} %get-tuple-element.49.middle_ref, f32[12,8,128]{2,1,0:T(8,128)S(1)} %get-tuple-element.50.edge_ref, f32[1,128]{1,0:T(1,128)S(1)} %get-tuple-element.51.wall_in_ref, ...), custom_call_target="tpu_custom_call" | custom-call | tf_op jit(solution)/shard_map/pallas_call | solution.py:350
  (1 shorter events, 0.0 us)
Async XLA Ops:
  0.6 6.5 %copy-start = (s32[11,16]{1,0:T(8,128)S(1)}, s32[11,16]{1,0:T(8,128)}, u32[]{:S(2)}) copy-start(s32[11,16]{1,0:T(8,128)} %param.10) | copy-start | bytes 2116
  0.6 6.5 %copy-start.1 = (f32[64]{0:T(128)S(1)}, f32[64]{0:T(128)}, u32[]{:S(2)}) copy-start(f32[64]{0:T(128)} %param.8) | copy-start | bytes 772
  1.5 10.0 %collective-permute-start.2 = (f32[13,8,128]{2,1,0:T(8,128)S(1)}, f32[13,8,128]{2,1,0:T(8,128)S(1)}, u32[]{:S(2)}, u32[]{:S(2)}) collective-permute-start(f32[13,8,128]{2,1,0:T(8,128)S(1)} %pad_maximum_fusion.block_ref.refs_0_), channel_id=1, source_target_pairs={{0,8},{4,12},{8,4},{12,0},{1,9},{5,13},{9,5},{13,1},{2,10},{6,14},... | collective-permute-start | bytes 159752 | tf_op jit(solution)/shard_map/ppermute | solution.py:330
  5.5 5.8 %collective-permute-start.1 = (f32[13,8,128]{2,1,0:T(8,128)S(1)}, f32[13,8,128]{2,1,0:T(8,128)S(1)}, u32[]{:S(2)}, u32[]{:S(2)}) collective-permute-start(f32[13,8,128]{2,1,0:T(8,128)S(1)} %pad_maximum_fusion.block_ref.refs_0_), channel_id=1, source_target_pairs={{0,12},{4,8},{8,0},{12,4},{1,13},{5,9},{9,1},{13,5},{2,14},{6,10},... | collective-permute-start | bytes 159752 | tf_op jit(solution)/shard_map/ppermute | solution.py:330
  6.5 4.7 %collective-permute-start = (f32[13,8,128]{2,1,0:T(8,128)S(1)}, f32[13,8,128]{2,1,0:T(8,128)S(1)}, u32[]{:S(2)}, u32[]{:S(2)}) collective-permute-start(f32[13,8,128]{2,1,0:T(8,128)S(1)} %pad_maximum_fusion.block_ref.refs_0_), channel_id=1, source_target_pairs={{0,4},{4,0},{8,12},{12,8},{1,5},{5,1},{9,13},{13,9},{2,6},{6,2},{1... | collective-permute-start | bytes 159752 | tf_op jit(solution)/shard_map/ppermute | solution.py:330
  7.3 0.7 %copy-start.2 = (f32[64]{0:T(128)S(1)}, f32[64]{0:T(128)}, u32[]{:S(2)}) copy-start(f32[64]{0:T(128)} %param.9) | copy-start | bytes 772
  7.3 0.7 %copy-start.3 = (s32[16]{0:T(128)S(1)}, s32[16]{0:T(128)}, u32[]{:S(2)}) copy-start(s32[16]{0:T(128)} %param.11) | copy-start | bytes 196
  11.9 3.3 %collective-permute-start.3 = (f32[5,8,128]{2,1,0:T(8,128)S(1)}, f32[5,8,128]{2,1,0:T(8,128)S(1)}, u32[]{:S(2)}, u32[]{:S(2)}) collective-permute-start(f32[5,8,128]{2,1,0:T(8,128)S(1)} %get-tuple-element.47.my_outer_ref), channel_id=1, source_target_pairs={{0,3},{1,2},{2,1},{3,0},{4,7},{5,6},{6,5},{7,4},{8,11},{9,10},{10,... | collective-permute-start | bytes 61448 | tf_op jit(solution)/shard_map/ppermute | solution.py:384
  11.9 3.3 %collective-permute-start.4 = (f32[5,8,128]{2,1,0:T(8,128)S(1)}, f32[5,8,128]{2,1,0:T(8,128)S(1)}, u32[]{:S(2)}, u32[]{:S(2)}) collective-permute-start(f32[5,8,128]{2,1,0:T(8,128)S(1)} %get-tuple-element.48.my_inner_ref), channel_id=1, source_target_pairs={{0,1},{1,0},{2,3},{3,2},{4,5},{5,4},{6,7},{7,6},{8,9},{9,8},{10,11... | collective-permute-start | bytes 61448 | tf_op jit(solution)/shard_map/ppermute | solution.py:383

commit v6 on v5

--- a/solution.py
+++ b/solution.py
@@ -319,15 +319,22 @@
     return lax.ppermute(x, axis, [(i, i ^ distance) for i in range(lax.axis_size(axis))])
 
 
-EXCHANGES = ((1, 0, 3, 2), (3, 2, 0, 1), (2, 3, 1, 0))
+EXCHANGES = ((1, 2, 3, 0), (2, 3, 0, 1), (3, 0, 1, 2))
+
+
+def copy_kernel(source_ref, *refs):
+    for ref in refs:
+        ref[...] = source_ref[...]
 
 
 def gather_lines(block):
     count = lax.axis_size("wall")
     if count == 4:
         blocks, slots = [block], [(0,) * count]
+        copies = list(call(copy_kernel, [block.shape] * 2, [], block))
         for targets in EXCHANGES:
-            blocks.append(lax.ppermute(block, "wall", list(enumerate(targets))))
+            sent = copies.pop() if copies and targets != EXCHANGES[0] else block
+            blocks.append(lax.ppermute(sent, "wall", list(enumerate(targets))))
             slots.append(tuple(w ^ targets.index(w) for w in range(count)))
         return blocks, tuple(slots)
     stack = block[None]

time: 16.8 us -> 16.6 us (0.988)
  waiting for transfers between devices: 3.59 us -> 1.92 us
  starting transfers between devices: 7.27 us -> 8.78 us
    ppermute x3, waiting for transfers between devices: 2.6 us -> 1.13 us  [gather_lines(): blocks.append(lax.ppermute(sent, 'wall', list(enumerate(targets))))]
    ppermute x3, starting transfers between devices: 5.62 us -> 7.03 us  [gather_lines(): blocks.append(lax.ppermute(sent, 'wall', list(enumerate(targets))))]
    ppermute x1, waiting for transfers between devices: 0.99 us -> 0.79 us  [local(): lax.ppermute(my_outer, 'azim', [(i, (i + 1) % ring if i % 2 else (i - 1)...]
    pallas_call x8 -> x9, Pallas kernels: 3 us -> 3.01 us  [call(): pl.pallas_call(kernel, out_shape=[jax.ShapeDtypeStruct(shape, jnp.float32...]
  transfers between devices with their start and end apart: 5 -> 5, of which waited for: 2 -> 3; matrix products, arithmetic and copies ran while one was open for 3% -> 3% of each run, Pallas kernels for 7% -> 8%
where the time goes in v6:
time: 16.6 us; the launch traced here: 16.4 us
  starting transfers between devices  8.78 us (53%)
  Pallas kernels  3.01 us (18%)
  waiting for transfers between devices  1.92 us (12%)
  other arithmetic  1.18 us (7%)
  local copies, waits for them, and re-layouts  0.81 us (5%)
  between operations  0.71 us (4%)
    ppermute x3, starting transfers between devices, gather_lines(): blocks.append(lax.ppermute(sent, 'wall', list(enumerate(targets))))  7.03 us
    pallas_call x9, Pallas kernels, call(): pl.pallas_call(kernel, out_shape=[jax.ShapeDtypeStruct(shape, jnp.float32...  3.01 us
    ppermute x1, starting transfers between devices, local(): inner = lax.ppermute(my_inner, 'azim', [(i, i ^ 1) for i in range(ring)])  1.75 us
    ppermute x3, waiting for transfers between devices, gather_lines(): blocks.append(lax.ppermute(sent, 'wall', list(enumerate(targets))))  1.13 us
    concatenate x1, other arithmetic, local(): jnp.concatenate([state.reshape(comps, rows, cols), courant.reshape((1,) +...  0.82 us
    ppermute x1, waiting for transfers between devices, local(): lax.ppermute(my_outer, 'azim', [(i, (i + 1) % ring if i % 2 else (i - 1)...  0.79 us
    unnamed x8, local copies, waits for them, and re-layouts  0.66 us
  transfers between devices with their start and end apart: 5, of which 3 were waited for; matrix products, arithmetic and copies ran while one was open for 3% of the time, Pallas kernels for 8%

profile of v6, /device:TPU:0, one launch (start us, length us, event | category | flops | bytes accessed | tf_op | source)
XLA Modules:
  0.0 16.4 jit_solution(7780164903623323794)
XLA Ops:
  0.6 0.8 %pad_maximum_fusion.source_ref.block_ref.refs_0_ = f32[13,8,128]{2,1,0:T(8,128)S(1)} fusion(f32[1,8,128]{2,1,0:T(8,128)} %param.7, f32[12,8,128]{2,1,0:T(8,128)} %bitcast.4), kind=kLoop, calls=%fused_computation.2 | loop fusion | flops 13312 | bytes 106496 | tf_op jit(solution)/shard_map/concatenate | solution.py:374
  1.4 3.0 %collective-permute-start = (f32[13,8,128]{2,1,0:T(8,128)S(1)}, f32[13,8,128]{2,1,0:T(8,128)S(1)}, u32[]{:S(2)}, u32[]{:S(2)}) collective-permute-start(f32[13,8,128]{2,1,0:T(8,128)S(1)} %pad_maximum_fusion.source_ref.block_ref.refs_0_), channel_id=1, source_target_pairs={{0,4},{4,8},{8,12},{12,0},{1,5},{5,9},{9,13},{13,1},{2,6},{6,10},{... | collective-permute-start | bytes 159752 | tf_op jit(solution)/shard_map/ppermute | solution.py:337
  4.5 0.0 copy-start
  4.5 0.0 copy-start.1
  4.5 2.7 %collective-permute-start.1 = (f32[13,8,128]{2,1,0:T(8,128)S(1)}, f32[13,8,128]{2,1,0:T(8,128)S(1)}, u32[]{:S(2)}, u32[]{:S(2)}) collective-permute-start(f32[13,8,128]{2,1,0:T(8,128)S(1)} %get-tuple-element.30), channel_id=1, source_target_pairs={{0,8},{4,12},{8,0},{12,4},{1,9},{5,13},{9,1},{13,5},{2,10},{6,14},... | collective-permute-start | bytes 159752 | tf_op jit(solution)/shard_map/ppermute | solution.py:337
  7.2 1.3 %collective-permute-start.2 = (f32[13,8,128]{2,1,0:T(8,128)S(1)}, f32[13,8,128]{2,1,0:T(8,128)S(1)}, u32[]{:S(2)}, u32[]{:S(2)}) collective-permute-start(f32[13,8,128]{2,1,0:T(8,128)S(1)} %get-tuple-element.31), channel_id=1, source_target_pairs={{0,12},{4,0},{8,4},{12,8},{1,13},{5,1},{9,5},{13,9},{2,14},{6,2},{... | collective-permute-start | bytes 159752 | tf_op jit(solution)/shard_map/ppermute | solution.py:337
  8.5 0.0 copy-done
  8.5 0.0 copy-done.1
  8.5 0.2 %select_reduce_fusion = f32[11,16]{1,0:T(8,128)S(1)} fusion(f32[64]{0:T(128)S(1)} %copy-done.1, s32[11,16]{1,0:T(8,128)S(1)} %copy-done), kind=kLoop, calls=%fused_computation | loop fusion | flops 33616 | bytes 1664 | tf_op jit(solution)/shard_map/reduce_sum | solution.py:312
  8.7 0.0 copy-start.2
  8.7 0.0 copy-start.3
  8.7 0.6 %copy-done.2 = f32[64]{0:T(128)S(1)} copy-done((f32[64]{0:T(128)S(1)}, f32[64]{0:T(128)}, u32[]{:S(2)}) %copy-start.2) | copy-done | bytes 280
  9.3 0.0 copy-done.3
  9.4 0.2 %select_reduce_fusion.1 = f32[16]{0:T(128)S(1)} fusion(f32[64]{0:T(128)S(1)} %copy-done.2, s32[16]{0:T(128)S(1)} %copy-done.3), kind=kLoop, calls=%fused_computation.3 | loop fusion | flops 3056 | bytes 384 | tf_op jit(solution)/shard_map/reduce_sum | solution.py:313
  9.5 0.1 broadcast_in_dim.45.share_ref
  9.6 0.1 broadcast_in_dim.42.cross_ref
  9.7 0.3 %shard_map.78 = (f32[32,16,128]{2,1,0:T(8,128)S(1)}, f32[32,16,128]{2,1,0:T(8,128)S(1)}, f32[5,8,128]{2,1,0:T(8,128)S(1)}, f32[5,8,128]{2,1,0:T(8,128)S(1)}) custom-call(f32[13,8,128]{2,1,0:T(8,128)S(1)} %pad_maximum_fusion.source_ref.block_ref.refs_0_, f32[11,16,128]{2,1,0:T(8,128)S(1)} %broadcast_in_dim.42.cross_ref, f32[16,128]{1,0:T(8,128)S(1)} %broadcast_in_dim.45.share_ref), custom_call_target="tpu_custom_call" | custom-call | tf_op jit(solution)/shard_map/pallas_call | solution.py:357
  10.1 0.0 collective-permute-done.block_ref.refs_1_
  10.1 0.1 shard_map.79
  10.2 0.8 %collective-permute-done.1.block_ref.refs_2_ = f32[13,8,128]{2,1,0:T(8,128)S(1)} collective-permute-done((f32[13,8,128]{2,1,0:T(8,128)S(1)}, f32[13,8,128]{2,1,0:T(8,128)S(1)}, u32[]{:S(2)}, u32[]{:S(2)}) %collective-permute-start.1) | collective-permute-done | bytes 53280 | tf_op jit(solution)/shard_map/ppermute | solution.py:337
  10.9 0.1 shard_map.80
  11.0 0.4 %collective-permute-done.2.block_ref.refs_3_ = f32[13,8,128]{2,1,0:T(8,128)S(1)} collective-permute-done((f32[13,8,128]{2,1,0:T(8,128)S(1)}, f32[13,8,128]{2,1,0:T(8,128)S(1)}, u32[]{:S(2)}, u32[]{:S(2)}) %collective-permute-start.2) | collective-permute-done | bytes 53280 | tf_op jit(solution)/shard_map/ppermute | solution.py:337
  11.4 0.1 shard_map.81
  11.5 0.3 %shard_map.82 = (f32[4,8,128]{2,1,0:T(8,128)S(1)}, f32[1,128]{1,0:T(1,128)S(1)}, f32[5,8,128]{2,1,0:T(8,128)S(1)}, f32[5,8,128]{2,1,0:T(8,128)S(1)}) custom-call(f32[32,16,128]{2,1,0:T(8,128)S(1)} %get-tuple-element.44.step_ref, f32[32,16,128]{2,1,0:T(8,128)S(1)} %get-tuple-element.45.emit_ref, f32[5,8,128]{2,1,0:T(8,128)S(1)} %get-tuple-element.46.outer_in_ref, ...), custom_call_target="tpu_custom_call" | custom-call | tf_op jit(solution)/shard_map/pallas_call | solution.py:357
  11.8 0.0 collective-permute-start.3
  11.8 1.7 %collective-permute-start.4 = (f32[5,8,128]{2,1,0:T(8,128)S(1)}, f32[5,8,128]{2,1,0:T(8,128)S(1)}, u32[]{:S(2)}, u32[]{:S(2)}) collective-permute-start(f32[5,8,128]{2,1,0:T(8,128)S(1)} %get-tuple-element.52.my_inner_ref), channel_id=1, source_target_pairs={{0,1},{1,0},{2,3},{3,2},{4,5},{5,4},{6,7},{7,6},{8,9},{9,8},{10,11... | collective-permute-start | bytes 61448 | tf_op jit(solution)/shard_map/ppermute | solution.py:390
  13.5 0.7 %shard_map.83 = (f32[4,12,8,128]{3,2,1,0:T(8,128)S(1)}, f32[4,8,128]{2,1,0:T(8,128)S(1)}) custom-call(f32[13,8,128]{2,1,0:T(8,128)S(1)} %pad_maximum_fusion.source_ref.block_ref.refs_0_, f32[13,8,128]{2,1,0:T(8,128)S(1)} %collective-permute-done.block_ref.refs_1_, f32[13,8,128]{2,1,0:T(8,128)S(1)} %collective-permute-done.1.block_ref.refs_2_, ...), custom_call_target="tpu_custom_call" | custom-call | tf_op jit(solution)/shard_map/pallas_call | solution.py:357
  14.2 0.8 %collective-permute-done.3.outer_ref = f32[5,8,128]{2,1,0:T(8,128)S(1)} collective-permute-done((f32[5,8,128]{2,1,0:T(8,128)S(1)}, f32[5,8,128]{2,1,0:T(8,128)S(1)}, u32[]{:S(2)}, u32[]{:S(2)}) %collective-permute-start.3) | collective-permute-done | bytes 20512 | tf_op jit(solution)/shard_map/ppermute | solution.py:391
  15.0 0.0 collective-permute-done.4.inner_ref
  15.0 0.2 %shard_map.84 = (f32[4,12,8,128]{3,2,1,0:T(8,128)S(1)}, f32[12,8,128]{2,1,0:T(8,128)S(1)}) custom-call(f32[4,12,8,128]{3,2,1,0:T(8,128)S(1)} %get-tuple-element.49.middle_in_ref, f32[4,8,128]{2,1,0:T(8,128)S(1)} %get-tuple-element.50.packed_ref, f32[5,8,128]{2,1,0:T(8,128)S(1)} %get-tuple-element.51.my_outer_ref, ...), custom_call_target="tpu_custom_call", output_to_operand_aliasing={{0}: (0, {})} | custom-call | tf_op jit(solution)/shard_map/pallas_call | solution.py:357
  15.3 1.1 %shard_map.85 = (f32[12,8,128]{2,1,0:T(8,128)}, f32[1,128]{1,0:T(1,128)}) custom-call(f32[13,8,128]{2,1,0:T(8,128)S(1)} %pad_maximum_fusion.source_ref.block_ref.refs_0_, f32[4,12,8,128]{3,2,1,0:T(8,128)S(1)} %get-tuple-element.53.middle_ref, f32[12,8,128]{2,1,0:T(8,128)S(1)} %get-tuple-element.54.edge_ref, f32[1,128]{1,0:T(1,128)S(1)} %get-tuple-element.55.wall_in_ref, ...), custom_call_target="tpu_custom_call" | custom-call | tf_op jit(solution)/shard_map/pallas_call | solution.py:357
  (2 shorter events, 0.0 us)
Async XLA Ops:
  1.4 8.6 %collective-permute-start = (f32[13,8,128]{2,1,0:T(8,128)S(1)}, f32[13,8,128]{2,1,0:T(8,128)S(1)}, u32[]{:S(2)}, u32[]{:S(2)}) collective-permute-start(f32[13,8,128]{2,1,0:T(8,128)S(1)} %pad_maximum_fusion.source_ref.block_ref.refs_0_), channel_id=1, source_target_pairs={{0,4},{4,8},{8,12},{12,0},{1,5},{5,9},{9,13},{13,1},{2,6},{6,10},{... | collective-permute-start | bytes 159752 | tf_op jit(solution)/shard_map/ppermute | solution.py:337
  4.5 4.0 %copy-start = (s32[11,16]{1,0:T(8,128)S(1)}, s32[11,16]{1,0:T(8,128)}, u32[]{:S(2)}) copy-start(s32[11,16]{1,0:T(8,128)} %param.10) | copy-start | bytes 2116
  4.5 4.0 %copy-start.1 = (f32[64]{0:T(128)S(1)}, f32[64]{0:T(128)}, u32[]{:S(2)}) copy-start(f32[64]{0:T(128)} %param.8) | copy-start | bytes 772
  4.5 6.4 %collective-permute-start.1 = (f32[13,8,128]{2,1,0:T(8,128)S(1)}, f32[13,8,128]{2,1,0:T(8,128)S(1)}, u32[]{:S(2)}, u32[]{:S(2)}) collective-permute-start(f32[13,8,128]{2,1,0:T(8,128)S(1)} %get-tuple-element.30), channel_id=1, source_target_pairs={{0,8},{4,12},{8,0},{12,4},{1,9},{5,13},{9,1},{13,5},{2,10},{6,14},... | collective-permute-start | bytes 159752 | tf_op jit(solution)/shard_map/ppermute | solution.py:337
  7.2 4.2 %collective-permute-start.2 = (f32[13,8,128]{2,1,0:T(8,128)S(1)}, f32[13,8,128]{2,1,0:T(8,128)S(1)}, u32[]{:S(2)}, u32[]{:S(2)}) collective-permute-start(f32[13,8,128]{2,1,0:T(8,128)S(1)} %get-tuple-element.31), channel_id=1, source_target_pairs={{0,12},{4,0},{8,4},{12,8},{1,13},{5,1},{9,5},{13,9},{2,14},{6,2},{... | collective-permute-start | bytes 159752 | tf_op jit(solution)/shard_map/ppermute | solution.py:337
  8.7 0.7 %copy-start.2 = (f32[64]{0:T(128)S(1)}, f32[64]{0:T(128)}, u32[]{:S(2)}) copy-start(f32[64]{0:T(128)} %param.9) | copy-start | bytes 772
  8.7 0.7 %copy-start.3 = (s32[16]{0:T(128)S(1)}, s32[16]{0:T(128)}, u32[]{:S(2)}) copy-start(s32[16]{0:T(128)} %param.11) | copy-start | bytes 196
  11.8 3.2 %collective-permute-start.3 = (f32[5,8,128]{2,1,0:T(8,128)S(1)}, f32[5,8,128]{2,1,0:T(8,128)S(1)}, u32[]{:S(2)}, u32[]{:S(2)}) collective-permute-start(f32[5,8,128]{2,1,0:T(8,128)S(1)} %get-tuple-element.51.my_outer_ref), channel_id=1, source_target_pairs={{0,3},{1,2},{2,1},{3,0},{4,7},{5,6},{6,5},{7,4},{8,11},{9,10},{10,... | collective-permute-start | bytes 61448 | tf_op jit(solution)/shard_map/ppermute | solution.py:391
  11.8 3.2 %collective-permute-start.4 = (f32[5,8,128]{2,1,0:T(8,128)S(1)}, f32[5,8,128]{2,1,0:T(8,128)S(1)}, u32[]{:S(2)}, u32[]{:S(2)}) collective-permute-start(f32[5,8,128]{2,1,0:T(8,128)S(1)} %get-tuple-element.52.my_inner_ref), channel_id=1, source_target_pairs={{0,1},{1,0},{2,3},{3,2},{4,5},{5,4},{6,7},{7,6},{8,9},{9,8},{10,11... | collective-permute-start | bytes 61448 | tf_op jit(solution)/shard_map/ppermute | solution.py:390

commit v7 on v6

--- a/solution.py
+++ b/solution.py
@@ -16,9 +16,10 @@
 BANDS = 16
 EDGE = 6
 COURANT = 12
+PIECES = 3
 TILES = 13
 PACKED = EDGE * COMPS
-HEAT_AT = 96
+HEAT_AT = PACKED + 8 * EDGE
 OFFSETS = (1, -1, 2, -2, 3, -3)
 
 
@@ -31,10 +32,10 @@
 
 
 def pack_kernel(state_ref, courant_ref, block_ref, sems):
-    copies = [
-        pltpu.make_async_copy(state_ref, block_ref.at[pl.ds(0, COMPS)], sems.at[0]),
-        pltpu.make_async_copy(courant_ref, block_ref.at[COURANT], sems.at[1]),
-    ]
+    copies = [pltpu.make_async_copy(courant_ref, block_ref.at[COURANT], sems.at[PIECES])]
+    for i in range(PIECES):
+        piece = pl.ds(i * (COMPS // PIECES), COMPS // PIECES)
+        copies.append(pltpu.make_async_copy(state_ref.at[piece], block_ref.at[piece], sems.at[i]))
     for copy in copies:
         copy.start()
     for copy in copies:
@@ -52,9 +53,9 @@
     return last, first
 
 
-def spread(value, lane):
-    group = jnp.where(lane < EDGE, roll(value, EDGE // 2), 0.0)
-    for width in (1, 2, 4, 8):
+def spread(value, lane, start, widths):
+    group = jnp.where((lane >= start) & (lane < start + EDGE), roll(value, EDGE // 2 + start), 0.0)
+    for width in widths:
         group = group + roll(group, EDGE * width)
     return group
 
@@ -67,35 +68,40 @@
     return lax.fori_loop(0, count, body, carry)
 
 
-def absorb(block, base, rows, cross_ref, share_ref, step_ref, emit_ref):
+def decay(gap, decay_ref, at):
+    for i, rate in enumerate(KERNEL_RATES):
+        decay_ref[i, at] = jnp.exp2(gap * (-0.5 * LOG2E * rate))
+
+
+def absorb(block, base, rows, cross_ref, share_ref, step_ref, emit_ref, decay_ref):
     hot = block[0]
     hot = hot * hot
     hot = hot * hot
+    before = None
     for r in range(rows):
         step = None
         for k in range(SPECIES):
             term = cross_ref[k] * block[1 + k, pl.ds(r, 1), :]
             step = term if step is None else step + term
-        step_ref[base + r] = step
+        if r in (0, rows - 1):
+            step_ref[base // rows, min(r, 1)] = step
         emit_ref[base + r] = share_ref[...] * step * hot[r : r + 1]
+        if r:
+            decay(before + step, decay_ref, base + r)
+        before = step
 
 
 def radiate(rows, step_ref, emit_ref, decay_ref, up_ref, down_ref, net_ref, heat_ref):
-    count = step_ref.shape[0]
+    count = emit_ref.shape[0]
     parts = count // rows
-    cols = step_ref.shape[-1]
+    cols = emit_ref.shape[-1]
+
+    zero = jnp.zeros((BANDS, cols), jnp.float32)
 
     def attenuate(part, before):
-        for r in range(rows):
-            at = part * rows + r
-            step = step_ref[at]
-            gap = before + step
-            for i, rate in enumerate(KERNEL_RATES):
-                decay_ref[i, at] = jnp.exp2(gap * (-0.5 * LOG2E * rate))
-            before = step
-        return before
-
-    zero = jnp.zeros((BANDS, cols), jnp.float32)
+        decay(before + step_ref[part, 0], decay_ref, part * rows)
+        return step_ref[part, 1]
+
     loop(parts, attenuate, zero)
 
     ratio = KERNEL_WEIGHTS[1] / KERNEL_WEIGHTS[0]
@@ -140,14 +146,14 @@
 
 
 def arrive_kernel(slots, block_ref, cross_ref, share_ref, *refs):
-    step_ref, emit_ref, outer_ref, inner_ref = refs[-4:]
+    step_ref, emit_ref, decay_ref, outer_ref, inner_ref = refs[-5:]
     rows, cols = block_ref.shape[-2:]
     lane = lanes((rows, cols))
     me = lax.axis_index("wall")
     odd = lax.rem(lax.axis_index("azim"), 2) == 1
 
     def take(block, slot):
-        absorb(block, (me ^ slot) * rows, rows, cross_ref, share_ref, step_ref, emit_ref)
+        absorb(block, (me ^ slot) * rows, rows, cross_ref, share_ref, step_ref, emit_ref, decay_ref)
         last, first = edge_tiles(block, lane)
         outer_ref[slot] = jnp.where(odd, last, first)
         inner_ref[slot] = jnp.where(odd, first, last)
@@ -163,25 +169,26 @@
         loop(block_ref.shape[0], body, 0)
     if slots[0] == 0:
         own = block_ref if len(block_ref.shape) == 3 else block_ref.at[0]
-        edges = spread(own[COURANT], lane)
-        outer_ref[outer_ref.shape[0] - 1] = edges
-        inner_ref[outer_ref.shape[0] - 1] = edges
-
-
-def first_kernel(step_ref, emit_ref, outer_in_ref, inner_in_ref, heating_ref, wall_ref, outer_ref, inner_ref, *scratch):
+        edges = spread(own[COURANT], lane, PACKED, (1, 2, 4))
+        for ref in (outer_ref, inner_ref):
+            ref[0] = jnp.where(lane < PACKED, ref[0], edges)
+
+
+def first_kernel(step_ref, emit_ref, decay_ref, outer_in_ref, inner_in_ref, heating_ref, wall_ref, outer_ref, inner_ref, *scratch):
     heat_ref = scratch[-1]
     parts, rows, cols = heating_ref.shape
     me = lax.axis_index("wall")
-    wall_ref[...] = radiate(rows, step_ref, emit_ref, *scratch)
+    wall_ref[...] = radiate(rows, step_ref, emit_ref, decay_ref, *scratch)
     lane = lanes((rows, cols))
     for s in range(parts):
         heating_ref[s] = heat_ref[me ^ s]
+    for s in range(1, parts):
         outer_ref[s] = outer_in_ref[s]
         inner_ref[s] = inner_in_ref[s]
     here = (lane >= HEAT_AT) & (lane < HEAT_AT + EDGE)
-    edges = jnp.where(here, roll(heat_ref[me], EDGE // 2 + HEAT_AT), outer_in_ref[parts])
-    outer_ref[parts] = edges
-    inner_ref[parts] = edges
+    edges = roll(heat_ref[me], EDGE // 2 + HEAT_AT)
+    outer_ref[0] = jnp.where(here, edges, outer_in_ref[0])
+    inner_ref[0] = jnp.where(here, edges, inner_in_ref[0])
 
 
 def coefficients(courant):
@@ -209,7 +216,7 @@
 
     def advance(block, s):
         factors = coefficients(block[COURANT])
-        packed_ref[s] = spread(block[COURANT], lane)
+        packed_ref[s] = spread(block[COURANT], lane, 0, (1, 2, 4, 8))
         for k in range(COMPS):
             moved = stencil(block[k], None, factors, lane, cols)
             if k == 0:
@@ -259,15 +266,16 @@
     loop(parts, differ, 0)
 
     left, right, last, first = sides(0)
-    outside = jnp.where(at < three, jnp.where(odd, inner_ref[parts], outer_ref[parts]), jnp.where(odd, outer_ref[parts], inner_ref[parts]))
-    factors = dict(zip(OFFSETS, coefficients(outside)))
+    outside = jnp.where(at < three, left, right)
+    courant = jnp.where(lane < 8 * EDGE, roll(outside, -PACKED), roll(outside, 8 * EDGE - PACKED))
+    factors = dict(zip(OFFSETS, coefficients(courant)))
     factors[0] = 0.6
     edge = jnp.where(lane < EDGE, COUPLING * roll(outside, -HEAT_AT), 0.0)
     for offset in range(-three, three + 1):
         behind = roll(jnp.where(at <= EDGE - 1 + offset, left, last), -(three + offset))
         ahead = roll(jnp.where(at < offset, first, right), three - offset)
         edge = edge + factors[offset] * jnp.where(at <= three - 1 - offset, behind, ahead)
-    change_ref[parts] = edge
+    edge_change = edge
 
     border = (lane < three) | (lane >= cols - three)
 
@@ -278,7 +286,7 @@
         return carry
 
     loop(parts, mend, 0)
-    edge = change_ref[parts]
+    edge = edge_change
     for k in range(COMPS):
         edge_ref[k] = roll(edge, -(EDGE * k + three))
 
@@ -289,10 +297,10 @@
     rows, cols = out_ref.shape[1:]
     lane = lanes((rows, cols))
     me = lax.axis_index("wall")
-    step_ref, emit_ref = scratch[:2]
+    step_ref, emit_ref, decay_ref = scratch[:3]
 
     def take(slot, carry):
-        absorb(middle_ref.at[slot], (me ^ slot) * rows, rows, cross_ref, share_ref, step_ref, emit_ref)
+        absorb(middle_ref.at[slot], (me ^ slot) * rows, rows, cross_ref, share_ref, step_ref, emit_ref, decay_ref)
         return carry
 
     loop(middle_ref.shape[0], take, 0)
@@ -365,27 +373,47 @@
     )(*args)
 
 
+def join_kernel(state_ref, courant_ref, block_ref, sems):
+    copies = [pltpu.make_async_copy(courant_ref, block_ref.at[COURANT], sems.at[PIECES])]
+    for i in range(PIECES):
+        piece = pl.ds(i * (COMPS // PIECES), COMPS // PIECES)
+        copies.append(pltpu.make_async_copy(state_ref.at[piece], block_ref.at[piece], sems.at[i]))
+    for copy in copies:
+        copy.start()
+    for copy in copies:
+        copy.wait()
+
+
 def local(state, courant, cross_sections, band_fractions, absorb_index, band_index):
     comps, stations, rows, cols = state.shape
     parts = lax.axis_size("wall")
     count = parts * rows
     ring = lax.axis_size("azim")
     tile = (rows, cols)
-    block = jnp.concatenate([state.reshape(comps, rows, cols), courant.reshape((1,) + tile)])
+    block = pl.pallas_call(
+        join_kernel,
+        out_shape=pltpu.VMEM((TILES,) + tile, jnp.float32),
+        in_specs=[pl.BlockSpec(memory_space=pl.ANY)] * 2,
+        out_specs=VMEM,
+        scratch_shapes=[pltpu.SemaphoreType.DMA((PIECES + 1,))],
+        compiler_params=pltpu.CompilerParams(vmem_limit_bytes=60 * 1024 * 1024),
+    )(state.reshape(comps, rows, cols), courant.reshape(tile))
     cross, share = band_tables(absorb_index, band_index, cross_sections, band_fractions, 1.0 / count, cols)
     blocks, ids = gather_lines(block)
     deep = (count, BANDS, cols)
     flat = (count, BANDS // 2, cols)
     whole = (parts,) + tile
-    message = (parts + 1,) + tile
-    state_of = [deep, deep, message, message]
+    message = (parts,) + tile
+    ends = (parts, 2, BANDS, cols)
+    both = (2,) + deep
+    state_of = [ends, deep, both, message, message]
     held = []
     for received, slot in zip(blocks, ids):
         held = call(
             functools.partial(arrive_kernel, slot), state_of, [], received, cross, share, *held,
             aliases={3 + j: j for j in range(len(held))},
         )
-    scratch = [(2,) + deep, flat, flat, (count + 2 * rows, cols), whole]
+    scratch = [flat, flat, (count + 2 * rows, cols), whole]
     heating, wall, my_outer, my_inner = call(first_kernel, [whole, (1, cols), message, message], scratch, *held)
     inner = lax.ppermute(my_inner, "azim", [(i, i ^ 1) for i in range(ring)])
     outer = lax.ppermute(my_outer, "azim", [(i, (i + 1) % ring if i % 2 else (i - 1) % ring) for i in range(ring)])
@@ -397,7 +425,7 @@
         middle, packed, my_outer, my_inner, outer, inner, aliases={0: 0},
     )
     new_state, wall = call(
-        last_kernel, [(comps,) + tile, (1, cols)], [deep, deep] + scratch,
+        last_kernel, [(comps,) + tile, (1, cols)], [ends, deep, both] + scratch,
         blocks[0], middle, edge, wall, cross, share,
     )
     return new_state.reshape(state.shape), wall

time: 16.6 us -> 16.6 us (level)
  other arithmetic: 1.18 us -> 0.36 us
  Pallas kernels: 3.01 us -> 3.66 us
    concatenate x1 -> x0, other arithmetic: 0.82 us -> none  [local(): jnp.concatenate([state.reshape(comps, rows, cols), courant.reshape((1,) +...]
    pallas_call x0 -> x1, Pallas kernels: none -> 0.8 us  [local(): pl.pallas_call(join_kernel, out_shape=pltpu.VMEM((TILES,) + tile, jnp.flo...]
  transfers between devices with their start and end apart: 5 -> 5, of which waited for: 3 -> 3; matrix products, arithmetic and copies ran while one was open for 3% -> 3% of each run, Pallas kernels for 8% -> 7%
where the time goes in v7:
time: 16.6 us; the launch traced here: 16.3 us
  starting transfers between devices  8.83 us (53%)
  Pallas kernels  3.66 us (22%)
  waiting for transfers between devices  1.93 us (12%)
  local copies, waits for them, and re-layouts  0.81 us (5%)
  between operations  0.72 us (4%)
  other arithmetic  0.36 us (2%)
    ppermute x3, starting transfers between devices, gather_lines(): blocks.append(lax.ppermute(sent, 'wall', list(enumerate(targets))))  7.08 us
    pallas_call x9, Pallas kernels, call(): pl.pallas_call(kernel, out_shape=[jax.ShapeDtypeStruct(shape, jnp.float32...  2.86 us
    ppermute x1, starting transfers between devices, local(): inner = lax.ppermute(my_inner, 'azim', [(i, i ^ 1) for i in range(ring)])  1.74 us
    ppermute x3, waiting for transfers between devices, gather_lines(): blocks.append(lax.ppermute(sent, 'wall', list(enumerate(targets))))  1.21 us
    pallas_call x1, Pallas kernels, local(): pl.pallas_call(join_kernel, out_shape=pltpu.VMEM((TILES,) + tile, jnp.flo...  0.8 us
    ppermute x1, waiting for transfers between devices, local(): lax.ppermute(my_outer, 'azim', [(i, (i + 1) % ring if i % 2 else (i - 1)...  0.72 us
    unnamed x8, local copies, waits for them, and re-layouts  0.66 us
  transfers between devices with their start and end apart: 5, of which 3 were waited for; matrix products, arithmetic and copies ran while one was open for 3% of the time, Pallas kernels for 7%

profile of v7, /device:TPU:0, one launch (start us, length us, event | category | flops | bytes accessed | tf_op | source)
XLA Modules:
  0.0 16.3 jit_solution(15175921271241386760)
XLA Ops:
  0.6 0.8 %shard_map.77.source_ref.block_ref.refs_0_ = f32[13,8,128]{2,1,0:T(8,128)S(1)} custom-call(f32[12,8,128]{2,1,0:T(8,128)} %bitcast.5, f32[8,128]{1,0:T(8,128)} %bitcast.6), custom_call_target="tpu_custom_call" | custom-call | tf_op jit(solution)/shard_map/pallas_call | solution.py:393
  1.4 3.1 %collective-permute-start = (f32[13,8,128]{2,1,0:T(8,128)S(1)}, f32[13,8,128]{2,1,0:T(8,128)S(1)}, u32[]{:S(2)}, u32[]{:S(2)}) collective-permute-start(f32[13,8,128]{2,1,0:T(8,128)S(1)} %shard_map.77.source_ref.block_ref.refs_0_), channel_id=1, source_target_pairs={{0,4},{4,8},{8,12},{12,0},{1,5},{5,9},{9,13},{13,1},{2,6},{6,10},{... | collective-permute-start | bytes 159752 | tf_op jit(solution)/shard_map/ppermute | solution.py:345
  4.5 0.0 copy-start
  4.5 0.0 copy-start.1
  4.5 2.7 %collective-permute-start.1 = (f32[13,8,128]{2,1,0:T(8,128)S(1)}, f32[13,8,128]{2,1,0:T(8,128)S(1)}, u32[]{:S(2)}, u32[]{:S(2)}) collective-permute-start(f32[13,8,128]{2,1,0:T(8,128)S(1)} %get-tuple-element.34), channel_id=1, source_target_pairs={{0,8},{4,12},{8,0},{12,4},{1,9},{5,13},{9,1},{13,5},{2,10},{6,14},... | collective-permute-start | bytes 159752 | tf_op jit(solution)/shard_map/ppermute | solution.py:345
  7.2 1.3 %collective-permute-start.2 = (f32[13,8,128]{2,1,0:T(8,128)S(1)}, f32[13,8,128]{2,1,0:T(8,128)S(1)}, u32[]{:S(2)}, u32[]{:S(2)}) collective-permute-start(f32[13,8,128]{2,1,0:T(8,128)S(1)} %get-tuple-element.35), channel_id=1, source_target_pairs={{0,12},{4,0},{8,4},{12,8},{1,13},{5,1},{9,5},{13,9},{2,14},{6,2},{... | collective-permute-start | bytes 159752 | tf_op jit(solution)/shard_map/ppermute | solution.py:345
  8.5 0.0 copy-done
  8.5 0.0 copy-done.1
  8.6 0.2 %select_reduce_fusion = f32[11,16]{1,0:T(8,128)S(1)} fusion(f32[64]{0:T(128)S(1)} %copy-done.1, s32[11,16]{1,0:T(8,128)S(1)} %copy-done), kind=kLoop, calls=%fused_computation | loop fusion | flops 33616 | bytes 1664 | tf_op jit(solution)/shard_map/reduce_sum | solution.py:320
  8.7 0.0 copy-start.2
  8.7 0.0 copy-start.3
  8.8 0.6 %copy-done.2 = f32[64]{0:T(128)S(1)} copy-done((f32[64]{0:T(128)S(1)}, f32[64]{0:T(128)}, u32[]{:S(2)}) %copy-start.2) | copy-done | bytes 280
  9.4 0.0 copy-done.3
  9.4 0.2 %select_reduce_fusion.1 = f32[16]{0:T(128)S(1)} fusion(f32[64]{0:T(128)S(1)} %copy-done.2, s32[16]{0:T(128)S(1)} %copy-done.3), kind=kLoop, calls=%fused_computation.2 | loop fusion | flops 3056 | bytes 384 | tf_op jit(solution)/shard_map/reduce_sum | solution.py:321
  9.6 0.1 broadcast_in_dim.45.share_ref
  9.7 0.1 broadcast_in_dim.42.cross_ref
  9.7 0.3 %shard_map.79 = (f32[4,2,16,128]{3,2,1,0:T(8,128)S(1)}, f32[32,16,128]{2,1,0:T(8,128)S(1)}, f32[2,32,16,128]{3,2,1,0:T(8,128)S(1)}, f32[4,8,128]{2,1,0:T(8,128)S(1)}, f32[4,8,128]{2,1,0:T(8,128)S(1)}) custom-call(f32[13,8,128]{2,1,0:T(8,128)S(1)} %shard_map.77.source_ref.block_ref.refs_0_, f32[11,16,128]{2,1,0:T(8,128)S(1)} %broadcast_in_dim.42.cross_ref, ...), custom_call_target="tpu_custom_call" | custom-call | tf_op jit(solution)/shard_map/pallas_call | solution.py:365
  10.0 0.0 collective-permute-done.block_ref.refs_1_
  10.0 0.1 shard_map.80
  10.1 0.8 %collective-permute-done.1.block_ref.refs_2_ = f32[13,8,128]{2,1,0:T(8,128)S(1)} collective-permute-done((f32[13,8,128]{2,1,0:T(8,128)S(1)}, f32[13,8,128]{2,1,0:T(8,128)S(1)}, u32[]{:S(2)}, u32[]{:S(2)}) %collective-permute-start.1) | collective-permute-done | bytes 53280 | tf_op jit(solution)/shard_map/ppermute | solution.py:345
  11.0 0.1 shard_map.81
  11.0 0.4 %collective-permute-done.2.block_ref.refs_3_ = f32[13,8,128]{2,1,0:T(8,128)S(1)} collective-permute-done((f32[13,8,128]{2,1,0:T(8,128)S(1)}, f32[13,8,128]{2,1,0:T(8,128)S(1)}, u32[]{:S(2)}, u32[]{:S(2)}) %collective-permute-start.2) | collective-permute-done | bytes 53280 | tf_op jit(solution)/shard_map/ppermute | solution.py:345
  11.4 0.1 shard_map.82
  11.5 0.3 %shard_map.83 = (f32[4,8,128]{2,1,0:T(8,128)S(1)}, f32[1,128]{1,0:T(1,128)S(1)}, f32[4,8,128]{2,1,0:T(8,128)S(1)}, f32[4,8,128]{2,1,0:T(8,128)S(1)}) custom-call(f32[4,2,16,128]{3,2,1,0:T(8,128)S(1)} %get-tuple-element.51.step_ref, f32[32,16,128]{2,1,0:T(8,128)S(1)} %get-tuple-element.52.emit_ref, f32[2,32,16,128]{3,2,1,0:T(8,128)S(1)} %get-tuple-element.53.decay_ref, ...), custom_call_target="tpu_custom_call" | custom-call | tf_op jit(solution)/shard_map/pallas_call | solution.py:365
  11.8 0.0 collective-permute-start.3
  11.8 1.7 %collective-permute-start.4 = (f32[4,8,128]{2,1,0:T(8,128)S(1)}, f32[4,8,128]{2,1,0:T(8,128)S(1)}, u32[]{:S(2)}, u32[]{:S(2)}) collective-permute-start(f32[4,8,128]{2,1,0:T(8,128)S(1)} %get-tuple-element.60.my_inner_ref), channel_id=1, source_target_pairs={{0,1},{1,0},{2,3},{3,2},{4,5},{5,4},{6,7},{7,6},{8,9},{9,8},{10,11... | collective-permute-start | bytes 49160 | tf_op jit(solution)/shard_map/ppermute | solution.py:418
  13.5 0.7 %shard_map.84 = (f32[4,12,8,128]{3,2,1,0:T(8,128)S(1)}, f32[4,8,128]{2,1,0:T(8,128)S(1)}) custom-call(f32[13,8,128]{2,1,0:T(8,128)S(1)} %shard_map.77.source_ref.block_ref.refs_0_, f32[13,8,128]{2,1,0:T(8,128)S(1)} %collective-permute-done.block_ref.refs_1_, f32[13,8,128]{2,1,0:T(8,128)S(1)} %collective-permute-done.1.block_ref.refs_2_, ...), custom_call_target="tpu_custom_call" | custom-call | tf_op jit(solution)/shard_map/pallas_call | solution.py:365
  14.2 0.7 %collective-permute-done.3.outer_ref = f32[4,8,128]{2,1,0:T(8,128)S(1)} collective-permute-done((f32[4,8,128]{2,1,0:T(8,128)S(1)}, f32[4,8,128]{2,1,0:T(8,128)S(1)}, u32[]{:S(2)}, u32[]{:S(2)}) %collective-permute-start.3) | collective-permute-done | bytes 16416 | tf_op jit(solution)/shard_map/ppermute | solution.py:419
  14.9 0.0 collective-permute-done.4.inner_ref
  15.0 0.2 %shard_map.85 = (f32[4,12,8,128]{3,2,1,0:T(8,128)S(1)}, f32[12,8,128]{2,1,0:T(8,128)S(1)}) custom-call(f32[4,12,8,128]{3,2,1,0:T(8,128)S(1)} %get-tuple-element.57.middle_in_ref, f32[4,8,128]{2,1,0:T(8,128)S(1)} %get-tuple-element.58.packed_ref, f32[4,8,128]{2,1,0:T(8,128)S(1)} %get-tuple-element.59.my_outer_ref, ...), custom_call_target="tpu_custom_call", output_to_operand_aliasing={{0}: (0, {})} | custom-call | tf_op jit(solution)/shard_map/pallas_call | solution.py:365
  15.2 1.1 %shard_map.86 = (f32[12,8,128]{2,1,0:T(8,128)}, f32[1,128]{1,0:T(1,128)}) custom-call(f32[13,8,128]{2,1,0:T(8,128)S(1)} %shard_map.77.source_ref.block_ref.refs_0_, f32[4,12,8,128]{3,2,1,0:T(8,128)S(1)} %get-tuple-element.61.middle_ref, f32[12,8,128]{2,1,0:T(8,128)S(1)} %get-tuple-element.62.edge_ref, f32[1,128]{1,0:T(1,128)S(1)} %get-tuple-element.63.wall_in_ref, ...), custom_call_target="tpu_custom_call" | custom-call | tf_op jit(solution)/shard_map/pallas_call | solution.py:365
  (2 shorter events, 0.0 us)
Async XLA Ops:
  1.4 8.6 %collective-permute-start = (f32[13,8,128]{2,1,0:T(8,128)S(1)}, f32[13,8,128]{2,1,0:T(8,128)S(1)}, u32[]{:S(2)}, u32[]{:S(2)}) collective-permute-start(f32[13,8,128]{2,1,0:T(8,128)S(1)} %shard_map.77.source_ref.block_ref.refs_0_), channel_id=1, source_target_pairs={{0,4},{4,8},{8,12},{12,0},{1,5},{5,9},{9,13},{13,1},{2,6},{6,10},{... | collective-permute-start | bytes 159752 | tf_op jit(solution)/shard_map/ppermute | solution.py:345
  4.5 4.0 %copy-start = (s32[11,16]{1,0:T(8,128)S(1)}, s32[11,16]{1,0:T(8,128)}, u32[]{:S(2)}) copy-start(s32[11,16]{1,0:T(8,128)} %param.10) | copy-start | bytes 2116
  4.5 4.0 %copy-start.1 = (f32[64]{0:T(128)S(1)}, f32[64]{0:T(128)}, u32[]{:S(2)}) copy-start(f32[64]{0:T(128)} %param.8) | copy-start | bytes 772
  4.5 6.4 %collective-permute-start.1 = (f32[13,8,128]{2,1,0:T(8,128)S(1)}, f32[13,8,128]{2,1,0:T(8,128)S(1)}, u32[]{:S(2)}, u32[]{:S(2)}) collective-permute-start(f32[13,8,128]{2,1,0:T(8,128)S(1)} %get-tuple-element.34), channel_id=1, source_target_pairs={{0,8},{4,12},{8,0},{12,4},{1,9},{5,13},{9,1},{13,5},{2,10},{6,14},... | collective-permute-start | bytes 159752 | tf_op jit(solution)/shard_map/ppermute | solution.py:345
  7.2 4.2 %collective-permute-start.2 = (f32[13,8,128]{2,1,0:T(8,128)S(1)}, f32[13,8,128]{2,1,0:T(8,128)S(1)}, u32[]{:S(2)}, u32[]{:S(2)}) collective-permute-start(f32[13,8,128]{2,1,0:T(8,128)S(1)} %get-tuple-element.35), channel_id=1, source_target_pairs={{0,12},{4,0},{8,4},{12,8},{1,13},{5,1},{9,5},{13,9},{2,14},{6,2},{... | collective-permute-start | bytes 159752 | tf_op jit(solution)/shard_map/ppermute | solution.py:345
  8.7 0.7 %copy-start.2 = (f32[64]{0:T(128)S(1)}, f32[64]{0:T(128)}, u32[]{:S(2)}) copy-start(f32[64]{0:T(128)} %param.9) | copy-start | bytes 772
  8.7 0.7 %copy-start.3 = (s32[16]{0:T(128)S(1)}, s32[16]{0:T(128)}, u32[]{:S(2)}) copy-start(s32[16]{0:T(128)} %param.11) | copy-start | bytes 196
  11.8 3.2 %collective-permute-start.3 = (f32[4,8,128]{2,1,0:T(8,128)S(1)}, f32[4,8,128]{2,1,0:T(8,128)S(1)}, u32[]{:S(2)}, u32[]{:S(2)}) collective-permute-start(f32[4,8,128]{2,1,0:T(8,128)S(1)} %get-tuple-element.59.my_outer_ref), channel_id=1, source_target_pairs={{0,3},{1,2},{2,1},{3,0},{4,7},{5,6},{6,5},{7,4},{8,11},{9,10},{10,... | collective-permute-start | bytes 49160 | tf_op jit(solution)/shard_map/ppermute | solution.py:419
  11.8 3.2 %collective-permute-start.4 = (f32[4,8,128]{2,1,0:T(8,128)S(1)}, f32[4,8,128]{2,1,0:T(8,128)S(1)}, u32[]{:S(2)}, u32[]{:S(2)}) collective-permute-start(f32[4,8,128]{2,1,0:T(8,128)S(1)} %get-tuple-element.60.my_inner_ref), channel_id=1, source_target_pairs={{0,1},{1,0},{2,3},{3,2},{4,5},{5,4},{6,7},{7,6},{8,9},{9,8},{10,11... | collective-permute-start | bytes 49160 | tf_op jit(solution)/shard_map/ppermute | solution.py:418

commit v8 on v7

--- a/solution.py
+++ b/solution.py
@@ -15,6 +15,8 @@
 SPECIES = 11
 BANDS = 16
 EDGE = 6
+HALF = 3
+SHARE = 3
 COURANT = 12
 PIECES = 3
 TILES = 13
@@ -51,6 +53,24 @@
         last = jnp.where(here, roll(block[k], EDGE * k - (cols - EDGE)), last)
         first = jnp.where(here, roll(block[k], EDGE * k), first)
     return last, first
+
+
+def border_tiles(block, lane, start):
+    cols = lane.shape[-1]
+    last = jnp.zeros(lane.shape, jnp.float32)
+    first = jnp.zeros(lane.shape, jnp.float32)
+    for k in range(COMPS):
+        left = start + HALF * k
+        here = (lane >= left) & (lane < left + HALF)
+        last = jnp.where(here, roll(block[k], left - (cols - HALF)), last)
+        first = jnp.where(here, roll(block[k], left), first)
+    return last, first
+
+
+def repeat(group, width):
+    group = group + roll(group, width)
+    group = group + roll(group, 2 * width)
+    return group + roll(group, 4 * width) + roll(group, 8 * width)
 
 
 def spread(value, lane, start, widths):
@@ -145,7 +165,11 @@
     return wall
 
 
-def arrive_kernel(slots, block_ref, cross_ref, share_ref, *refs):
+def seat(arrival):
+    return (0, 0) if arrival == 0 else (1 + (arrival - 1) // SHARE, (arrival - 1) % SHARE * HALF * COMPS)
+
+
+def arrive_kernel(arrival, slots, block_ref, cross_ref, share_ref, *refs):
     step_ref, emit_ref, decay_ref, outer_ref, inner_ref = refs[-5:]
     rows, cols = block_ref.shape[-2:]
     lane = lanes((rows, cols))
@@ -154,12 +178,16 @@
 
     def take(block, slot):
         absorb(block, (me ^ slot) * rows, rows, cross_ref, share_ref, step_ref, emit_ref, decay_ref)
-        last, first = edge_tiles(block, lane)
-        outer_ref[slot] = jnp.where(odd, last, first)
-        inner_ref[slot] = jnp.where(odd, first, last)
+
+    def pack(block, arrival):
+        tile, start = seat(arrival)
+        last, first = edge_tiles(block, lane) if arrival == 0 else border_tiles(block, lane, start)
+        for ref, value in ((outer_ref, jnp.where(odd, last, first)), (inner_ref, jnp.where(odd, first, last))):
+            ref[tile] = value if start == 0 else jnp.where(lane < start, ref[tile], value)
 
     if len(block_ref.shape) == 3:
         take(block_ref, slot_here(slots))
+        pack(block_ref, arrival)
     else:
 
         def body(i, carry):
@@ -167,6 +195,8 @@
             return carry
 
         loop(block_ref.shape[0], body, 0)
+        for i in range(block_ref.shape[0]):
+            pack(block_ref.at[i], i)
     if slots[0] == 0:
         own = block_ref if len(block_ref.shape) == 3 else block_ref.at[0]
         edges = spread(own[COURANT], lane, PACKED, (1, 2, 4))
@@ -182,7 +212,7 @@
     lane = lanes((rows, cols))
     for s in range(parts):
         heating_ref[s] = heat_ref[me ^ s]
-    for s in range(1, parts):
+    for s in range(1, outer_ref.shape[0]):
         outer_ref[s] = outer_in_ref[s]
         inner_ref[s] = inner_in_ref[s]
     here = (lane >= HEAT_AT) & (lane < HEAT_AT + EDGE)
@@ -214,25 +244,42 @@
     rows, cols = heating_ref.shape[1:]
     lane = lanes((rows, cols))
 
-    def advance(block, s):
+    def advance(block, s, slot):
         factors = coefficients(block[COURANT])
-        packed_ref[s] = spread(block[COURANT], lane, 0, (1, 2, 4, 8))
         for k in range(COMPS):
             moved = stencil(block[k], None, factors, lane, cols)
             if k == 0:
-                moved = moved + COUPLING * heating_ref[s]
+                moved = moved + COUPLING * heating_ref[slot]
             middle_ref[s, k] = moved
 
     if len(ids) > 1:
-        for block, slot in zip(blocks, ids):
-            advance(block, slot_here(slot))
+        for s, (block, slots) in enumerate(zip(blocks, ids)):
+            advance(block, s, slot_here(slots))
+        arrivals = blocks
     else:
 
         def body(s, carry):
-            advance(blocks[0].at[s], s)
+            advance(blocks[0].at[s], s, s)
             return carry
 
         loop(heating_ref.shape[0], body, 0)
+        arrivals = [blocks[0].at[s] for s in range(heating_ref.shape[0])]
+
+    odd = lax.rem(lax.axis_index("azim"), 2) == 1
+    packed_ref[...] = jnp.zeros(packed_ref.shape, jnp.float32)
+    for arrival, block in enumerate(arrivals):
+        courant = block[COURANT]
+        tile, start = seat(arrival)
+        if arrival == 0:
+            own = repeat(jnp.where(lane < EDGE, roll(courant, HALF), 0.0), EDGE)
+            packed_ref[0, 0] = own
+            continue
+        here = (lane >= start) & (lane < start + HALF)
+        right = repeat(jnp.where(here, roll(courant, start + HALF), 0.0), HALF)
+        left = repeat(jnp.where(here, roll(courant, start), 0.0), HALF)
+        fresh = lane >= start
+        packed_ref[0, tile] = jnp.where(fresh, right, packed_ref[0, tile])
+        packed_ref[1, tile] = jnp.where(fresh, left, packed_ref[1, tile])
 
 
 def border_kernel(middle_in_ref, packed_ref, my_outer_ref, my_inner_ref, outer_ref, inner_ref, middle_ref, edge_ref, change_ref):
@@ -250,22 +297,33 @@
             jnp.where(odd, my_outer, my_inner), jnp.where(odd, my_inner, my_outer),
         )
 
-    def differ(s, carry):
-        left, right, last, first = sides(s)
-        left, right = left - last, right - first
-        factors = coefficients(packed_ref[s])
-        change = jnp.zeros((rows, cols), jnp.float32)
+    tiles = outer_ref.shape[0]
+    left, right, last, first = sides(0)
+    factors = coefficients(packed_ref[0, 0])
+    far, near = right - first, left - last
+    change = jnp.zeros((rows, cols), jnp.float32)
+    for reach in range(1, three + 1):
+        ahead = factors[2 * reach - 2] * roll(far, three - reach)
+        behind = factors[2 * reach - 1] * roll(near, reach - three)
+        ahead = jnp.where((at >= three - reach) & (at < three), ahead, 0.0)
+        change = change + jnp.where((at >= three) & (at < three + reach), behind, ahead)
+    change_ref[0, 0] = change
+    third = lax.rem(lane, three)
+    even_group = at < three
+    for tile in range(1, tiles):
+        other_left, other_right, other_last, other_first = sides(tile)
+        far, near = other_right - other_first, other_left - other_last
+        ahead_factors, behind_factors = coefficients(packed_ref[0, tile]), coefficients(packed_ref[1, tile])
+        ahead = behind = jnp.zeros((rows, cols), jnp.float32)
         for reach in range(1, three + 1):
-            ahead = factors[2 * reach - 2] * roll(right, three - reach)
-            behind = factors[2 * reach - 1] * roll(left, reach - three)
-            ahead = jnp.where((at >= three - reach) & (at < three), ahead, 0.0)
-            change = change + jnp.where((at >= three) & (at < three + reach), behind, ahead)
-        change_ref[s] = change
-        return carry
-
-    loop(parts, differ, 0)
-
-    left, right, last, first = sides(0)
+            term = ahead_factors[2 * reach - 2] * roll(far, three - reach)
+            ahead = ahead + jnp.where(third >= three - reach, term, 0.0)
+            term = behind_factors[2 * reach - 1] * roll(near, reach - three)
+            behind = behind + jnp.where(third < reach, term, 0.0)
+        behind = roll(behind, three)
+        change_ref[0, tile] = jnp.where(even_group, ahead, behind)
+        change_ref[1, tile] = jnp.where(even_group, behind, ahead)
+
     outside = jnp.where(at < three, left, right)
     courant = jnp.where(lane < 8 * EDGE, roll(outside, -PACKED), roll(outside, 8 * EDGE - PACKED))
     factors = dict(zip(OFFSETS, coefficients(courant)))
@@ -278,20 +336,20 @@
     edge_change = edge
 
     border = (lane < three) | (lane >= cols - three)
-
-    def mend(s, carry):
-        change = change_ref[s]
+    for arrival in range(parts):
+        tile, start = seat(arrival)
+        changes = change_ref[0, tile], change_ref[1, tile]
         for k in range(COMPS):
-            middle_ref[s, k] = middle_in_ref[s, k] + jnp.where(border, roll(change, -(EDGE * k + three)), 0.0)
-        return carry
-
-    loop(parts, mend, 0)
+            moved = changes[0] if arrival == 0 else changes[k % 2]
+            width = EDGE if arrival == 0 else three
+            gain = jnp.where(border, roll(moved, -(start + width * k + three)), 0.0)
+            middle_ref[arrival, k] = middle_in_ref[arrival, k] + gain
     edge = edge_change
     for k in range(COMPS):
         edge_ref[k] = roll(edge, -(EDGE * k + three))
 
 
-def last_kernel(block_ref, middle_ref, edge_ref, wall_in_ref, cross_ref, share_ref, out_ref, wall_ref, *scratch):
+def last_kernel(ids, block_ref, middle_ref, edge_ref, wall_in_ref, cross_ref, share_ref, out_ref, wall_ref, *scratch):
     heat_ref = scratch[-1]
     own = block_ref if len(block_ref.shape) == 3 else block_ref.at[0]
     rows, cols = out_ref.shape[1:]
@@ -299,8 +357,9 @@
     me = lax.axis_index("wall")
     step_ref, emit_ref, decay_ref = scratch[:3]
 
-    def take(slot, carry):
-        absorb(middle_ref.at[slot], (me ^ slot) * rows, rows, cross_ref, share_ref, step_ref, emit_ref, decay_ref)
+    def take(s, carry):
+        slot = slot_here(ids[s]) if len(ids) > 1 else s
+        absorb(middle_ref.at[s], (me ^ slot) * rows, rows, cross_ref, share_ref, step_ref, emit_ref, decay_ref)
         return carry
 
     loop(middle_ref.shape[0], take, 0)
@@ -403,14 +462,14 @@
     deep = (count, BANDS, cols)
     flat = (count, BANDS // 2, cols)
     whole = (parts,) + tile
-    message = (parts,) + tile
+    message = (1 + pl.cdiv(parts - 1, SHARE),) + tile
     ends = (parts, 2, BANDS, cols)
     both = (2,) + deep
     state_of = [ends, deep, both, message, message]
     held = []
-    for received, slot in zip(blocks, ids):
+    for arrival, (received, slot) in enumerate(zip(blocks, ids)):
         held = call(
-            functools.partial(arrive_kernel, slot), state_of, [], received, cross, share, *held,
+            functools.partial(arrive_kernel, arrival, slot), state_of, [], received, cross, share, *held,
             aliases={3 + j: j for j in range(len(held))},
         )
     scratch = [flat, flat, (count + 2 * rows, cols), whole]
@@ -418,14 +477,14 @@
     inner = lax.ppermute(my_inner, "azim", [(i, i ^ 1) for i in range(ring)])
     outer = lax.ppermute(my_outer, "azim", [(i, (i + 1) % ring if i % 2 else (i - 1) % ring) for i in range(ring)])
     middle, packed = call(
-        functools.partial(center_kernel, ids), [(parts, comps) + tile, whole], [], *blocks, heating,
+        functools.partial(center_kernel, ids), [(parts, comps) + tile, (2,) + message], [], *blocks, heating,
     )
     middle, edge = call(
-        border_kernel, [(parts, comps) + tile, (comps,) + tile], [message],
+        border_kernel, [(parts, comps) + tile, (comps,) + tile], [(2,) + message],
         middle, packed, my_outer, my_inner, outer, inner, aliases={0: 0},
     )
     new_state, wall = call(
-        last_kernel, [(comps,) + tile, (1, cols)], [ends, deep, both] + scratch,
+        functools.partial(last_kernel, ids), [(comps,) + tile, (1, cols)], [ends, deep, both] + scratch,
         blocks[0], middle, edge, wall, cross, share,
     )
     return new_state.reshape(state.shape), wall

time: 16.6 us -> 16.5 us (level)
  transfers between devices with their start and end apart: 5 -> 5, of which waited for: 3 -> 3; matrix products, arithmetic and copies ran while one was open for 3% -> 3% of each run, Pallas kernels for 7% -> 6%
where the time goes in v8:
time: 16.5 us; the launch traced here: 16.3 us
  starting transfers between devices  8.83 us (54%)
  Pallas kernels  3.53 us (21%)
  waiting for transfers between devices  2.02 us (12%)
  local copies, waits for them, and re-layouts  0.81 us (5%)
  between operations  0.72 us (4%)
  other arithmetic  0.36 us (2%)
    ppermute x3, starting transfers between devices, gather_lines(): blocks.append(lax.ppermute(sent, 'wall', list(enumerate(targets))))  7.08 us
    pallas_call x9, Pallas kernels, call(): pl.pallas_call(kernel, out_shape=[jax.ShapeDtypeStruct(shape, jnp.float32...  2.72 us
    ppermute x1, starting transfers between devices, local(): inner = lax.ppermute(my_inner, 'azim', [(i, i ^ 1) for i in range(ring)])  1.74 us
    ppermute x3, waiting for transfers between devices, gather_lines(): blocks.append(lax.ppermute(sent, 'wall', list(enumerate(targets))))  1.2 us
    ppermute x1, waiting for transfers between devices, local(): lax.ppermute(my_outer, 'azim', [(i, (i + 1) % ring if i % 2 else (i - 1)...  0.82 us
    pallas_call x1, Pallas kernels, local(): pl.pallas_call(join_kernel, out_shape=pltpu.VMEM((TILES,) + tile, jnp.flo...  0.8 us
    unnamed x8, local copies, waits for them, and re-layouts  0.66 us
  transfers between devices with their start and end apart: 5, of which 3 were waited for; matrix products, arithmetic and copies ran while one was open for 3% of the time, Pallas kernels for 6%

profile of v8, /device:TPU:0, one launch (start us, length us, event | category | flops | bytes accessed | tf_op | source)
XLA Modules:
  0.0 16.3 jit_solution(5708231214421821183)
XLA Ops:
  0.6 0.8 %shard_map.77.source_ref.block_ref.refs_0_ = f32[13,8,128]{2,1,0:T(8,128)S(1)} custom-call(f32[12,8,128]{2,1,0:T(8,128)} %bitcast.5, f32[8,128]{1,0:T(8,128)} %bitcast.6), custom_call_target="tpu_custom_call" | custom-call | tf_op jit(solution)/shard_map/pallas_call | solution.py:452
  1.4 3.1 %collective-permute-start = (f32[13,8,128]{2,1,0:T(8,128)S(1)}, f32[13,8,128]{2,1,0:T(8,128)S(1)}, u32[]{:S(2)}, u32[]{:S(2)}) collective-permute-start(f32[13,8,128]{2,1,0:T(8,128)S(1)} %shard_map.77.source_ref.block_ref.refs_0_), channel_id=1, source_target_pairs={{0,4},{4,8},{8,12},{12,0},{1,5},{5,9},{9,13},{13,1},{2,6},{6,10},{... | collective-permute-start | bytes 159752 | tf_op jit(solution)/shard_map/ppermute | solution.py:404
  4.5 0.0 copy-start
  4.5 0.0 copy-start.1
  4.5 2.7 %collective-permute-start.1 = (f32[13,8,128]{2,1,0:T(8,128)S(1)}, f32[13,8,128]{2,1,0:T(8,128)S(1)}, u32[]{:S(2)}, u32[]{:S(2)}) collective-permute-start(f32[13,8,128]{2,1,0:T(8,128)S(1)} %get-tuple-element.34), channel_id=1, source_target_pairs={{0,8},{4,12},{8,0},{12,4},{1,9},{5,13},{9,1},{13,5},{2,10},{6,14},... | collective-permute-start | bytes 159752 | tf_op jit(solution)/shard_map/ppermute | solution.py:404
  7.2 1.3 %collective-permute-start.2 = (f32[13,8,128]{2,1,0:T(8,128)S(1)}, f32[13,8,128]{2,1,0:T(8,128)S(1)}, u32[]{:S(2)}, u32[]{:S(2)}) collective-permute-start(f32[13,8,128]{2,1,0:T(8,128)S(1)} %get-tuple-element.35), channel_id=1, source_target_pairs={{0,12},{4,0},{8,4},{12,8},{1,13},{5,1},{9,5},{13,9},{2,14},{6,2},{... | collective-permute-start | bytes 159752 | tf_op jit(solution)/shard_map/ppermute | solution.py:404
  8.5 0.0 copy-done
  8.5 0.0 copy-done.1
  8.6 0.2 %select_reduce_fusion = f32[11,16]{1,0:T(8,128)S(1)} fusion(f32[64]{0:T(128)S(1)} %copy-done.1, s32[11,16]{1,0:T(8,128)S(1)} %copy-done), kind=kLoop, calls=%fused_computation | loop fusion | flops 33616 | bytes 1664 | tf_op jit(solution)/shard_map/reduce_sum | solution.py:379
  8.7 0.0 copy-start.2
  8.7 0.0 copy-start.3
  8.8 0.6 %copy-done.2 = f32[64]{0:T(128)S(1)} copy-done((f32[64]{0:T(128)S(1)}, f32[64]{0:T(128)}, u32[]{:S(2)}) %copy-start.2) | copy-done | bytes 280
  9.4 0.0 copy-done.3
  9.4 0.2 %select_reduce_fusion.1 = f32[16]{0:T(128)S(1)} fusion(f32[64]{0:T(128)S(1)} %copy-done.2, s32[16]{0:T(128)S(1)} %copy-done.3), kind=kLoop, calls=%fused_computation.2 | loop fusion | flops 3056 | bytes 384 | tf_op jit(solution)/shard_map/reduce_sum | solution.py:380
  9.6 0.1 broadcast_in_dim.45.share_ref
  9.7 0.1 broadcast_in_dim.42.cross_ref
  9.7 0.3 %shard_map.79 = (f32[4,2,16,128]{3,2,1,0:T(8,128)S(1)}, f32[32,16,128]{2,1,0:T(8,128)S(1)}, f32[2,32,16,128]{3,2,1,0:T(8,128)S(1)}, f32[2,8,128]{2,1,0:T(8,128)S(1)}, f32[2,8,128]{2,1,0:T(8,128)S(1)}) custom-call(f32[13,8,128]{2,1,0:T(8,128)S(1)} %shard_map.77.source_ref.block_ref.refs_0_, f32[11,16,128]{2,1,0:T(8,128)S(1)} %broadcast_in_dim.42.cross_ref, ...), custom_call_target="tpu_custom_call" | custom-call | tf_op jit(solution)/shard_map/pallas_call | solution.py:424
  10.0 0.0 collective-permute-done.block_ref.refs_1_
  10.0 0.1 shard_map.80
  10.1 0.8 %collective-permute-done.1.block_ref.refs_2_ = f32[13,8,128]{2,1,0:T(8,128)S(1)} collective-permute-done((f32[13,8,128]{2,1,0:T(8,128)S(1)}, f32[13,8,128]{2,1,0:T(8,128)S(1)}, u32[]{:S(2)}, u32[]{:S(2)}) %collective-permute-start.1) | collective-permute-done | bytes 53280 | tf_op jit(solution)/shard_map/ppermute | solution.py:404
  11.0 0.1 shard_map.81
  11.0 0.4 %collective-permute-done.2.block_ref.refs_3_ = f32[13,8,128]{2,1,0:T(8,128)S(1)} collective-permute-done((f32[13,8,128]{2,1,0:T(8,128)S(1)}, f32[13,8,128]{2,1,0:T(8,128)S(1)}, u32[]{:S(2)}, u32[]{:S(2)}) %collective-permute-start.2) | collective-permute-done | bytes 53280 | tf_op jit(solution)/shard_map/ppermute | solution.py:404
  11.4 0.1 shard_map.82
  11.5 0.3 %shard_map.83 = (f32[4,8,128]{2,1,0:T(8,128)S(1)}, f32[1,128]{1,0:T(1,128)S(1)}, f32[2,8,128]{2,1,0:T(8,128)S(1)}, f32[2,8,128]{2,1,0:T(8,128)S(1)}) custom-call(f32[4,2,16,128]{3,2,1,0:T(8,128)S(1)} %get-tuple-element.51.step_ref, f32[32,16,128]{2,1,0:T(8,128)S(1)} %get-tuple-element.52.emit_ref, f32[2,32,16,128]{3,2,1,0:T(8,128)S(1)} %get-tuple-element.53.decay_ref, ...), custom_call_target="tpu_custom_call" | custom-call | tf_op jit(solution)/shard_map/pallas_call | solution.py:424
  11.8 0.0 collective-permute-start.3
  11.8 1.7 %collective-permute-start.4 = (f32[2,8,128]{2,1,0:T(8,128)S(1)}, f32[2,8,128]{2,1,0:T(8,128)S(1)}, u32[]{:S(2)}, u32[]{:S(2)}) collective-permute-start(f32[2,8,128]{2,1,0:T(8,128)S(1)} %get-tuple-element.60.my_inner_ref), channel_id=1, source_target_pairs={{0,1},{1,0},{2,3},{3,2},{4,5},{5,4},{6,7},{7,6},{8,9},{9,8},{10,11... | collective-permute-start | bytes 24584 | tf_op jit(solution)/shard_map/ppermute | solution.py:477
  13.5 0.5 %shard_map.84 = (f32[4,12,8,128]{3,2,1,0:T(8,128)S(1)}, f32[2,2,8,128]{3,2,1,0:T(8,128)S(1)}) custom-call(f32[13,8,128]{2,1,0:T(8,128)S(1)} %shard_map.77.source_ref.block_ref.refs_0_, f32[13,8,128]{2,1,0:T(8,128)S(1)} %collective-permute-done.block_ref.refs_1_, f32[13,8,128]{2,1,0:T(8,128)S(1)} %collective-permute-done.1.block_ref.refs_2_, ...), custom_call_target="tpu_custom_call" | custom-call | tf_op jit(solution)/shard_map/pallas_call | solution.py:424
  14.0 0.8 %collective-permute-done.3.outer_ref = f32[2,8,128]{2,1,0:T(8,128)S(1)} collective-permute-done((f32[2,8,128]{2,1,0:T(8,128)S(1)}, f32[2,8,128]{2,1,0:T(8,128)S(1)}, u32[]{:S(2)}, u32[]{:S(2)}) %collective-permute-start.3) | collective-permute-done | bytes 8224 | tf_op jit(solution)/shard_map/ppermute | solution.py:478
  14.9 0.0 collective-permute-done.4.inner_ref
  14.9 0.3 %shard_map.85 = (f32[4,12,8,128]{3,2,1,0:T(8,128)S(1)}, f32[12,8,128]{2,1,0:T(8,128)S(1)}) custom-call(f32[4,12,8,128]{3,2,1,0:T(8,128)S(1)} %get-tuple-element.57.middle_in_ref, f32[2,2,8,128]{3,2,1,0:T(8,128)S(1)} %get-tuple-element.58.packed_ref, f32[2,8,128]{2,1,0:T(8,128)S(1)} %get-tuple-element.59.my_outer_ref, ...), custom_call_target="tpu_custom_call", output_to_operand_aliasing={{0}: (0, {})} | custom-call | tf_op jit(solution)/shard_map/pallas_call | solution.py:424
  15.1 1.1 %shard_map.86 = (f32[12,8,128]{2,1,0:T(8,128)}, f32[1,128]{1,0:T(1,128)}) custom-call(f32[13,8,128]{2,1,0:T(8,128)S(1)} %shard_map.77.source_ref.block_ref.refs_0_, f32[4,12,8,128]{3,2,1,0:T(8,128)S(1)} %get-tuple-element.61.middle_ref, f32[12,8,128]{2,1,0:T(8,128)S(1)} %get-tuple-element.62.edge_ref, f32[1,128]{1,0:T(1,128)S(1)} %get-tuple-element.63.wall_in_ref, ...), custom_call_target="tpu_custom_call" | custom-call | tf_op jit(solution)/shard_map/pallas_call | solution.py:424
  (2 shorter events, 0.0 us)
Async XLA Ops:
  1.4 8.6 %collective-permute-start = (f32[13,8,128]{2,1,0:T(8,128)S(1)}, f32[13,8,128]{2,1,0:T(8,128)S(1)}, u32[]{:S(2)}, u32[]{:S(2)}) collective-permute-start(f32[13,8,128]{2,1,0:T(8,128)S(1)} %shard_map.77.source_ref.block_ref.refs_0_), channel_id=1, source_target_pairs={{0,4},{4,8},{8,12},{12,0},{1,5},{5,9},{9,13},{13,1},{2,6},{6,10},{... | collective-permute-start | bytes 159752 | tf_op jit(solution)/shard_map/ppermute | solution.py:404
  4.5 4.0 %copy-start = (s32[11,16]{1,0:T(8,128)S(1)}, s32[11,16]{1,0:T(8,128)}, u32[]{:S(2)}) copy-start(s32[11,16]{1,0:T(8,128)} %param.10) | copy-start | bytes 2116
  4.5 4.0 %copy-start.1 = (f32[64]{0:T(128)S(1)}, f32[64]{0:T(128)}, u32[]{:S(2)}) copy-start(f32[64]{0:T(128)} %param.8) | copy-start | bytes 772
  4.5 6.4 %collective-permute-start.1 = (f32[13,8,128]{2,1,0:T(8,128)S(1)}, f32[13,8,128]{2,1,0:T(8,128)S(1)}, u32[]{:S(2)}, u32[]{:S(2)}) collective-permute-start(f32[13,8,128]{2,1,0:T(8,128)S(1)} %get-tuple-element.34), channel_id=1, source_target_pairs={{0,8},{4,12},{8,0},{12,4},{1,9},{5,13},{9,1},{13,5},{2,10},{6,14},... | collective-permute-start | bytes 159752 | tf_op jit(solution)/shard_map/ppermute | solution.py:404
  7.2 4.2 %collective-permute-start.2 = (f32[13,8,128]{2,1,0:T(8,128)S(1)}, f32[13,8,128]{2,1,0:T(8,128)S(1)}, u32[]{:S(2)}, u32[]{:S(2)}) collective-permute-start(f32[13,8,128]{2,1,0:T(8,128)S(1)} %get-tuple-element.35), channel_id=1, source_target_pairs={{0,12},{4,0},{8,4},{12,8},{1,13},{5,1},{9,5},{13,9},{2,14},{6,2},{... | collective-permute-start | bytes 159752 | tf_op jit(solution)/shard_map/ppermute | solution.py:404
  8.7 0.7 %copy-start.2 = (f32[64]{0:T(128)S(1)}, f32[64]{0:T(128)}, u32[]{:S(2)}) copy-start(f32[64]{0:T(128)} %param.9) | copy-start | bytes 772
  8.7 0.7 %copy-start.3 = (s32[16]{0:T(128)S(1)}, s32[16]{0:T(128)}, u32[]{:S(2)}) copy-start(s32[16]{0:T(128)} %param.11) | copy-start | bytes 196
  11.8 3.1 %collective-permute-start.3 = (f32[2,8,128]{2,1,0:T(8,128)S(1)}, f32[2,8,128]{2,1,0:T(8,128)S(1)}, u32[]{:S(2)}, u32[]{:S(2)}) collective-permute-start(f32[2,8,128]{2,1,0:T(8,128)S(1)} %get-tuple-element.59.my_outer_ref), channel_id=1, source_target_pairs={{0,3},{1,2},{2,1},{3,0},{4,7},{5,6},{6,5},{7,4},{8,11},{9,10},{10,... | collective-permute-start | bytes 24584 | tf_op jit(solution)/shard_map/ppermute | solution.py:478
  11.8 3.1 %collective-permute-start.4 = (f32[2,8,128]{2,1,0:T(8,128)S(1)}, f32[2,8,128]{2,1,0:T(8,128)S(1)}, u32[]{:S(2)}, u32[]{:S(2)}) collective-permute-start(f32[2,8,128]{2,1,0:T(8,128)S(1)} %get-tuple-element.60.my_inner_ref), channel_id=1, source_target_pairs={{0,1},{1,0},{2,3},{3,2},{4,5},{5,4},{6,7},{7,6},{8,9},{9,8},{10,11... | collective-permute-start | bytes 24584 | tf_op jit(solution)/shard_map/ppermute | solution.py:477

commit v9 on v8

--- a/solution.py
+++ b/solution.py
@@ -135,19 +135,19 @@
             at = part * rows + r
             emitted = emit_ref[at]
             up0 = up0 * decay_ref[0, at] + emitted
-            up1 = up1 * decay_ref[1, at] + emitted
-            up_ref[at] = halve(up0 + ratio * up1)
+            up1 = up1 * decay_ref[1, at] + ratio * emitted
+            up_ref[at] = halve(up0 + up1)
             back = count - 1 - at
             emitted = emit_ref[back]
             down0 = down0 + emitted
-            down1 = down1 + emitted
-            down_ref[back] = halve(down0 + ratio * down1)
+            down1 = down1 + ratio * emitted
+            down_ref[back] = halve(down0 + down1)
             down0 = down0 * decay_ref[0, back]
             down1 = down1 * decay_ref[1, back]
         return up0, up1, down0, down1
 
     _, _, down0, down1 = loop(parts, sweep, (zero, zero, zero, zero))
-    wall = KERNEL_WEIGHTS[0] * jnp.sum(down0 + ratio * down1, axis=0, keepdims=True)
+    wall = KERNEL_WEIGHTS[0] * jnp.sum(down0 + down1, axis=0, keepdims=True)
 
     def combine(part, carry):
         rows_here = pl.ds(part * rows, rows)
@@ -204,7 +204,7 @@
             ref[0] = jnp.where(lane < PACKED, ref[0], edges)
 
 
-def first_kernel(step_ref, emit_ref, decay_ref, outer_in_ref, inner_in_ref, heating_ref, wall_ref, outer_ref, inner_ref, *scratch):
+def first_kernel(step_ref, emit_ref, decay_ref, outer_in_ref, inner_in_ref, outer_ref, inner_ref, heating_ref, wall_ref, *scratch):
     heat_ref = scratch[-1]
     parts, rows, cols = heating_ref.shape
     me = lax.axis_index("wall")
@@ -212,9 +212,6 @@
     lane = lanes((rows, cols))
     for s in range(parts):
         heating_ref[s] = heat_ref[me ^ s]
-    for s in range(1, outer_ref.shape[0]):
-        outer_ref[s] = outer_in_ref[s]
-        inner_ref[s] = inner_in_ref[s]
     here = (lane >= HEAT_AT) & (lane < HEAT_AT + EDGE)
     edges = roll(heat_ref[me], EDGE // 2 + HEAT_AT)
     outer_ref[0] = jnp.where(here, edges, outer_in_ref[0])
@@ -473,7 +470,9 @@
             aliases={3 + j: j for j in range(len(held))},
         )
     scratch = [flat, flat, (count + 2 * rows, cols), whole]
-    heating, wall, my_outer, my_inner = call(first_kernel, [whole, (1, cols), message, message], scratch, *held)
+    my_outer, my_inner, heating, wall = call(
+        first_kernel, [message, message, whole, (1, cols)], scratch, *held, aliases={3: 0, 4: 1},
+    )
     inner = lax.ppermute(my_inner, "azim", [(i, i ^ 1) for i in range(ring)])
     outer = lax.ppermute(my_outer, "azim", [(i, (i + 1) % ring if i % 2 else (i - 1) % ring) for i in range(ring)])
     middle, packed = call(

time: 16.5 us -> 16.5 us (level)
  no operation moved by 1% of the time
where the time goes in v9:
time: 16.5 us; the launch traced here: 16.3 us
  starting transfers between devices  8.83 us (54%)
  Pallas kernels  3.52 us (21%)
  waiting for transfers between devices  2.02 us (12%)
  local copies, waits for them, and re-layouts  0.81 us (5%)
  between operations  0.72 us (4%)
  other arithmetic  0.36 us (2%)
    ppermute x3, starting transfers between devices, gather_lines(): blocks.append(lax.ppermute(sent, 'wall', list(enumerate(targets))))  7.08 us
    pallas_call x9, Pallas kernels, call(): pl.pallas_call(kernel, out_shape=[jax.ShapeDtypeStruct(shape, jnp.float32...  2.71 us
    ppermute x1, starting transfers between devices, local(): inner = lax.ppermute(my_inner, 'azim', [(i, i ^ 1) for i in range(ring)])  1.74 us
    ppermute x3, waiting for transfers between devices, gather_lines(): blocks.append(lax.ppermute(sent, 'wall', list(enumerate(targets))))  1.2 us
    ppermute x1, waiting for transfers between devices, local(): lax.ppermute(my_outer, 'azim', [(i, (i + 1) % ring if i % 2 else (i - 1)...  0.82 us
    pallas_call x1, Pallas kernels, local(): pl.pallas_call(join_kernel, out_shape=pltpu.VMEM((TILES,) + tile, jnp.flo...  0.8 us
    unnamed x8, local copies, waits for them, and re-layouts  0.66 us
  transfers between devices with their start and end apart: 5, of which 3 were waited for; matrix products, arithmetic and copies ran while one was open for 3% of the time, Pallas kernels for 6%

profile of v9, /device:TPU:0, one launch (start us, length us, event | category | flops | bytes accessed | tf_op | source)
XLA Modules:
  0.0 16.3 jit_solution(4751836774450494286)
XLA Ops:
  0.6 0.8 %shard_map.77.source_ref.block_ref.refs_0_ = f32[13,8,128]{2,1,0:T(8,128)S(1)} custom-call(f32[12,8,128]{2,1,0:T(8,128)} %bitcast.5, f32[8,128]{1,0:T(8,128)} %bitcast.6), custom_call_target="tpu_custom_call" | custom-call | tf_op jit(solution)/shard_map/pallas_call | solution.py:449
  1.4 3.1 %collective-permute-start = (f32[13,8,128]{2,1,0:T(8,128)S(1)}, f32[13,8,128]{2,1,0:T(8,128)S(1)}, u32[]{:S(2)}, u32[]{:S(2)}) collective-permute-start(f32[13,8,128]{2,1,0:T(8,128)S(1)} %shard_map.77.source_ref.block_ref.refs_0_), channel_id=1, source_target_pairs={{0,4},{4,8},{8,12},{12,0},{1,5},{5,9},{9,13},{13,1},{2,6},{6,10},{... | collective-permute-start | bytes 159752 | tf_op jit(solution)/shard_map/ppermute | solution.py:401
  4.5 0.0 copy-start
  4.5 0.0 copy-start.1
  4.5 2.7 %collective-permute-start.1 = (f32[13,8,128]{2,1,0:T(8,128)S(1)}, f32[13,8,128]{2,1,0:T(8,128)S(1)}, u32[]{:S(2)}, u32[]{:S(2)}) collective-permute-start(f32[13,8,128]{2,1,0:T(8,128)S(1)} %get-tuple-element.34), channel_id=1, source_target_pairs={{0,8},{4,12},{8,0},{12,4},{1,9},{5,13},{9,1},{13,5},{2,10},{6,14},... | collective-permute-start | bytes 159752 | tf_op jit(solution)/shard_map/ppermute | solution.py:401
  7.2 1.3 %collective-permute-start.2 = (f32[13,8,128]{2,1,0:T(8,128)S(1)}, f32[13,8,128]{2,1,0:T(8,128)S(1)}, u32[]{:S(2)}, u32[]{:S(2)}) collective-permute-start(f32[13,8,128]{2,1,0:T(8,128)S(1)} %get-tuple-element.35), channel_id=1, source_target_pairs={{0,12},{4,0},{8,4},{12,8},{1,13},{5,1},{9,5},{13,9},{2,14},{6,2},{... | collective-permute-start | bytes 159752 | tf_op jit(solution)/shard_map/ppermute | solution.py:401
  8.5 0.0 copy-done
  8.5 0.0 copy-done.1
  8.6 0.2 %select_reduce_fusion = f32[11,16]{1,0:T(8,128)S(1)} fusion(f32[64]{0:T(128)S(1)} %copy-done.1, s32[11,16]{1,0:T(8,128)S(1)} %copy-done), kind=kLoop, calls=%fused_computation | loop fusion | flops 33616 | bytes 1664 | tf_op jit(solution)/shard_map/reduce_sum | solution.py:376
  8.7 0.0 copy-start.2
  8.7 0.0 copy-start.3
  8.8 0.6 %copy-done.2 = f32[64]{0:T(128)S(1)} copy-done((f32[64]{0:T(128)S(1)}, f32[64]{0:T(128)}, u32[]{:S(2)}) %copy-start.2) | copy-done | bytes 280
  9.4 0.0 copy-done.3
  9.4 0.2 %select_reduce_fusion.1 = f32[16]{0:T(128)S(1)} fusion(f32[64]{0:T(128)S(1)} %copy-done.2, s32[16]{0:T(128)S(1)} %copy-done.3), kind=kLoop, calls=%fused_computation.2 | loop fusion | flops 3056 | bytes 384 | tf_op jit(solution)/shard_map/reduce_sum | solution.py:377
  9.6 0.1 broadcast_in_dim.45.share_ref
  9.7 0.1 broadcast_in_dim.42.cross_ref
  9.7 0.3 %shard_map.79 = (f32[4,2,16,128]{3,2,1,0:T(8,128)S(1)}, f32[32,16,128]{2,1,0:T(8,128)S(1)}, f32[2,32,16,128]{3,2,1,0:T(8,128)S(1)}, f32[2,8,128]{2,1,0:T(8,128)S(1)}, f32[2,8,128]{2,1,0:T(8,128)S(1)}) custom-call(f32[13,8,128]{2,1,0:T(8,128)S(1)} %shard_map.77.source_ref.block_ref.refs_0_, f32[11,16,128]{2,1,0:T(8,128)S(1)} %broadcast_in_dim.42.cross_ref, ...), custom_call_target="tpu_custom_call" | custom-call | tf_op jit(solution)/shard_map/pallas_call | solution.py:421
  10.0 0.0 collective-permute-done.block_ref.refs_1_
  10.0 0.1 shard_map.80
  10.1 0.8 %collective-permute-done.1.block_ref.refs_2_ = f32[13,8,128]{2,1,0:T(8,128)S(1)} collective-permute-done((f32[13,8,128]{2,1,0:T(8,128)S(1)}, f32[13,8,128]{2,1,0:T(8,128)S(1)}, u32[]{:S(2)}, u32[]{:S(2)}) %collective-permute-start.1) | collective-permute-done | bytes 53280 | tf_op jit(solution)/shard_map/ppermute | solution.py:401
  11.0 0.1 shard_map.81
  11.0 0.4 %collective-permute-done.2.block_ref.refs_3_ = f32[13,8,128]{2,1,0:T(8,128)S(1)} collective-permute-done((f32[13,8,128]{2,1,0:T(8,128)S(1)}, f32[13,8,128]{2,1,0:T(8,128)S(1)}, u32[]{:S(2)}, u32[]{:S(2)}) %collective-permute-start.2) | collective-permute-done | bytes 53280 | tf_op jit(solution)/shard_map/ppermute | solution.py:401
  11.4 0.1 shard_map.82
  11.5 0.3 %shard_map.83 = (f32[2,8,128]{2,1,0:T(8,128)S(1)}, f32[2,8,128]{2,1,0:T(8,128)S(1)}, f32[4,8,128]{2,1,0:T(8,128)S(1)}, f32[1,128]{1,0:T(1,128)S(1)}) custom-call(f32[4,2,16,128]{3,2,1,0:T(8,128)S(1)} %get-tuple-element.51.step_ref, f32[32,16,128]{2,1,0:T(8,128)S(1)} %get-tuple-element.52.emit_ref, ...), custom_call_target="tpu_custom_call", output_to_operand_aliasing={{0}: (3, {}), {1}: (4, {})} | custom-call | tf_op jit(solution)/shard_map/pallas_call | solution.py:421
  11.8 0.0 collective-permute-start.3
  11.8 1.7 %collective-permute-start.4 = (f32[2,8,128]{2,1,0:T(8,128)S(1)}, f32[2,8,128]{2,1,0:T(8,128)S(1)}, u32[]{:S(2)}, u32[]{:S(2)}) collective-permute-start(f32[2,8,128]{2,1,0:T(8,128)S(1)} %get-tuple-element.60.my_inner_ref), channel_id=1, source_target_pairs={{0,1},{1,0},{2,3},{3,2},{4,5},{5,4},{6,7},{7,6},{8,9},{9,8},{10,11... | collective-permute-start | bytes 24584 | tf_op jit(solution)/shard_map/ppermute | solution.py:476
  13.5 0.5 %shard_map.84 = (f32[4,12,8,128]{3,2,1,0:T(8,128)S(1)}, f32[2,2,8,128]{3,2,1,0:T(8,128)S(1)}) custom-call(f32[13,8,128]{2,1,0:T(8,128)S(1)} %shard_map.77.source_ref.block_ref.refs_0_, f32[13,8,128]{2,1,0:T(8,128)S(1)} %collective-permute-done.block_ref.refs_1_, f32[13,8,128]{2,1,0:T(8,128)S(1)} %collective-permute-done.1.block_ref.refs_2_, ...), custom_call_target="tpu_custom_call" | custom-call | tf_op jit(solution)/shard_map/pallas_call | solution.py:421
  14.0 0.8 %collective-permute-done.3.outer_ref = f32[2,8,128]{2,1,0:T(8,128)S(1)} collective-permute-done((f32[2,8,128]{2,1,0:T(8,128)S(1)}, f32[2,8,128]{2,1,0:T(8,128)S(1)}, u32[]{:S(2)}, u32[]{:S(2)}) %collective-permute-start.3) | collective-permute-done | bytes 8224 | tf_op jit(solution)/shard_map/ppermute | solution.py:477
  14.9 0.0 collective-permute-done.4.inner_ref
  14.9 0.3 %shard_map.85 = (f32[4,12,8,128]{3,2,1,0:T(8,128)S(1)}, f32[12,8,128]{2,1,0:T(8,128)S(1)}) custom-call(f32[4,12,8,128]{3,2,1,0:T(8,128)S(1)} %get-tuple-element.57.middle_in_ref, f32[2,2,8,128]{3,2,1,0:T(8,128)S(1)} %get-tuple-element.58.packed_ref, f32[2,8,128]{2,1,0:T(8,128)S(1)} %get-tuple-element.59.my_outer_ref, ...), custom_call_target="tpu_custom_call", output_to_operand_aliasing={{0}: (0, {})} | custom-call | tf_op jit(solution)/shard_map/pallas_call | solution.py:421
  15.1 1.1 %shard_map.86 = (f32[12,8,128]{2,1,0:T(8,128)}, f32[1,128]{1,0:T(1,128)}) custom-call(f32[13,8,128]{2,1,0:T(8,128)S(1)} %shard_map.77.source_ref.block_ref.refs_0_, f32[4,12,8,128]{3,2,1,0:T(8,128)S(1)} %get-tuple-element.61.middle_ref, f32[12,8,128]{2,1,0:T(8,128)S(1)} %get-tuple-element.62.edge_ref, f32[1,128]{1,0:T(1,128)S(1)} %get-tuple-element.63.wall_in_ref, ...), custom_call_target="tpu_custom_call" | custom-call | tf_op jit(solution)/shard_map/pallas_call | solution.py:421
  (2 shorter events, 0.0 us)
Async XLA Ops:
  1.4 8.6 %collective-permute-start = (f32[13,8,128]{2,1,0:T(8,128)S(1)}, f32[13,8,128]{2,1,0:T(8,128)S(1)}, u32[]{:S(2)}, u32[]{:S(2)}) collective-permute-start(f32[13,8,128]{2,1,0:T(8,128)S(1)} %shard_map.77.source_ref.block_ref.refs_0_), channel_id=1, source_target_pairs={{0,4},{4,8},{8,12},{12,0},{1,5},{5,9},{9,13},{13,1},{2,6},{6,10},{... | collective-permute-start | bytes 159752 | tf_op jit(solution)/shard_map/ppermute | solution.py:401
  4.5 4.0 %copy-start = (s32[11,16]{1,0:T(8,128)S(1)}, s32[11,16]{1,0:T(8,128)}, u32[]{:S(2)}) copy-start(s32[11,16]{1,0:T(8,128)} %param.10) | copy-start | bytes 2116
  4.5 4.0 %copy-start.1 = (f32[64]{0:T(128)S(1)}, f32[64]{0:T(128)}, u32[]{:S(2)}) copy-start(f32[64]{0:T(128)} %param.8) | copy-start | bytes 772
  4.5 6.4 %collective-permute-start.1 = (f32[13,8,128]{2,1,0:T(8,128)S(1)}, f32[13,8,128]{2,1,0:T(8,128)S(1)}, u32[]{:S(2)}, u32[]{:S(2)}) collective-permute-start(f32[13,8,128]{2,1,0:T(8,128)S(1)} %get-tuple-element.34), channel_id=1, source_target_pairs={{0,8},{4,12},{8,0},{12,4},{1,9},{5,13},{9,1},{13,5},{2,10},{6,14},... | collective-permute-start | bytes 159752 | tf_op jit(solution)/shard_map/ppermute | solution.py:401
  7.2 4.2 %collective-permute-start.2 = (f32[13,8,128]{2,1,0:T(8,128)S(1)}, f32[13,8,128]{2,1,0:T(8,128)S(1)}, u32[]{:S(2)}, u32[]{:S(2)}) collective-permute-start(f32[13,8,128]{2,1,0:T(8,128)S(1)} %get-tuple-element.35), channel_id=1, source_target_pairs={{0,12},{4,0},{8,4},{12,8},{1,13},{5,1},{9,5},{13,9},{2,14},{6,2},{... | collective-permute-start | bytes 159752 | tf_op jit(solution)/shard_map/ppermute | solution.py:401
  8.7 0.7 %copy-start.2 = (f32[64]{0:T(128)S(1)}, f32[64]{0:T(128)}, u32[]{:S(2)}) copy-start(f32[64]{0:T(128)} %param.9) | copy-start | bytes 772
  8.7 0.7 %copy-start.3 = (s32[16]{0:T(128)S(1)}, s32[16]{0:T(128)}, u32[]{:S(2)}) copy-start(s32[16]{0:T(128)} %param.11) | copy-start | bytes 196
  11.8 3.1 %collective-permute-start.3 = (f32[2,8,128]{2,1,0:T(8,128)S(1)}, f32[2,8,128]{2,1,0:T(8,128)S(1)}, u32[]{:S(2)}, u32[]{:S(2)}) collective-permute-start(f32[2,8,128]{2,1,0:T(8,128)S(1)} %get-tuple-element.59.my_outer_ref), channel_id=1, source_target_pairs={{0,3},{1,2},{2,1},{3,0},{4,7},{5,6},{6,5},{7,4},{8,11},{9,10},{10,... | collective-permute-start | bytes 24584 | tf_op jit(solution)/shard_map/ppermute | solution.py:477
  11.8 3.1 %collective-permute-start.4 = (f32[2,8,128]{2,1,0:T(8,128)S(1)}, f32[2,8,128]{2,1,0:T(8,128)S(1)}, u32[]{:S(2)}, u32[]{:S(2)}) collective-permute-start(f32[2,8,128]{2,1,0:T(8,128)S(1)} %get-tuple-element.60.my_inner_ref), channel_id=1, source_target_pairs={{0,1},{1,0},{2,3},{3,2},{4,5},{5,4},{6,7},{7,6},{8,9},{9,8},{10,11... | collective-permute-start | bytes 24584 | tf_op jit(solution)/shard_map/ppermute | solution.py:476
